TPU v7x, 32 devices: a whole 2x2x4 slice. The times are simulated.
32 devices in a mesh: dp: 32 (over z, y, x, core), tensor: 1.
Axes of the slice: x: 2, y: 2, z: 4, core: 2. Of those that a mesh axis runs over, the one named last changes fastest.
Arguments:
- hidden_in: bfloat16 [8192, 8192], P('dp', 'tensor'), may hold values from -6 to 6
- query_weight: bfloat16 [128, 8192], P('tensor'), may hold values from -0.0625 to 0.0625
- saved_keys: bfloat16 [8192, 64], P('dp', 'tensor'), may hold values from -128 to 128
- saved_values: bfloat16 [8192, 64], P('dp', 'tensor'), may hold values from -6 to 6
- grad_out: bfloat16 [8192, 128], P('dp', 'tensor'), may hold values from -6 to 6
Outputs:
- grad_query_weight: bfloat16 [128, 8192], P('tensor')
- grad_hidden: bfloat16 [8192, 8192], P('dp', 'tensor')
All inputs are finite; a program needn't handle non-finite values.
Results may differ from a plain program's by a relative error of at most 0.035.
The roundings to bfloat16 on the way count: a program that leaves them out, or rounds other values in their place, can miss the bound.
Values may be sent and summed in bfloat16 or wider, within the bound.
No kernel may reach another device: no remote copies, remote signals or barrier semaphores. Data moves between devices by JAX's collectives and lax.ppermute only.
A program may use at most 64 MiB of HBM per device.

v0:
```python
import jax
import jax.numpy as jnp
from jax import lax
from jax.sharding import PartitionSpec as P


def head_grad(query, keys, values, grad_out):
    length = query.shape[0]
    score_scale = query.shape[1] ** (-0.5)
    scores = jnp.einsum("qd,kd->qk", query, keys, preferred_element_type=jnp.float32) * score_scale
    row_index = jnp.arange(length)[:, None]
    col_index = jnp.arange(length)[None, :]
    causal_mask = col_index <= row_index
    scores = jnp.where(causal_mask, scores, -1e30)
    row_peak = jnp.max(scores, axis=1, keepdims=True)
    raised = jnp.where(causal_mask, jnp.exp(scores - row_peak), 0.0)
    attn_weights = raised / jnp.sum(raised, axis=1, keepdims=True)
    grad_prob = jnp.einsum("qd,kd->qk", grad_out, values, preferred_element_type=jnp.float32)
    row_delta = jnp.sum(attn_weights * grad_prob, axis=1, keepdims=True)
    grad_score = (attn_weights * (grad_prob - row_delta) * score_scale).astype(jnp.bfloat16)
    return jnp.dot(grad_score, keys, preferred_element_type=jnp.float32).astype(jnp.bfloat16)


def group_grad(query, keys, values, grad_out):
    head_size = keys.shape[1]
    count = query.shape[1] // head_size
    pieces = [
        head_grad(
            query[:, i * head_size : (i + 1) * head_size],
            keys,
            values,
            grad_out[:, i * head_size : (i + 1) * head_size],
        )
        for i in range(count)
    ]
    return jnp.concatenate(pieces, axis=1)


def per_device(hidden_in, query_weight, saved_keys, saved_values, grad_out):
    whole_in = lax.all_gather(hidden_in, "tensor", axis=1, tiled=True)
    query = lax.dot_general(
        whole_in, query_weight, (((1,), (1,)), ((), ())), preferred_element_type=jnp.float32
    ).astype(jnp.bfloat16)
    grad_query = group_grad(query, saved_keys, saved_values, grad_out)
    grad_rows = lax.dot_general(
        grad_query, whole_in, (((0,), (0,)), ((), ())), preferred_element_type=jnp.float32
    )
    input_terms = jnp.dot(grad_query, query_weight, preferred_element_type=jnp.float32)
    grad_hidden = lax.psum_scatter(
        input_terms.astype(jnp.bfloat16), "tensor", scatter_dimension=1, tiled=True
    )
    grad_query_weight = lax.psum(grad_rows, "dp").astype(jnp.bfloat16)
    return (grad_query_weight, grad_hidden)


def solution(mesh):
    placed = (
        P("dp", "tensor"),
        P("tensor", None),
        P("dp", "tensor"),
        P("dp", "tensor"),
        P("dp", "tensor"),
    )
    return jax.shard_map(
        per_device,
        mesh=mesh,
        in_specs=placed,
        out_specs=(P("tensor", None), P("dp", "tensor")),
        check_vma=False,
    )
```

profile of v0, /device:TPU:0, one launch (start us, length us, event | category | flops | bytes accessed | tf_op | source)
XLA Modules:
  0.0 108.2 jit_solution(11833917786863159941)
XLA Ops:
  0.6 0.0 copy-start
  0.6 0.0 copy-start.4
  0.7 0.0 copy-start.3
  0.7 1.6 %copy-done = bf16[128,8192]{1,0:T(8,128)(2,1)S(1)} copy-done((bf16[128,8192]{1,0:T(8,128)(2,1)S(1)}, bf16[128,8192]{1,0:T(8,128)(2,1)}, u32[]{:S(2)}) %copy-start) | copy-done | bytes 2097176
  2.2 0.0 copy-start.2
  2.2 3.7 %convolution_convert_fusion.1 = bf16[256,128]{0,1:T(8,128)(2,1)S(1)} fusion(bf16[256,8192]{1,0:T(8,128)(2,1)} %param.5, bf16[128,8192]{1,0:T(8,128)(2,1)S(1)} %copy-done), kind=kOutput, calls=%fused_computation.5 | convolution fusion | flops 536903680 | bytes 6356992 | tf_op jit(solution)/shard_map/dot_general | solution.py:41
  6.0 0.0 copy-done.4
  6.0 0.0 copy-start.1
  6.0 0.3 fusion.26
  6.3 0.1 fusion.3
  6.3 0.0 copy-done.3
  6.3 0.0 copy-done.2
  6.3 0.3 multiply_reduce_fusion.1
  6.6 0.2 convolution_convert_fusion.3
  6.8 0.3 fusion.25
  7.1 0.1 fusion.5
  7.1 0.3 multiply_reduce_fusion
  7.4 0.2 convolution_convert_fusion.2
  7.6 0.6 copy-done.1
  8.2 2.8 %fusion.16 = f32[128,8192]{1,0:T(8,128)} fusion(bf16[256,8192]{1,0:T(8,128)(2,1)S(1)} %copy-done.1, bf16[256,64]{0,1:T(8,128)(2,1)S(1)} %convolution_convert_fusion.2, bf16[256,64]{0,1:T(8,128)(2,1)S(1)} %convolution_convert_fusion.3), kind=kOutput, calls=%fused_computation.28 | convolution fusion | flops 537001984 | bytes 8454144 | tf_op jit(solution)/shard_map/dot_general | solution.py:45
  10.9 94.0 %all-reduce.1 = bf16[128,8192]{1,0:T(8,128)(2,1)} all-reduce(f32[128,8192]{1,0:T(8,128)} %fusion.16), channel_id=1, replica_groups=mesh['dp'=32,'tensor'=1] {'dp'}, use_global_device_ids=true, to_apply=%region_6.7 | all-reduce | flops 1048576 | bytes 6291456 | tf_op jit(solution)/shard_map/psum | solution.py:52
  105.0 3.3 %convolution_convert_fusion = bf16[256,8192]{1,0:T(8,128)(2,1)} fusion(bf16[128,8192]{1,0:T(8,128)(2,1)S(1)} %copy-done, bf16[256,64]{0,1:T(8,128)(2,1)S(1)} %convolution_convert_fusion.2, bf16[256,64]{0,1:T(8,128)(2,1)S(1)} %convolution_convert_fusion.3), kind=kOutput, calls=%fused_computation | convolution fusion | flops 539099136 | bytes 6356992 | tf_op jit(solution)/shard_map/dot_general | solution.py:48
Async XLA Ops:
  0.6 1.6 %copy-start = (bf16[128,8192]{1,0:T(8,128)(2,1)S(1)}, bf16[128,8192]{1,0:T(8,128)(2,1)}, u32[]{:S(2)}) copy-start(bf16[128,8192]{1,0:T(8,128)(2,1)} %param.6) | copy-start | bytes 6291460
  0.6 5.3 %copy-start.4 = (bf16[256,64]{0,1:T(8,128)(2,1)S(1)}, bf16[256,64]{0,1:T(8,128)(2,1)}, u32[]{:S(2)}) copy-start(bf16[256,64]{0,1:T(8,128)(2,1)} %param.7) | copy-start | bytes 98308
  0.7 5.7 %copy-start.3 = (bf16[256,64]{0,1:T(8,128)(2,1)S(1)}, bf16[256,64]{0,1:T(8,128)(2,1)}, u32[]{:S(2)}) copy-start(bf16[256,64]{0,1:T(8,128)(2,1)} %param.8) | copy-start | bytes 98308
  2.2 4.1 %copy-start.2 = (bf16[256,128]{1,0:T(8,128)(2,1)S(1)}, bf16[256,128]{1,0:T(8,128)(2,1)}, u32[]{:S(2)}) copy-start(bf16[256,128]{1,0:T(8,128)(2,1)} %param.9) | copy-start | bytes 196612
  6.0 2.2 %copy-start.1 = (bf16[256,8192]{1,0:T(8,128)(2,1)S(1)}, bf16[256,8192]{1,0:T(8,128)(2,1)}, u32[]{:S(2)}) copy-start(bf16[256,8192]{1,0:T(8,128)(2,1)} %param.5) | copy-start | bytes 12582916
where the time goes:
time: 109 us; the launch traced here: 108 us
  blocking collectives  94 us (86%)
  matrix products  11.2 us (10%)
  local copies, waits for them, and re-layouts  2.14 us (2%)
    psum x1, blocking collectives, per_device(): grad_query_weight = lax.psum(grad_rows, 'dp').astype(jnp.bfloat16)  94 us
    dot_general x1, matrix products, per_device(): lax.dot_general(whole_in, query_weight, (((1,), (1,)), ((), ())), preferr...  3.75 us
    dot_general x1, matrix products, per_device(): jnp.dot(grad_query, query_weight, preferred_element_type=jnp.float32)  3.28 us
    dot_general x1, matrix products, per_device(): lax.dot_general(grad_query, whole_in, (((0,), (0,)), ((), ())), preferred...  2.75 us

commit v1 on v0

--- a/solution.py
+++ b/solution.py
@@ -36,7 +36,31 @@
     return jnp.concatenate(pieces, axis=1)
 
 
-def per_device(hidden_in, query_weight, saved_keys, saved_values, grad_out):
+def stages_of(count):
+    bits = count.bit_length() - 1
+    return [(0, 1)] + [(low, min(low + 3, bits)) for low in range(1, bits, 3)]
+
+
+def add_over_devices(blocks, count):
+    swap = lambda array, step: lax.ppermute(array, "dp", [(i, i ^ step) for i in range(count)])
+    stages = stages_of(count)
+    total = blocks
+    for low, high in stages:
+        ways = 1 << (high - low)
+        parts = total.reshape(-1, ways, *total.shape[1:])
+        arrived = [swap(parts[:, way], way << low) for way in range(1, ways)]
+        added = parts[:, 0].astype(jnp.float32)
+        for piece in arrived:
+            added = added + piece.astype(jnp.float32)
+        total = added.astype(jnp.bfloat16)
+    for low, high in reversed(stages):
+        ways = 1 << (high - low)
+        pieces = [total] + [swap(total, way << low) for way in range(1, ways)]
+        total = jnp.stack(pieces, axis=1).reshape(-1, *total.shape[1:])
+    return total
+
+
+def per_device(count, hidden_in, query_weight, saved_keys, saved_values, grad_out):
     whole_in = lax.all_gather(hidden_in, "tensor", axis=1, tiled=True)
     query = lax.dot_general(
         whole_in, query_weight, (((1,), (1,)), ((), ())), preferred_element_type=jnp.float32
@@ -44,16 +68,21 @@
     grad_query = group_grad(query, saved_keys, saved_values, grad_out)
     grad_rows = lax.dot_general(
         grad_query, whole_in, (((0,), (0,)), ((), ())), preferred_element_type=jnp.float32
-    )
+    ).astype(jnp.bfloat16)
     input_terms = jnp.dot(grad_query, query_weight, preferred_element_type=jnp.float32)
     grad_hidden = lax.psum_scatter(
         input_terms.astype(jnp.bfloat16), "tensor", scatter_dimension=1, tiled=True
     )
-    grad_query_weight = lax.psum(grad_rows, "dp").astype(jnp.bfloat16)
+    rows, columns = grad_rows.shape
+    order = jnp.arange(count) ^ lax.axis_index("dp")
+    blocks = grad_rows.reshape(rows, count, columns // count).transpose(1, 0, 2)
+    total = add_over_devices(blocks[order], count)
+    grad_query_weight = total[order].transpose(1, 0, 2).reshape(rows, columns)
     return (grad_query_weight, grad_hidden)
 
 
 def solution(mesh):
+    count = mesh.shape["dp"]
     placed = (
         P("dp", "tensor"),
         P("tensor", None),
@@ -62,7 +91,7 @@
         P("dp", "tensor"),
     )
     return jax.shard_map(
-        per_device,
+        lambda *arrays: per_device(count, *arrays),
         mesh=mesh,
         in_specs=placed,
         out_specs=(P("tensor", None), P("dp", "tensor")),

time: 109 us -> 86.4 us (0.79)
  blocking collectives: 94 us -> 0 us
  starting transfers between devices: 0 us -> 26.3 us
  waiting for transfers between devices: 0 us -> 25.7 us
  local copies, waits for them, and re-layouts: 2.14 us -> 23.1 us
  matrix products: 11.2 us -> 9.23 us
    psum x1 -> x0, blocking collectives: 94 us -> none  [per_device(): grad_query_weight = lax.psum(grad_rows, 'dp').astype(jnp.bfloat16)]
    ppermute x0 -> x18, starting transfers between devices: none -> 26.3 us  [add_over_devices(): lax.ppermute(array, 'dp', [(i, i ^ step) for i in range(count)])]
    ppermute x0 -> x18, waiting for transfers between devices: none -> 25.7 us  [add_over_devices(): lax.ppermute(array, 'dp', [(i, i ^ step) for i in range(count)])]
    gather x0 -> x2, local copies, waits for them, and re-layouts: none -> 7.19 us  [the longest x1 3.6 us: per_device(): grad_query_weight = total[order].transpose(1, 0, 2).reshape(rows, columns)]
    unnamed x10 -> x19, local copies, waits for them, and re-layouts: 2.14 us -> 7.21 us
    transpose x0 -> x1, local copies, waits for them, and re-layouts: none -> 4.07 us  [per_device(): grad_query_weight = total[order].transpose(1, 0, 2).reshape(rows, columns)]
    dot_general x1, matrix products: 2.75 us -> 0.73 us  [per_device(): lax.dot_general(grad_query, whole_in, (((0,), (0,)), ((), ())), preferred...]
    reshape x0 -> x1, local copies, waits for them, and re-layouts: none -> 1.58 us  [per_device(): blocks = grad_rows.reshape(rows, count, columns // count).transpose(1, 0, 2)]
  transfers between devices with their start and end apart: 0 -> 18, of which waited for: 0 -> 9; matrix products, arithmetic and copies ran while one was open for 0% -> 4% of each run, Pallas kernels for 0% -> 0%
where the time goes in v1:
time: 86.4 us; the launch traced here: 86 us
  starting transfers between devices  26.3 us (30%)
  waiting for transfers between devices  25.7 us (30%)
  local copies, waits for them, and re-layouts  23.1 us (27%)
  matrix products  9.23 us (11%)
    ppermute x18, starting transfers between devices, add_over_devices(): lax.ppermute(array, 'dp', [(i, i ^ step) for i in range(count)])  26.3 us
    ppermute x18, waiting for transfers between devices, add_over_devices(): lax.ppermute(array, 'dp', [(i, i ^ step) for i in range(count)])  25.7 us
    unnamed x19, local copies, waits for them, and re-layouts  7.21 us
    transpose x1, local copies, waits for them, and re-layouts, per_device(): grad_query_weight = total[order].transpose(1, 0, 2).reshape(rows, columns)  4.07 us
    dot_general x1, matrix products, per_device(): lax.dot_general(whole_in, query_weight, (((1,), (1,)), ((), ())), preferr...  3.75 us
    gather x1, local copies, waits for them, and re-layouts, per_device(): grad_query_weight = total[order].transpose(1, 0, 2).reshape(rows, columns)  3.6 us
    gather x1, local copies, waits for them, and re-layouts, per_device(): total = add_over_devices(blocks[order], count)  3.59 us
    dot_general x1, matrix products, per_device(): jnp.dot(grad_query, query_weight, preferred_element_type=jnp.float32)  3.29 us
  transfers between devices with their start and end apart: 18, of which 9 were waited for; matrix products, arithmetic and copies ran while one was open for 4% of the time, Pallas kernels for 0%

profile of v1, /device:TPU:0, one launch (start us, length us, event | category | flops | bytes accessed | tf_op | source)
XLA Modules:
  0.0 86.0 jit_solution(6353146959097327316)
XLA Ops:
  0.6 0.0 copy-start
  0.6 1.6 %copy-done = bf16[128,8192]{1,0:T(8,128)(2,1)S(1)} copy-done((bf16[128,8192]{1,0:T(8,128)(2,1)S(1)}, bf16[128,8192]{1,0:T(8,128)(2,1)}, u32[]{:S(2)}) %copy-start) | copy-done | bytes 2097176
  2.2 3.8 %convolution_convert_fusion.2 = bf16[256,128]{0,1:T(8,128)(2,1)S(1)} fusion(bf16[256,8192]{1,0:T(8,128)(2,1)} %param.5, bf16[128,8192]{1,0:T(8,128)(2,1)S(1)} %copy-done), kind=kOutput, calls=%fused_computation.12 | convolution fusion | flops 536903680 | bytes 6356992 | tf_op jit(solution)/shard_map/dot_general | solution.py:65
  6.0 0.0 copy-done.5
  6.0 0.3 fusion.36
  6.3 0.3 fusion.37
  6.5 0.1 fusion.13
  6.6 0.1 fusion.11
  6.7 0.3 multiply_reduce_fusion.1
  6.9 0.0 copy-start.1
  7.0 0.3 multiply_reduce_fusion
  7.3 0.2 convolution_convert_fusion.4
  7.5 0.2 convolution_convert_fusion.3
  7.7 1.5 %copy-done.1 = bf16[256,8192]{1,0:T(8,128)(2,1)S(1)} copy-done((bf16[256,8192]{1,0:T(8,128)(2,1)S(1)}, bf16[256,8192]{1,0:T(8,128)(2,1)}, u32[]{:S(2)}) %copy-start.1) | copy-done | bytes 4194328
  9.1 0.7 convolution_convert_fusion.1
  9.9 1.6 %copy.58 = bf16[16,32,8,256]{3,2,0,1:T(8,128)(2,1)} copy(bf16[16,32,8,256]{3,2,1,0:T(8,128)(2,1)S(1)} %bitcast.102) | data formatting | bytes 4194304 | tf_op jit(solution)/shard_map/reshape | solution.py:78
  11.5 3.6 %gather_fusion = bf16[32,128,256]{2,1,0:T(8,128)(2,1)} fusion(bf16[32,128,256]{2,1,0:T(8,128)(2,1)} %bitcast.107, s32[1024]{0:T(1024)S(1)} %pad_clamp_fusion), kind=kCustom, calls=%fused_computation | custom fusion | bytes 4194432 | tf_op jit(solution)/shard_map/gather | solution.py:79
  15.0 1.4 %slice_bitcast_fusion = bf16[16,128,256]{2,1,0:T(8,128)(2,1)S(1)} fusion(bf16[16,2,128,256]{3,2,1,0:T(8,128)(2,1)} %bitcast.103), kind=kLoop, calls=%fused_computation.15 | loop fusion | bytes 2097152 | tf_op jit(solution)/shard_map/squeeze | solution.py:51
  16.5 0.5 collective-permute-start
  17.0 2.3 %collective-permute-done = bf16[16,128,256]{2,1,0:T(8,128)(2,1)S(1)} collective-permute-done((bf16[16,128,256]{2,1,0:T(8,128)(2,1)S(1)}, bf16[16,128,256]{2,1,0:T(8,128)(2,1)S(1)}, u32[]{:S(2)}, u32[]{:S(2)}) %collective-permute-start) | collective-permute-done | bytes 1048608 | tf_op jit(solution)/shard_map/ppermute | solution.py:45
  19.3 0.3 fusion
  19.6 0.1 slice_bitcast_fusion.8
  19.7 2.9 %collective-permute-start.1 = (bf16[2,128,256]{2,1,0:T(8,128)(2,1)S(1)}, bf16[2,128,256]{2,1,0:T(8,128)(2,1)S(1)}, u32[]{:S(2)}, u32[]{:S(2)}) collective-permute-start(bf16[2,128,256]{2,1,0:T(8,128)(2,1)S(1)} %get-tuple-element.4), channel_id=1, source_target_pairs={{0,2},{1,3},{2,0},{3,1},{4,6},{5,7},{6,4},{7,5},{8,10},{9,11},{10,... | collective-permute-start | bytes 393224 | tf_op jit(solution)/shard_map/ppermute | solution.py:45
  22.6 2.5 %collective-permute-start.6 = (bf16[2,128,256]{2,1,0:T(8,128)(2,1)S(1)}, bf16[2,128,256]{2,1,0:T(8,128)(2,1)S(1)}, u32[]{:S(2)}, u32[]{:S(2)}) collective-permute-start(bf16[2,128,256]{2,1,0:T(8,128)(2,1)S(1)} %get-tuple-element.5), channel_id=1, source_target_pairs={{0,12},{1,13},{2,14},{3,15},{4,8},{5,9},{6,10},{7,11},{8,4},{9,5},... | collective-permute-start | bytes 393224 | tf_op jit(solution)/shard_map/ppermute | solution.py:45
  25.2 0.4 collective-permute-start.5
  25.6 1.6 %collective-permute-start.4 = (bf16[2,128,256]{2,1,0:T(8,128)(2,1)S(1)}, bf16[2,128,256]{2,1,0:T(8,128)(2,1)S(1)}, u32[]{:S(2)}, u32[]{:S(2)}) collective-permute-start(bf16[2,128,256]{2,1,0:T(8,128)(2,1)S(1)} %get-tuple-element.7), channel_id=1, source_target_pairs={{0,8},{1,9},{2,10},{3,11},{4,12},{5,13},{6,14},{7,15},{8,0},{9,1},... | collective-permute-start | bytes 393224 | tf_op jit(solution)/shard_map/ppermute | solution.py:45
  27.2 1.4 %collective-permute-start.3 = (bf16[2,128,256]{2,1,0:T(8,128)(2,1)S(1)}, bf16[2,128,256]{2,1,0:T(8,128)(2,1)S(1)}, u32[]{:S(2)}, u32[]{:S(2)}) collective-permute-start(bf16[2,128,256]{2,1,0:T(8,128)(2,1)S(1)} %get-tuple-element.8), channel_id=1, source_target_pairs={{0,6},{1,7},{2,4},{3,5},{4,2},{5,3},{6,0},{7,1},{8,14},{9,15},{10,... | collective-permute-start | bytes 393224 | tf_op jit(solution)/shard_map/ppermute | solution.py:45
  28.6 0.0 collective-permute-done.1
  28.6 1.5 %collective-permute-start.2 = (bf16[2,128,256]{2,1,0:T(8,128)(2,1)S(1)}, bf16[2,128,256]{2,1,0:T(8,128)(2,1)S(1)}, u32[]{:S(2)}, u32[]{:S(2)}) collective-permute-start(bf16[2,128,256]{2,1,0:T(8,128)(2,1)S(1)} %get-tuple-element.9), channel_id=1, source_target_pairs={{0,4},{1,5},{2,6},{3,7},{4,0},{5,1},{6,2},{7,3},{8,12},{9,13},{10,... | collective-permute-start | bytes 393224 | tf_op jit(solution)/shard_map/ppermute | solution.py:45
  30.1 0.0 collective-permute-done.6
  30.1 2.4 %collective-permute-start.7 = (bf16[2,128,256]{2,1,0:T(8,128)(2,1)S(1)}, bf16[2,128,256]{2,1,0:T(8,128)(2,1)S(1)}, u32[]{:S(2)}, u32[]{:S(2)}) collective-permute-start(bf16[2,128,256]{2,1,0:T(8,128)(2,1)S(1)} %get-tuple-element.10), channel_id=1, source_target_pairs={{0,14},{1,15},{2,12},{3,13},{4,10},{5,11},{6,8},{7,9},{8,6},{9,7},... | collective-permute-start | bytes 393224 | tf_op jit(solution)/shard_map/ppermute | solution.py:45
  32.5 0.0 collective-permute-done.5
  32.5 3.1 %collective-permute-done.4 = bf16[2,128,256]{2,1,0:T(8,128)(2,1)S(1)} collective-permute-done((bf16[2,128,256]{2,1,0:T(8,128)(2,1)S(1)}, bf16[2,128,256]{2,1,0:T(8,128)(2,1)S(1)}, u32[]{:S(2)}, u32[]{:S(2)}) %collective-permute-start.4) | collective-permute-done | bytes 131104 | tf_op jit(solution)/shard_map/ppermute | solution.py:45
  35.6 1.6 %collective-permute-done.3 = bf16[2,128,256]{2,1,0:T(8,128)(2,1)S(1)} collective-permute-done((bf16[2,128,256]{2,1,0:T(8,128)(2,1)S(1)}, bf16[2,128,256]{2,1,0:T(8,128)(2,1)S(1)}, u32[]{:S(2)}, u32[]{:S(2)}) %collective-permute-start.3) | collective-permute-done | bytes 131104 | tf_op jit(solution)/shard_map/ppermute | solution.py:45
  37.2 1.2 %collective-permute-done.2 = bf16[2,128,256]{2,1,0:T(8,128)(2,1)S(1)} collective-permute-done((bf16[2,128,256]{2,1,0:T(8,128)(2,1)S(1)}, bf16[2,128,256]{2,1,0:T(8,128)(2,1)S(1)}, u32[]{:S(2)}, u32[]{:S(2)}) %collective-permute-start.2) | collective-permute-done | bytes 131104 | tf_op jit(solution)/shard_map/ppermute | solution.py:45
  38.4 0.0 collective-permute-done.7
  38.4 0.1 fusion.14
  38.5 2.8 %collective-permute-start.8 = (bf16[1,128,256]{2,1,0:T(8,128)(2,1)S(1)}, bf16[1,128,256]{2,1,0:T(8,128)(2,1)S(1)}, u32[]{:S(2)}, u32[]{:S(2)}) collective-permute-start(bf16[1,128,256]{2,1,0:T(8,128)(2,1)S(1)} %slice_bitcast_fusion.10), channel_id=1, source_target_pairs={{0,16},{1,17},{2,18},{3,19},{4,20},{5,21},{6,22},{7,23},{8,24},{9,... | collective-permute-start | bytes 196616 | tf_op jit(solution)/shard_map/ppermute | solution.py:45
  41.3 3.4 %collective-permute-done.8 = bf16[1,128,256]{2,1,0:T(8,128)(2,1)S(1)} collective-permute-done((bf16[1,128,256]{2,1,0:T(8,128)(2,1)S(1)}, bf16[1,128,256]{2,1,0:T(8,128)(2,1)S(1)}, u32[]{:S(2)}, u32[]{:S(2)}) %collective-permute-start.8) | collective-permute-done | bytes 65568 | tf_op jit(solution)/shard_map/ppermute | solution.py:45
  44.8 1.8 %collective-permute-start.9 = (bf16[1,128,256]{2,1,0:T(8,128)(2,1)S(1)}, bf16[1,128,256]{2,1,0:T(8,128)(2,1)S(1)}, u32[]{:S(2)}, u32[]{:S(2)}) collective-permute-start(bf16[1,128,256]{2,1,0:T(8,128)(2,1)S(1)} %fusion.15), channel_id=1, source_target_pairs={{0,16},{1,17},{2,18},{3,19},{4,20},{5,21},{6,22},{7,23},{8,24},{9,... | collective-permute-start | bytes 196616 | tf_op jit(solution)/shard_map/ppermute | solution.py:45
  46.6 3.6 %collective-permute-done.9 = bf16[1,128,256]{2,1,0:T(8,128)(2,1)S(1)} collective-permute-done((bf16[1,128,256]{2,1,0:T(8,128)(2,1)S(1)}, bf16[1,128,256]{2,1,0:T(8,128)(2,1)S(1)}, u32[]{:S(2)}, u32[]{:S(2)}) %collective-permute-start.9) | collective-permute-done | bytes 65568 | tf_op jit(solution)/shard_map/ppermute | solution.py:45
  50.2 1.2 %collective-permute-start.10 = (bf16[2,128,256]{2,1,0:T(8,128)(2,1)S(1)}, bf16[2,128,256]{2,1,0:T(8,128)(2,1)S(1)}, u32[]{:S(2)}, u32[]{:S(2)}) collective-permute-start(bf16[2,128,256]{2,1,0:T(8,128)(2,1)S(1)} %fusion.20), channel_id=1, source_target_pairs={{0,2},{1,3},{2,0},{3,1},{4,6},{5,7},{6,4},{7,5},{8,10},{9,11},{10,... | collective-permute-start | bytes 393224 | tf_op jit(solution)/shard_map/ppermute | solution.py:45
  51.4 0.6 collective-permute-start.16
  52.1 2.6 %collective-permute-start.15 = (bf16[2,128,256]{2,1,0:T(8,128)(2,1)S(1)}, bf16[2,128,256]{2,1,0:T(8,128)(2,1)S(1)}, u32[]{:S(2)}, u32[]{:S(2)}) collective-permute-start(bf16[2,128,256]{2,1,0:T(8,128)(2,1)S(1)} %fusion.20), channel_id=1, source_target_pairs={{0,12},{1,13},{2,14},{3,15},{4,8},{5,9},{6,10},{7,11},{8,4},{9,5},... | collective-permute-start | bytes 393224 | tf_op jit(solution)/shard_map/ppermute | solution.py:45
  54.6 0.6 collective-permute-start.14
  55.3 2.0 %collective-permute-start.13 = (bf16[2,128,256]{2,1,0:T(8,128)(2,1)S(1)}, bf16[2,128,256]{2,1,0:T(8,128)(2,1)S(1)}, u32[]{:S(2)}, u32[]{:S(2)}) collective-permute-start(bf16[2,128,256]{2,1,0:T(8,128)(2,1)S(1)} %fusion.20), channel_id=1, source_target_pairs={{0,8},{1,9},{2,10},{3,11},{4,12},{5,13},{6,14},{7,15},{8,0},{9,1},... | collective-permute-start | bytes 393224 | tf_op jit(solution)/shard_map/ppermute | solution.py:45
  57.3 0.5 collective-permute-done.10
  57.8 0.4 collective-permute-start.11
  58.1 5.1 %collective-permute-done.11 = bf16[2,128,256]{2,1,0:T(8,128)(2,1)S(1)} collective-permute-done((bf16[2,128,256]{2,1,0:T(8,128)(2,1)S(1)}, bf16[2,128,256]{2,1,0:T(8,128)(2,1)S(1)}, u32[]{:S(2)}, u32[]{:S(2)}) %collective-permute-start.11) | collective-permute-done | bytes 131104 | tf_op jit(solution)/shard_map/ppermute | solution.py:45
  63.2 0.9 %collective-permute-start.12 = (bf16[2,128,256]{2,1,0:T(8,128)(2,1)S(1)}, bf16[2,128,256]{2,1,0:T(8,128)(2,1)S(1)}, u32[]{:S(2)}, u32[]{:S(2)}) collective-permute-start(bf16[2,128,256]{2,1,0:T(8,128)(2,1)S(1)} %fusion.20), channel_id=1, source_target_pairs={{0,6},{1,7},{2,4},{3,5},{4,2},{5,3},{6,0},{7,1},{8,14},{9,15},{10,... | collective-permute-start | bytes 393224 | tf_op jit(solution)/shard_map/ppermute | solution.py:45
  64.1 4.9 %collective-permute-done.12 = bf16[2,128,256]{2,1,0:T(8,128)(2,1)S(1)} collective-permute-done((bf16[2,128,256]{2,1,0:T(8,128)(2,1)S(1)}, bf16[2,128,256]{2,1,0:T(8,128)(2,1)S(1)}, u32[]{:S(2)}, u32[]{:S(2)}) %collective-permute-start.12) | collective-permute-done | bytes 131104 | tf_op jit(solution)/shard_map/ppermute | solution.py:45
  69.1 0.0 collective-permute-done.13
  69.1 0.0 collective-permute-done.14
  69.1 0.0 collective-permute-done.15
  69.2 0.0 collective-permute-done.16
  69.2 0.1 copy.41
  69.3 0.1 collective-permute-start.17
  69.4 3.3 %convolution_convert_fusion = bf16[256,8192]{1,0:T(8,128)(2,1)} fusion(bf16[128,8192]{1,0:T(8,128)(2,1)S(1)} %copy-done, bf16[256,64]{0,1:T(8,128)(2,1)S(1)} %convolution_convert_fusion.3, bf16[256,64]{0,1:T(8,128)(2,1)S(1)} %convolution_convert_fusion.4), kind=kOutput, calls=%fused_computation.2 | convolution fusion | flops 539099136 | bytes 6356992 | tf_op jit(solution)/shard_map/dot_general | solution.py:72
  72.6 0.0 collective-permute-done.17
  72.6 0.2 pad_maximum_fusion
  72.8 1.5 %copy.43 = bf16[16,2,128,256]{3,2,1,0:T(8,128)(2,1)} copy(bf16[16,2,128,256]{3,2,0,1:T(8,128)(2,1)S(1)} %pad_maximum_fusion) | data formatting | bytes 4194304 | tf_op jit(solution)/shard_map/stack | solution.py:59
  74.3 3.6 %gather_fusion.1 = bf16[32,128,256]{2,1,0:T(8,128)(2,1)} fusion(bf16[32,128,256]{2,1,0:T(8,128)(2,1)} %bitcast.105, s32[1024]{0:T(1024)S(1)} %pad_clamp_fusion), kind=kCustom, calls=%fused_computation.1 | custom fusion | bytes 4194432 | tf_op jit(solution)/shard_map/gather | solution.py:80
  77.9 4.1 %copy.44 = bf16[128,32,256]{0,2,1:T(8,128)(2,1)} copy(bf16[128,32,256]{2,0,1:T(8,128)(2,1)} %bitcast.106) | data formatting | bytes 4194304 | tf_op jit(solution)/shard_map/transpose | solution.py:80
  82.0 4.1 %copy.45 = bf16[128,8192]{1,0:T(8,128)(2,1)} copy(bf16[128,8192]{0,1:T(8,128)(2,1)} %bitcast.108) | data formatting | bytes 4194304
  (20 shorter events, 0.1 us)
Async XLA Ops:
  0.6 1.6 %copy-start = (bf16[128,8192]{1,0:T(8,128)(2,1)S(1)}, bf16[128,8192]{1,0:T(8,128)(2,1)}, u32[]{:S(2)}) copy-start(bf16[128,8192]{1,0:T(8,128)(2,1)} %param.6) | copy-start | bytes 6291460
  2.2 3.8 %copy-start.5 = (bf16[256,64]{0,1:T(8,128)(2,1)S(1)}, bf16[256,64]{0,1:T(8,128)(2,1)}, u32[]{:S(2)}) copy-start(bf16[256,64]{0,1:T(8,128)(2,1)} %param.7) | copy-start | bytes 98308
  2.2 4.4 %copy-start.3 = (bf16[256,128]{1,0:T(8,128)(2,1)S(1)}, bf16[256,128]{1,0:T(8,128)(2,1)}, u32[]{:S(2)}) copy-start(bf16[256,128]{1,0:T(8,128)(2,1)} %param.9) | copy-start | bytes 196612
  2.2 4.4 %copy-start.4 = (bf16[256,64]{0,1:T(8,128)(2,1)S(1)}, bf16[256,64]{0,1:T(8,128)(2,1)}, u32[]{:S(2)}) copy-start(bf16[256,64]{0,1:T(8,128)(2,1)} %param.8) | copy-start | bytes 98308
  6.9 2.2 %copy-start.1 = (bf16[256,8192]{1,0:T(8,128)(2,1)S(1)}, bf16[256,8192]{1,0:T(8,128)(2,1)}, u32[]{:S(2)}) copy-start(bf16[256,8192]{1,0:T(8,128)(2,1)} %param.5) | copy-start | bytes 12582916
  15.0 4.3 %copy-start.2 = (bf16[32,128,256]{2,1,0:T(8,128)(2,1)S(1)}, bf16[32,128,256]{2,1,0:T(8,128)(2,1)}, u32[]{:S(2)}) copy-start(bf16[32,128,256]{2,1,0:T(8,128)(2,1)} %gather_fusion) | copy-start | bytes 6291460
  16.5 2.8 %collective-permute-start = (bf16[16,128,256]{2,1,0:T(8,128)(2,1)S(1)}, bf16[16,128,256]{2,1,0:T(8,128)(2,1)S(1)}, u32[]{:S(2)}, u32[]{:S(2)}) collective-permute-start(bf16[16,128,256]{2,1,0:T(8,128)(2,1)S(1)} %slice_bitcast_fusion), channel_id=1, source_target_pairs={{0,1},{1,0},{2,3},{3,2},{4,5},{5,4},{6,7},{7,6},{8,9},{9,8},{10,11... | collective-permute-start | bytes 3145736 | tf_op jit(solution)/shard_map/ppermute | solution.py:45
  19.7 8.9 %collective-permute-start.1 = (bf16[2,128,256]{2,1,0:T(8,128)(2,1)S(1)}, bf16[2,128,256]{2,1,0:T(8,128)(2,1)S(1)}, u32[]{:S(2)}, u32[]{:S(2)}) collective-permute-start(bf16[2,128,256]{2,1,0:T(8,128)(2,1)S(1)} %get-tuple-element.4), channel_id=1, source_target_pairs={{0,2},{1,3},{2,0},{3,1},{4,6},{5,7},{6,4},{7,5},{8,10},{9,11},{10,... | collective-permute-start | bytes 393224 | tf_op jit(solution)/shard_map/ppermute | solution.py:45
  22.6 7.5 %collective-permute-start.6 = (bf16[2,128,256]{2,1,0:T(8,128)(2,1)S(1)}, bf16[2,128,256]{2,1,0:T(8,128)(2,1)S(1)}, u32[]{:S(2)}, u32[]{:S(2)}) collective-permute-start(bf16[2,128,256]{2,1,0:T(8,128)(2,1)S(1)} %get-tuple-element.5), channel_id=1, source_target_pairs={{0,12},{1,13},{2,14},{3,15},{4,8},{5,9},{6,10},{7,11},{8,4},{9,5},... | collective-permute-start | bytes 393224 | tf_op jit(solution)/shard_map/ppermute | solution.py:45
  25.2 7.4 %collective-permute-start.5 = (bf16[2,128,256]{2,1,0:T(8,128)(2,1)S(1)}, bf16[2,128,256]{2,1,0:T(8,128)(2,1)S(1)}, u32[]{:S(2)}, u32[]{:S(2)}) collective-permute-start(bf16[2,128,256]{2,1,0:T(8,128)(2,1)S(1)} %get-tuple-element.6), channel_id=1, source_target_pairs={{0,10},{1,11},{2,8},{3,9},{4,14},{5,15},{6,12},{7,13},{8,2},{9,3},... | collective-permute-start | bytes 393224 | tf_op jit(solution)/shard_map/ppermute | solution.py:45
  25.6 10.0 %collective-permute-start.4 = (bf16[2,128,256]{2,1,0:T(8,128)(2,1)S(1)}, bf16[2,128,256]{2,1,0:T(8,128)(2,1)S(1)}, u32[]{:S(2)}, u32[]{:S(2)}) collective-permute-start(bf16[2,128,256]{2,1,0:T(8,128)(2,1)S(1)} %get-tuple-element.7), channel_id=1, source_target_pairs={{0,8},{1,9},{2,10},{3,11},{4,12},{5,13},{6,14},{7,15},{8,0},{9,1},... | collective-permute-start | bytes 393224 | tf_op jit(solution)/shard_map/ppermute | solution.py:45
  27.2 10.0 %collective-permute-start.3 = (bf16[2,128,256]{2,1,0:T(8,128)(2,1)S(1)}, bf16[2,128,256]{2,1,0:T(8,128)(2,1)S(1)}, u32[]{:S(2)}, u32[]{:S(2)}) collective-permute-start(bf16[2,128,256]{2,1,0:T(8,128)(2,1)S(1)} %get-tuple-element.8), channel_id=1, source_target_pairs={{0,6},{1,7},{2,4},{3,5},{4,2},{5,3},{6,0},{7,1},{8,14},{9,15},{10,... | collective-permute-start | bytes 393224 | tf_op jit(solution)/shard_map/ppermute | solution.py:45
  28.6 9.7 %collective-permute-start.2 = (bf16[2,128,256]{2,1,0:T(8,128)(2,1)S(1)}, bf16[2,128,256]{2,1,0:T(8,128)(2,1)S(1)}, u32[]{:S(2)}, u32[]{:S(2)}) collective-permute-start(bf16[2,128,256]{2,1,0:T(8,128)(2,1)S(1)} %get-tuple-element.9), channel_id=1, source_target_pairs={{0,4},{1,5},{2,6},{3,7},{4,0},{5,1},{6,2},{7,3},{8,12},{9,13},{10,... | collective-permute-start | bytes 393224 | tf_op jit(solution)/shard_map/ppermute | solution.py:45
  30.1 8.2 %collective-permute-start.7 = (bf16[2,128,256]{2,1,0:T(8,128)(2,1)S(1)}, bf16[2,128,256]{2,1,0:T(8,128)(2,1)S(1)}, u32[]{:S(2)}, u32[]{:S(2)}) collective-permute-start(bf16[2,128,256]{2,1,0:T(8,128)(2,1)S(1)} %get-tuple-element.10), channel_id=1, source_target_pairs={{0,14},{1,15},{2,12},{3,13},{4,10},{5,11},{6,8},{7,9},{8,6},{9,7},... | collective-permute-start | bytes 393224 | tf_op jit(solution)/shard_map/ppermute | solution.py:45
  38.5 6.2 %collective-permute-start.8 = (bf16[1,128,256]{2,1,0:T(8,128)(2,1)S(1)}, bf16[1,128,256]{2,1,0:T(8,128)(2,1)S(1)}, u32[]{:S(2)}, u32[]{:S(2)}) collective-permute-start(bf16[1,128,256]{2,1,0:T(8,128)(2,1)S(1)} %slice_bitcast_fusion.10), channel_id=1, source_target_pairs={{0,16},{1,17},{2,18},{3,19},{4,20},{5,21},{6,22},{7,23},{8,24},{9,... | collective-permute-start | bytes 196616 | tf_op jit(solution)/shard_map/ppermute | solution.py:45
  44.8 5.4 %collective-permute-start.9 = (bf16[1,128,256]{2,1,0:T(8,128)(2,1)S(1)}, bf16[1,128,256]{2,1,0:T(8,128)(2,1)S(1)}, u32[]{:S(2)}, u32[]{:S(2)}) collective-permute-start(bf16[1,128,256]{2,1,0:T(8,128)(2,1)S(1)} %fusion.15), channel_id=1, source_target_pairs={{0,16},{1,17},{2,18},{3,19},{4,20},{5,21},{6,22},{7,23},{8,24},{9,... | collective-permute-start | bytes 196616 | tf_op jit(solution)/shard_map/ppermute | solution.py:45
  50.2 7.6 %collective-permute-start.10 = (bf16[2,128,256]{2,1,0:T(8,128)(2,1)S(1)}, bf16[2,128,256]{2,1,0:T(8,128)(2,1)S(1)}, u32[]{:S(2)}, u32[]{:S(2)}) collective-permute-start(bf16[2,128,256]{2,1,0:T(8,128)(2,1)S(1)} %fusion.20), channel_id=1, source_target_pairs={{0,2},{1,3},{2,0},{3,1},{4,6},{5,7},{6,4},{7,5},{8,10},{9,11},{10,... | collective-permute-start | bytes 393224 | tf_op jit(solution)/shard_map/ppermute | solution.py:45
  51.4 17.7 %collective-permute-start.16 = (bf16[2,128,256]{2,1,0:T(8,128)(2,1)S(1)}, bf16[2,128,256]{2,1,0:T(8,128)(2,1)S(1)}, u32[]{:S(2)}, u32[]{:S(2)}) collective-permute-start(bf16[2,128,256]{2,1,0:T(8,128)(2,1)S(1)} %fusion.20), channel_id=1, source_target_pairs={{0,14},{1,15},{2,12},{3,13},{4,10},{5,11},{6,8},{7,9},{8,6},{9,7},... | collective-permute-start | bytes 393224 | tf_op jit(solution)/shard_map/ppermute | solution.py:45
  52.1 17.1 %collective-permute-start.15 = (bf16[2,128,256]{2,1,0:T(8,128)(2,1)S(1)}, bf16[2,128,256]{2,1,0:T(8,128)(2,1)S(1)}, u32[]{:S(2)}, u32[]{:S(2)}) collective-permute-start(bf16[2,128,256]{2,1,0:T(8,128)(2,1)S(1)} %fusion.20), channel_id=1, source_target_pairs={{0,12},{1,13},{2,14},{3,15},{4,8},{5,9},{6,10},{7,11},{8,4},{9,5},... | collective-permute-start | bytes 393224 | tf_op jit(solution)/shard_map/ppermute | solution.py:45
  54.6 14.5 %collective-permute-start.14 = (bf16[2,128,256]{2,1,0:T(8,128)(2,1)S(1)}, bf16[2,128,256]{2,1,0:T(8,128)(2,1)S(1)}, u32[]{:S(2)}, u32[]{:S(2)}) collective-permute-start(bf16[2,128,256]{2,1,0:T(8,128)(2,1)S(1)} %fusion.20), channel_id=1, source_target_pairs={{0,10},{1,11},{2,8},{3,9},{4,14},{5,15},{6,12},{7,13},{8,2},{9,3},... | collective-permute-start | bytes 393224 | tf_op jit(solution)/shard_map/ppermute | solution.py:45
  55.3 13.8 %collective-permute-start.13 = (bf16[2,128,256]{2,1,0:T(8,128)(2,1)S(1)}, bf16[2,128,256]{2,1,0:T(8,128)(2,1)S(1)}, u32[]{:S(2)}, u32[]{:S(2)}) collective-permute-start(bf16[2,128,256]{2,1,0:T(8,128)(2,1)S(1)} %fusion.20), channel_id=1, source_target_pairs={{0,8},{1,9},{2,10},{3,11},{4,12},{5,13},{6,14},{7,15},{8,0},{9,1},... | collective-permute-start | bytes 393224 | tf_op jit(solution)/shard_map/ppermute | solution.py:45
  57.8 5.4 %collective-permute-start.11 = (bf16[2,128,256]{2,1,0:T(8,128)(2,1)S(1)}, bf16[2,128,256]{2,1,0:T(8,128)(2,1)S(1)}, u32[]{:S(2)}, u32[]{:S(2)}) collective-permute-start(bf16[2,128,256]{2,1,0:T(8,128)(2,1)S(1)} %fusion.20), channel_id=1, source_target_pairs={{0,4},{1,5},{2,6},{3,7},{4,0},{5,1},{6,2},{7,3},{8,12},{9,13},{10,... | collective-permute-start | bytes 393224 | tf_op jit(solution)/shard_map/ppermute | solution.py:45
  63.2 5.9 %collective-permute-start.12 = (bf16[2,128,256]{2,1,0:T(8,128)(2,1)S(1)}, bf16[2,128,256]{2,1,0:T(8,128)(2,1)S(1)}, u32[]{:S(2)}, u32[]{:S(2)}) collective-permute-start(bf16[2,128,256]{2,1,0:T(8,128)(2,1)S(1)} %fusion.20), channel_id=1, source_target_pairs={{0,6},{1,7},{2,4},{3,5},{4,2},{5,3},{6,0},{7,1},{8,14},{9,15},{10,... | collective-permute-start | bytes 393224 | tf_op jit(solution)/shard_map/ppermute | solution.py:45
  69.3 3.4 %collective-permute-start.17 = (bf16[16,128,256]{2,1,0:T(8,128)(2,1)S(1)}, bf16[16,128,256]{2,1,0:T(8,128)(2,1)S(1)}, u32[]{:S(2)}, u32[]{:S(2)}) collective-permute-start(bf16[16,128,256]{2,1,0:T(8,128)(2,1)S(1)} %bitcast.111), channel_id=1, source_target_pairs={{0,1},{1,0},{2,3},{3,2},{4,5},{5,4},{6,7},{7,6},{8,9},{9,8},{10,11... | collective-permute-start | bytes 3145736 | tf_op jit(solution)/shard_map/ppermute | solution.py:45

commit v2 on v0

v2 whole, which is shorter than its diff:
```python
import functools

import jax
import jax.numpy as jnp
from jax import lax
from jax.experimental import pallas as pl
from jax.experimental.pallas import tpu as pltpu
from jax.sharding import PartitionSpec as P

VMEM_LIMIT = 40 * 1024 * 1024
ANY = pl.BlockSpec(memory_space=pl.ANY)
WHOLE = pl.BlockSpec(memory_space=pltpu.VMEM)


def dot_tt(left, right):
    return lax.dot_general(left, right, (((1,), (1,)), ((), ())), preferred_element_type=jnp.float32)


def head_grad(query, keys, values, grad_out):
    length, head_size = query.shape
    score_scale = head_size ** (-0.5)
    causal_mask = lax.broadcasted_iota(jnp.int32, (length, length), 1) <= lax.broadcasted_iota(
        jnp.int32, (length, length), 0
    )
    scores = jnp.where(causal_mask, dot_tt(query, keys) * score_scale, -1e30)
    raised = jnp.exp(scores - jnp.max(scores, axis=1, keepdims=True))
    attn_weights = raised * (1.0 / jnp.sum(raised, axis=1, keepdims=True))
    grad_prob = dot_tt(grad_out, values)
    row_delta = jnp.sum(attn_weights * grad_prob, axis=1, keepdims=True)
    grad_score = (attn_weights * (grad_prob - row_delta) * score_scale).astype(jnp.bfloat16)
    return jnp.dot(grad_score, keys, preferred_element_type=jnp.float32).astype(jnp.bfloat16)


def rows_kernel(
    blocks, core_ref, hidden_hbm, weight_hbm, keys_ref, values_ref, grad_out_ref,
    other_hbm, own_hbm, grad_query_ref,
    hidden, weight, other, own, hidden_sem, weight_sem, out_sem,
):
    tokens, width = hidden.shape
    rows = weight.shape[0]
    half, step = rows // 2, width // blocks
    head_size = keys_ref.shape[1]
    core = core_ref[0]
    copies = []
    for block in range(blocks):
        columns = pl.ds(block * step, step)
        from_hidden = pltpu.make_async_copy(hidden_hbm.at[:, columns], hidden.at[:, columns], hidden_sem.at[block])
        from_hidden.start()
        halves = []
        for place, source in enumerate((1 - core, core)):
            here = pl.ds(place * half, half)
            there = pl.ds(pl.multiple_of(source * half, half), half)
            copy = pltpu.make_async_copy(
                weight_hbm.at[there, columns], weight.at[here, columns], weight_sem.at[place, block]
            )
            copy.start()
            halves.append(copy)
        copies.append((from_hidden, *halves))
    total = jnp.zeros((tokens, rows), jnp.float32)
    for block in range(blocks):
        for copy in copies[block]:
            copy.wait()
        columns = pl.ds(block * step, step)
        total += dot_tt(hidden[:, columns], weight[:, columns])
    query = total.astype(jnp.bfloat16)
    keys, values = keys_ref[...], values_ref[...]
    given = grad_out_ref[...]
    first = core == 0
    given = jnp.concatenate(
        [
            jnp.where(first, given[:, half:], given[:, :half]),
            jnp.where(first, given[:, :half], given[:, half:]),
        ],
        axis=1,
    )
    grads = jnp.concatenate(
        [
            head_grad(query[:, low : low + head_size], keys, values, given[:, low : low + head_size])
            for low in range(0, rows, head_size)
        ],
        axis=1,
    )
    grad_query_ref[...] = jnp.concatenate(
        [
            jnp.where(first, grads[:, half:], grads[:, :half]),
            jnp.where(first, grads[:, :half], grads[:, half:]),
        ],
        axis=1,
    )
    turned = grads.T
    sent = []
    for block in range(blocks):
        columns = pl.ds(block * step, step)
        term = jnp.dot(turned, hidden[:, columns], preferred_element_type=jnp.float32).astype(jnp.bfloat16)
        other[block] = term[:half]
        own[block] = term[half:]
        for place, (buffer, target) in enumerate(((other, other_hbm), (own, own_hbm))):
            copy = pltpu.make_async_copy(buffer.at[block], target.at[block], out_sem.at[place, block])
            copy.start()
            sent.append(copy)
    for copy in sent:
        copy.wait()


def rows_of(blocks, core, hidden_in, query_weight, saved_keys, saved_values, grad_out):
    tokens, width = hidden_in.shape
    rows = query_weight.shape[0]
    piece = (blocks, rows // 2, width // blocks)
    return pl.pallas_call(
        functools.partial(rows_kernel, blocks),
        out_shape=(
            jax.ShapeDtypeStruct(piece, jnp.bfloat16),
            jax.ShapeDtypeStruct(piece, jnp.bfloat16),
            jax.ShapeDtypeStruct((tokens, rows), jnp.bfloat16),
        ),
        in_specs=[pl.BlockSpec(memory_space=pltpu.SMEM), ANY, ANY, WHOLE, WHOLE, WHOLE],
        out_specs=(ANY, ANY, WHOLE),
        scratch_shapes=[
            pltpu.VMEM((tokens, width), jnp.bfloat16),
            pltpu.VMEM((rows, width), jnp.bfloat16),
            pltpu.VMEM(piece, jnp.bfloat16),
            pltpu.VMEM(piece, jnp.bfloat16),
            pltpu.SemaphoreType.DMA((blocks,)),
            pltpu.SemaphoreType.DMA((2, blocks)),
            pltpu.SemaphoreType.DMA((2, blocks)),
        ],
        compiler_params=pltpu.CompilerParams(vmem_limit_bytes=VMEM_LIMIT),
        cost_estimate=pl.CostEstimate(
            flops=4 * tokens * width * rows,
            bytes_accessed=2 * (tokens * width + 2 * rows * width),
            transcendentals=tokens * tokens * 2,
        ),
    )(core, hidden_in, query_weight, saved_keys, saved_values, grad_out)


def assemble_kernel(core_ref, own_hbm, other_hbm, out_hbm, sem):
    blocks, half, step = own_hbm.shape
    core = core_ref[0]
    copies = []
    for place, (source, rows) in enumerate(((own_hbm, core), (other_hbm, 1 - core))):
        there = pl.ds(pl.multiple_of(rows * half, half), half)
        for block in range(blocks):
            copy = pltpu.make_async_copy(
                source.at[block], out_hbm.at[there, pl.ds(block * step, step)], sem.at[place, block]
            )
            copy.start()
            copies.append(copy)
    for copy in copies:
        copy.wait()


def assemble(core, own, other):
    blocks, half, step = own.shape
    return pl.pallas_call(
        assemble_kernel,
        out_shape=jax.ShapeDtypeStruct((2 * half, blocks * step), jnp.bfloat16),
        in_specs=[pl.BlockSpec(memory_space=pltpu.SMEM), ANY, ANY],
        out_specs=ANY,
        scratch_shapes=[pltpu.SemaphoreType.DMA((2, blocks))],
        compiler_params=pltpu.CompilerParams(vmem_limit_bytes=VMEM_LIMIT),
        cost_estimate=pl.CostEstimate(flops=0, bytes_accessed=8 * half * blocks * step, transcendentals=0),
    )(core, own, other)


def swap(array, step, count):
    return lax.ppermute(array, "dp", [(i, i ^ step) for i in range(count)])


def add(left, right):
    return (left.astype(jnp.float32) + right.astype(jnp.float32)).astype(jnp.bfloat16)


def per_device(count, hidden_in, query_weight, saved_keys, saved_values, grad_out):
    bits = count.bit_length() - 1
    wide = min(3, bits - 1)
    blocks = 1 << wide
    groups = [
        [high << (wide + 1) | (place ^ (high & 1) * (blocks >> 1)) << 1 | core for place in range(blocks)]
        for high in range(count >> (wide + 1))
        for core in range(2)
    ]
    if hidden_in.shape[1] != query_weight.shape[1]:
        hidden_in = lax.all_gather(hidden_in, "tensor", axis=1, tiled=True)
    core = (lax.axis_index("dp") & 1).astype(jnp.int32).reshape(1)
    other, own, grad_query = rows_of(
        blocks, core, hidden_in, query_weight, saved_keys, saved_values, grad_out
    )
    chip = add(own, swap(other, 1, count))
    parts = lax.all_to_all(chip, "dp", 0, 0, axis_index_groups=groups)
    total = jnp.sum(parts.astype(jnp.float32), axis=0).astype(jnp.bfloat16)
    grad_query, total = lax.optimization_barrier((grad_query, total))
    input_terms = jnp.dot(grad_query, query_weight, preferred_element_type=jnp.float32)
    grad_hidden = lax.psum_scatter(
        input_terms.astype(jnp.bfloat16), "tensor", scatter_dimension=1, tiled=True
    )
    for bit in range(wide + 1, bits):
        total = add(total, swap(total, 3 << wide if bit == wide + 1 else 1 << bit, count))
    copies = jnp.broadcast_to(total[None], (blocks, *total.shape))
    gathered = lax.all_to_all(copies, "dp", 0, 0, axis_index_groups=groups)
    grad_query_weight = assemble(core, gathered, swap(gathered, 1, count))
    return (grad_query_weight, grad_hidden)


def solution(mesh):
    count = mesh.shape["dp"]
    placed = (
        P("dp", "tensor"),
        P("tensor", None),
        P("dp", "tensor"),
        P("dp", "tensor"),
        P("dp", "tensor"),
    )
    return jax.shard_map(
        functools.partial(per_device, count),
        mesh=mesh,
        in_specs=placed,
        out_specs=(P("tensor", None), P("dp", "tensor")),
        check_vma=False,
    )
```

time: 109 us -> 72.2 us (0.66)
  blocking collectives: 94 us -> 39.7 us
  Pallas kernels: 0 us -> 11.1 us
  matrix products: 11.2 us -> 3.26 us
  waiting for transfers between devices: 0 us -> 6.57 us
  local copies, waits for them, and re-layouts: 2.14 us -> 6.49 us
  starting transfers between devices: 0 us -> 3.18 us
    psum x1 -> x0, blocking collectives: 94 us -> none  [per_device(): grad_query_weight = lax.psum(grad_rows, 'dp').astype(jnp.bfloat16)]
    all_to_all x0 -> x2, blocking collectives: none -> 39.7 us  [the longest x1 21.2 us: per_device(): parts = lax.all_to_all(chip, 'dp', 0, 0, axis_index_groups=groups)]
    pallas_call x0 -> x2, Pallas kernels: none -> 11.1 us  [the longest x1 9.7 us: rows_of(): pl.pallas_call(functools.partial(rows_kernel, blocks), out_shape=(jax.Sha...]
    dot_general x8 -> x0, matrix products: 7.96 us -> none  [the longest x1 3.75 us: per_device(): lax.dot_general(whole_in, query_weight, (((1,), (1,)), ((), ())), preferr...]
    ppermute x0 -> x3, waiting for transfers between devices: none -> 6.57 us  [swap(): return lax.ppermute(array, 'dp', [(i, i ^ step) for i in range(count)])]
    unnamed x10, local copies, waits for them, and re-layouts: 2.14 us -> 6.37 us
    ppermute x0 -> x3, starting transfers between devices: none -> 3.18 us  [swap(): return lax.ppermute(array, 'dp', [(i, i ^ step) for i in range(count)])]
  transfers between devices with their start and end apart: 0 -> 3, of which waited for: 0 -> 2; matrix products, arithmetic and copies ran while one was open for 0% -> 5% of each run, Pallas kernels for 0% -> 0%
where the time goes in v2:
time: 72.2 us; the launch traced here: 71.7 us
  blocking collectives  39.7 us (55%)
  Pallas kernels  11.1 us (15%)
  waiting for transfers between devices  6.57 us (9%)
  local copies, waits for them, and re-layouts  6.49 us (9%)
  matrix products  3.26 us (5%)
  starting transfers between devices  3.18 us (4%)
    all_to_all x1, blocking collectives, per_device(): parts = lax.all_to_all(chip, 'dp', 0, 0, axis_index_groups=groups)  21.2 us
    all_to_all x1, blocking collectives, per_device(): gathered = lax.all_to_all(copies, 'dp', 0, 0, axis_index_groups=groups)  18.5 us
    pallas_call x1, Pallas kernels, rows_of(): pl.pallas_call(functools.partial(rows_kernel, blocks), out_shape=(jax.Sha...  9.7 us
    ppermute x3, waiting for transfers between devices, swap(): return lax.ppermute(array, 'dp', [(i, i ^ step) for i in range(count)])  6.57 us
    unnamed x10, local copies, waits for them, and re-layouts  6.37 us
    dot_general x1, matrix products, per_device(): jnp.dot(grad_query, query_weight, preferred_element_type=jnp.float32)  3.26 us
    ppermute x3, starting transfers between devices, swap(): return lax.ppermute(array, 'dp', [(i, i ^ step) for i in range(count)])  3.18 us
  transfers between devices with their start and end apart: 3, of which 2 were waited for; matrix products, arithmetic and copies ran while one was open for 5% of the time, Pallas kernels for 0%

profile of v2, /device:TPU:0, one launch (start us, length us, event | category | flops | bytes accessed | tf_op | source)
XLA Modules:
  0.0 71.7 jit_solution(9950764676673334045)
XLA Ops:
  0.6 0.9 %copy.7.keys_ref = bf16[256,64]{1,0:T(8,128)(2,1)S(1)} copy(bf16[256,64]{0,1:T(8,128)(2,1)} %param.7) | data formatting | bytes 65536 | tf_op args[2]
  1.5 0.9 %copy.8.values_ref = bf16[256,64]{1,0:T(8,128)(2,1)S(1)} copy(bf16[256,64]{0,1:T(8,128)(2,1)} %param.8) | data formatting | bytes 65536 | tf_op args[3]
  2.4 0.0 copy-start
  2.4 1.6 %copy-done = bf16[128,8192]{1,0:T(8,128)(2,1)S(1)} copy-done((bf16[128,8192]{1,0:T(8,128)(2,1)S(1)}, bf16[128,8192]{1,0:T(8,128)(2,1)}, u32[]{:S(2)}) %copy-start) | copy-done | bytes 2097176
  4.0 0.0 copy-start.2
  4.0 2.2 %copy-done.2 = bf16[256,8192]{1,0:T(8,128)(2,1)S(1)} copy-done((bf16[256,8192]{1,0:T(8,128)(2,1)S(1)}, bf16[256,8192]{1,0:T(8,128)(2,1)}, u32[]{:S(2)}) %copy-start.2) | copy-done | bytes 4194328
  6.2 0.0 copy-start.3
  6.2 0.8 %copy-done.3 = bf16[256,128]{1,0:T(8,128)(2,1)S(1)} copy-done((bf16[256,128]{1,0:T(8,128)(2,1)S(1)}, bf16[256,128]{1,0:T(8,128)(2,1)}, u32[]{:S(2)}) %copy-start.3) | copy-done | bytes 65560
  7.0 9.7 %shard_map.68 = (bf16[8,64,1024]{2,1,0:T(8,128)(2,1)S(1)}, bf16[8,64,1024]{2,1,0:T(8,128)(2,1)S(1)}, bf16[256,128]{1,0:T(8,128)(2,1)S(1)}) custom-call(s32[1]{0:T(128)} %bitcast.core_ref, bf16[256,8192]{1,0:T(8,128)(2,1)S(1)} %copy-done.2, bf16[128,8192]{1,0:T(8,128)(2,1)S(1)} %copy-done, bf16[256,64]{1,0:T(8,128)(2,1)S(1)} %copy.7.keys_ref, ...), custom_call_target="tpu_custom_call" | custom-call | flops 1073741824 | bytes 8388608 | tf_op jit(solution)/shard_map/pallas_call | solution.py:109
  16.7 0.5 collective-permute-start
  17.2 2.3 %collective-permute-done = bf16[8,64,1024]{2,1,0:T(8,128)(2,1)S(1)} collective-permute-done((bf16[8,64,1024]{2,1,0:T(8,128)(2,1)S(1)}, bf16[8,64,1024]{2,1,0:T(8,128)(2,1)S(1)}, u32[]{:S(2)}, u32[]{:S(2)}) %collective-permute-start) | collective-permute-done | bytes 1048608 | tf_op jit(solution)/shard_map/ppermute | solution.py:166
  19.5 0.4 add_convert_fusion
  20.0 21.2 %all_to_all.10 = bf16[8,64,1024]{2,1,0:T(8,128)(2,1)S(1)} all-to-all(bf16[8,64,1024]{2,1,0:T(8,128)(2,1)S(1)} %add_convert_fusion), channel_id=1, replica_groups={{0,2,4,6,8,10,12,14},{1,3,5,7,9,11,13,15},{24,26,28,30,16,18,20,22},{25..., dimensions={0} | all-to-all | bytes 2097152 | tf_op jit(solution)/shard_map/all_to_all | solution.py:189
  41.2 0.2 reduce_sum.12
  41.4 0.0 copy-start.1
  41.4 2.7 %collective-permute-start.1 = (bf16[64,1024]{1,0:T(8,128)(2,1)S(1)}, bf16[64,1024]{1,0:T(8,128)(2,1)S(1)}, u32[]{:S(2)}, u32[]{:S(2)}) collective-permute-start(bf16[64,1024]{1,0:T(8,128)(2,1)S(1)} %reduce_sum.12), channel_id=1, source_target_pairs={{0,24},{1,25},{2,26},{3,27},{4,28},{5,29},{6,30},{7,31},{8,16},{9,... | collective-permute-start | bytes 393224 | tf_op jit(solution)/shard_map/ppermute | solution.py:166
  44.1 4.3 %collective-permute-done.1 = bf16[64,1024]{1,0:T(8,128)(2,1)S(1)} collective-permute-done((bf16[64,1024]{1,0:T(8,128)(2,1)S(1)}, bf16[64,1024]{1,0:T(8,128)(2,1)S(1)}, u32[]{:S(2)}, u32[]{:S(2)}) %collective-permute-start.1) | collective-permute-done | bytes 131104 | tf_op jit(solution)/shard_map/ppermute | solution.py:166
  48.4 0.1 broadcast_in_dim.2
  48.5 18.5 %all_to_all.11.own_hbm = bf16[8,64,1024]{2,1,0:T(8,128)(2,1)S(1)} all-to-all(bf16[8,64,1024]{2,1,0:T(8,128)(2,1)S(1)} %broadcast_in_dim.2), channel_id=1, replica_groups={{0,2,4,6,8,10,12,14},{1,3,5,7,9,11,13,15},{24,26,28,30,16,18,20,22},{25..., dimensions={0} | all-to-all | bytes 2097152 | tf_op jit(solution)/shard_map/all_to_all | solution.py:199
  67.0 0.0 collective-permute-start.2
  67.0 0.0 copy-done.1
  67.0 3.3 %convolution_convert_fusion = bf16[256,8192]{1,0:T(8,128)(2,1)} fusion(bf16[256,128]{1,0:T(8,128)(2,1)S(1)} %get-tuple-element.11, bf16[128,8192]{1,0:T(8,128)(2,1)S(1)} %copy-done.1), kind=kOutput, calls=%fused_computation | convolution fusion | flops 538968064 | bytes 6356992 | tf_op jit(solution)/shard_map/dot_general | solution.py:192
  70.2 0.0 collective-permute-done.2.other_hbm
  70.2 1.4 %shard_map.69 = bf16[128,8192]{1,0:T(8,128)(2,1)} custom-call(s32[1]{0:T(128)} %bitcast.core_ref, bf16[8,64,1024]{2,1,0:T(8,128)(2,1)S(1)} %all_to_all.11.own_hbm, bf16[8,64,1024]{2,1,0:T(8,128)(2,1)S(1)} %collective-permute-done.2.other_hbm), custom_call_target="tpu_custom_call" | custom-call | bytes 4194304 | tf_op jit(solution)/shard_map/pallas_call | solution.py:154
  (1 shorter events, 0.0 us)
Async XLA Ops:
  2.4 1.6 %copy-start = (bf16[128,8192]{1,0:T(8,128)(2,1)S(1)}, bf16[128,8192]{1,0:T(8,128)(2,1)}, u32[]{:S(2)}) copy-start(bf16[128,8192]{1,0:T(8,128)(2,1)} %weight_hbm.1) | copy-start | bytes 6291460
  4.0 2.2 %copy-start.2 = (bf16[256,8192]{1,0:T(8,128)(2,1)S(1)}, bf16[256,8192]{1,0:T(8,128)(2,1)}, u32[]{:S(2)}) copy-start(bf16[256,8192]{1,0:T(8,128)(2,1)} %hidden_hbm.1) | copy-start | bytes 12582916
  6.2 0.8 %copy-start.3 = (bf16[256,128]{1,0:T(8,128)(2,1)S(1)}, bf16[256,128]{1,0:T(8,128)(2,1)}, u32[]{:S(2)}) copy-start(bf16[256,128]{1,0:T(8,128)(2,1)} %grad_out_ref.1) | copy-start | bytes 196612
  16.7 2.8 %collective-permute-start = (bf16[8,64,1024]{2,1,0:T(8,128)(2,1)S(1)}, bf16[8,64,1024]{2,1,0:T(8,128)(2,1)S(1)}, u32[]{:S(2)}, u32[]{:S(2)}) collective-permute-start(bf16[8,64,1024]{2,1,0:T(8,128)(2,1)S(1)} %get-tuple-element.9), channel_id=1, source_target_pairs={{0,1},{1,0},{2,3},{3,2},{4,5},{5,4},{6,7},{7,6},{8,9},{9,8},{10,11... | collective-permute-start | bytes 3145736 | tf_op jit(solution)/shard_map/ppermute | solution.py:166
  41.4 25.6 %copy-start.1 = (bf16[128,8192]{1,0:T(8,128)(2,1)S(1)}, bf16[128,8192]{1,0:T(8,128)(2,1)}, u32[]{:S(2)}) copy-start(bf16[128,8192]{1,0:T(8,128)(2,1)} %weight_hbm.1) | copy-start | bytes 6291460
  41.4 6.9 %collective-permute-start.1 = (bf16[64,1024]{1,0:T(8,128)(2,1)S(1)}, bf16[64,1024]{1,0:T(8,128)(2,1)S(1)}, u32[]{:S(2)}, u32[]{:S(2)}) collective-permute-start(bf16[64,1024]{1,0:T(8,128)(2,1)S(1)} %reduce_sum.12), channel_id=1, source_target_pairs={{0,24},{1,25},{2,26},{3,27},{4,28},{5,29},{6,30},{7,31},{8,16},{9,... | collective-permute-start | bytes 393224 | tf_op jit(solution)/shard_map/ppermute | solution.py:166
  67.0 3.3 %collective-permute-start.2 = (bf16[8,64,1024]{2,1,0:T(8,128)(2,1)S(1)}, bf16[8,64,1024]{2,1,0:T(8,128)(2,1)S(1)}, u32[]{:S(2)}, u32[]{:S(2)}) collective-permute-start(bf16[8,64,1024]{2,1,0:T(8,128)(2,1)S(1)} %all_to_all.11.own_hbm), channel_id=1, source_target_pairs={{0,1},{1,0},{2,3},{3,2},{4,5},{5,4},{6,7},{7,6},{8,9},{9,8},{10,11... | collective-permute-start | bytes 3145736 | tf_op jit(solution)/shard_map/ppermute | solution.py:166

commit v3 on v2

v3 whole, which is shorter than its diff:
```python
import functools

import jax
import jax.numpy as jnp
from jax import lax
from jax.experimental import pallas as pl
from jax.experimental.pallas import tpu as pltpu
from jax.sharding import PartitionSpec as P

VMEM_LIMIT = 40 * 1024 * 1024
ANY = pl.BlockSpec(memory_space=pl.ANY)
SCALAR = pl.BlockSpec(memory_space=pltpu.SMEM)


def dot(left, right):
    return jnp.dot(left, right, preferred_element_type=jnp.float32)


def dot_tt(left, right):
    return lax.dot_general(left, right, (((1,), (1,)), ((), ())), preferred_element_type=jnp.float32)


def head_grad(query, keys, values, grad_out):
    head_size, length = keys.shape
    score_scale = head_size ** (-0.5)
    causal_mask = lax.broadcasted_iota(jnp.int32, (length, length), 1) <= lax.broadcasted_iota(
        jnp.int32, (length, length), 0
    )
    scores = jnp.where(causal_mask, dot(query, keys) * score_scale, -1e30)
    raised = jnp.exp(scores - jnp.max(scores, axis=1, keepdims=True))
    attn_weights = raised * (1.0 / jnp.sum(raised, axis=1, keepdims=True))
    grad_prob = dot(grad_out, values)
    row_delta = jnp.sum(attn_weights * grad_prob, axis=1, keepdims=True)
    grad_score = (attn_weights * (grad_prob - row_delta) * score_scale).astype(jnp.bfloat16)
    return dot_tt(grad_score, keys).astype(jnp.bfloat16)


def turned_round(first, array):
    half = array.shape[1] // 2
    low, high = array[:, :half], array[:, half:]
    return jnp.concatenate([jnp.where(first, low, high), jnp.where(first, high, low)], axis=1)


def query_kernel(
    blocks, core_ref, hidden_hbm, weight_hbm, keys_hbm, values_hbm, grad_out_hbm,
    other_hbm, grad_query_hbm,
    hidden, weight, keys, values, grad_out, other, grad_query, hidden_sem, weight_sem, small_sem, out_sem,
):
    tokens, width = hidden.shape
    rows = weight.shape[0]
    head_size = keys.shape[0]
    step = width // blocks
    core = core_ref[0]
    copies = []
    for block in range(blocks):
        columns = pl.ds(block * step, step)
        pair = [
            pltpu.make_async_copy(weight_hbm.at[:, columns], weight.at[:, columns], weight_sem.at[block]),
            pltpu.make_async_copy(hidden_hbm.at[:, columns], hidden.at[:, columns], hidden_sem.at[block]),
        ]
        for copy in pair:
            copy.start()
        copies.append(pair)
    small = [
        pltpu.make_async_copy(source, target, small_sem.at[place])
        for place, (source, target) in enumerate(
            ((keys_hbm, keys), (values_hbm, values), (grad_out_hbm, grad_out))
        )
    ]
    for copy in small:
        copy.start()
    total = jnp.zeros((tokens, rows), jnp.float32)
    for block in range(blocks):
        for copy in copies[block]:
            copy.wait()
        columns = pl.ds(block * step, step)
        total += dot_tt(hidden[:, columns], weight[:, columns])
    query = total.astype(jnp.bfloat16)
    for copy in small:
        copy.wait()
    given = grad_out[...]
    grads = jnp.concatenate(
        [
            head_grad(
                query[:, low : low + head_size], keys[...], values[...], given[:, low : low + head_size]
            )
            for low in range(0, rows, head_size)
        ],
        axis=1,
    )
    grad_query[...] = grads
    sent = [pltpu.make_async_copy(grad_query, grad_query_hbm, small_sem.at[3])]
    sent[0].start()
    half = rows // 2
    turned = jnp.where(core == 0, grads[:, half:], grads[:, :half]).T
    for block in range(blocks):
        term = dot(turned, hidden[:, pl.ds(block * step, step)])
        other[block] = term.astype(jnp.bfloat16)
        sent.append(pltpu.make_async_copy(other.at[block], other_hbm.at[block], out_sem.at[block]))
        sent[-1].start()
    for copy in sent:
        copy.wait()


def query_and_other(blocks, core, hidden_in, query_weight, keys, values, grad_out):
    tokens, width = hidden_in.shape
    rows = query_weight.shape[0]
    piece = (blocks, rows // 2, width // blocks)
    like = lambda array: pltpu.VMEM(array.shape, array.dtype)
    return pl.pallas_call(
        functools.partial(query_kernel, blocks),
        out_shape=(
            jax.ShapeDtypeStruct(piece, jnp.bfloat16),
            jax.ShapeDtypeStruct((tokens, rows), jnp.bfloat16),
        ),
        in_specs=[SCALAR] + [ANY] * 5,
        out_specs=(ANY, ANY),
        scratch_shapes=[
            like(hidden_in),
            like(query_weight),
            like(keys),
            like(values),
            like(grad_out),
            pltpu.VMEM(piece, jnp.bfloat16),
            pltpu.VMEM((tokens, rows), jnp.bfloat16),
            pltpu.SemaphoreType.DMA((blocks,)),
            pltpu.SemaphoreType.DMA((blocks,)),
            pltpu.SemaphoreType.DMA((4,)),
            pltpu.SemaphoreType.DMA((blocks,)),
        ],
        compiler_params=pltpu.CompilerParams(vmem_limit_bytes=VMEM_LIMIT),
        cost_estimate=pl.CostEstimate(
            flops=3 * tokens * width * rows,
            bytes_accessed=2 * (tokens * width + rows * width),
            transcendentals=tokens * tokens * 2,
        ),
    )(core, *(pltpu.with_memory_space_constraint(x, pltpu.HBM) for x in (hidden_in, query_weight, keys, values, grad_out)))


def own_kernel(core_ref, grad_query_hbm, hidden_hbm, own_hbm, grad_query, hidden, own, in_sem, hidden_sem, out_sem):
    blocks, half, step = own.shape
    first = pltpu.make_async_copy(grad_query_hbm, grad_query, in_sem)
    first.start()
    copies = []
    for block in range(blocks):
        columns = pl.ds(block * step, step)
        copies.append(
            pltpu.make_async_copy(hidden_hbm.at[:, columns], hidden.at[:, columns], hidden_sem.at[block])
        )
        copies[-1].start()
    first.wait()
    turned = jnp.where(core_ref[0] == 0, grad_query[:, :half], grad_query[:, half:]).T
    sent = []
    for block in range(blocks):
        copies[block].wait()
        own[block] = dot(turned, hidden[:, pl.ds(block * step, step)]).astype(jnp.bfloat16)
        sent.append(pltpu.make_async_copy(own.at[block], own_hbm.at[block], out_sem.at[block]))
        sent[-1].start()
    for copy in sent:
        copy.wait()


def own_rows(blocks, core, grad_query, hidden_in):
    tokens, width = hidden_in.shape
    rows = grad_query.shape[1]
    piece = (blocks, rows // 2, width // blocks)
    return pl.pallas_call(
        own_kernel,
        out_shape=jax.ShapeDtypeStruct(piece, jnp.bfloat16),
        in_specs=[SCALAR, ANY, ANY],
        out_specs=ANY,
        scratch_shapes=[
            pltpu.VMEM((tokens, rows), jnp.bfloat16),
            pltpu.VMEM((tokens, width), jnp.bfloat16),
            pltpu.VMEM(piece, jnp.bfloat16),
            pltpu.SemaphoreType.DMA(()),
            pltpu.SemaphoreType.DMA((blocks,)),
            pltpu.SemaphoreType.DMA((blocks,)),
        ],
        compiler_params=pltpu.CompilerParams(vmem_limit_bytes=VMEM_LIMIT),
        cost_estimate=pl.CostEstimate(
            flops=tokens * width * rows, bytes_accessed=2 * tokens * width, transcendentals=0
        ),
    )(core, grad_query, pltpu.with_memory_space_constraint(hidden_in, pltpu.HBM))


def place_kernel(core_ref, piece_hbm, out_hbm, sem):
    blocks, half, step = piece_hbm.shape
    rows = pl.ds(pl.multiple_of(core_ref[0] * half, half), half)
    copies = [
        pltpu.make_async_copy(piece_hbm.at[block], out_hbm.at[rows, pl.ds(block * step, step)], sem.at[block])
        for block in range(blocks)
    ]
    for copy in copies:
        copy.start()
    for copy in copies:
        copy.wait()


def place_kernel_on(core_ref, piece_hbm, before_hbm, out_hbm, sem):
    place_kernel(core_ref, piece_hbm, out_hbm, sem)


def place(core, piece, before=None):
    blocks, half, step = piece.shape
    return pl.pallas_call(
        place_kernel if before is None else place_kernel_on,
        out_shape=jax.ShapeDtypeStruct((2 * half, blocks * step), jnp.bfloat16),
        in_specs=[SCALAR, ANY] + [ANY] * (before is not None),
        out_specs=ANY,
        scratch_shapes=[pltpu.SemaphoreType.DMA((blocks,))],
        input_output_aliases={} if before is None else {2: 0},
        compiler_params=pltpu.CompilerParams(vmem_limit_bytes=VMEM_LIMIT),
        cost_estimate=pl.CostEstimate(flops=0, bytes_accessed=4 * half * blocks * step, transcendentals=0),
    )(core, piece, *(() if before is None else (before,)))


def swap(array, step, count):
    return lax.ppermute(array, "dp", [(i, i ^ step) for i in range(count)])


def add(left, right):
    return (left.astype(jnp.float32) + right.astype(jnp.float32)).astype(jnp.bfloat16)


def per_device(count, hidden_in, query_weight, saved_keys, saved_values, grad_out):
    bits = count.bit_length() - 1
    wide = min(3, bits - 1)
    blocks = 1 << wide
    groups = [
        [high << (wide + 1) | (place ^ (high & 1) * (blocks >> 1)) << 1 | core for place in range(blocks)]
        for high in range(count >> (wide + 1))
        for core in range(2)
    ]
    if hidden_in.shape[1] != query_weight.shape[1]:
        hidden_in = lax.all_gather(hidden_in, "tensor", axis=1, tiled=True)
    core = (lax.axis_index("dp") & 1).astype(jnp.int32).reshape(1)
    other, grad_query = query_and_other(
        blocks, core, hidden_in, query_weight, saved_keys.T, saved_values.T, grad_out
    )
    arriving = swap(other, 1, count)
    own = own_rows(blocks, core, grad_query, hidden_in)
    chip = add(own, arriving)
    parts = lax.all_to_all(chip, "dp", 0, 0, axis_index_groups=groups)
    total = jnp.sum(parts.astype(jnp.float32), axis=0).astype(jnp.bfloat16)
    grad_query, total = lax.optimization_barrier((grad_query, total))
    input_terms = dot(grad_query, query_weight)
    grad_hidden = lax.psum_scatter(
        input_terms.astype(jnp.bfloat16), "tensor", scatter_dimension=1, tiled=True
    )
    for bit in range(wide + 1, bits):
        arriving = swap(total, 3 << wide if bit == wide + 1 else 1 << bit, count)
        if bit == wide + 1:
            arriving, grad_hidden = lax.optimization_barrier((arriving, grad_hidden))
        total = add(total, arriving)
    copies = jnp.broadcast_to(total[None], (blocks, *total.shape))
    gathered = lax.all_to_all(copies, "dp", 0, 0, axis_index_groups=groups)
    arriving = swap(gathered, 1, count)
    grad_query_weight = place(1 - core, arriving, place(core, gathered))
    return (grad_query_weight, grad_hidden)


def solution(mesh):
    count = mesh.shape["dp"]
    placed = (
        P("dp", "tensor"),
        P("tensor", None),
        P("dp", "tensor"),
        P("dp", "tensor"),
        P("dp", "tensor"),
    )
    return jax.shard_map(
        functools.partial(per_device, count),
        mesh=mesh,
        in_specs=placed,
        out_specs=(P("tensor", None), P("dp", "tensor")),
        check_vma=False,
    )
```

time: 72.2 us -> 65.7 us (0.910)
  local copies, waits for them, and re-layouts: 6.49 us -> 0.12 us
  Pallas kernels: 11.1 us -> 15.2 us
  waiting for transfers between devices: 6.57 us -> 2.65 us
    unnamed x10 -> x2, local copies, waits for them, and re-layouts: 6.37 us -> 0.01 us
    pallas_call x2 -> x4, Pallas kernels: 11.1 us -> 15.2 us  [the longest x1 8.95 us: query_and_other(): pl.pallas_call(functools.partial(query_kernel, blocks), out_shape=(jax.Sh...]
    ppermute x3, waiting for transfers between devices: 6.57 us -> 2.65 us  [swap(): return lax.ppermute(array, 'dp', [(i, i ^ step) for i in range(count)])]
  transfers between devices with their start and end apart: 3 -> 3, of which waited for: 2 -> 2; matrix products, arithmetic and copies ran while one was open for 5% -> 5% of each run, Pallas kernels for 0% -> 8%
where the time goes in v3:
time: 65.7 us; the launch traced here: 65.5 us
  blocking collectives  39.7 us (60%)
  Pallas kernels  15.2 us (23%)
  matrix products  3.26 us (5%)
  starting transfers between devices  3.17 us (5%)
  waiting for transfers between devices  2.65 us (4%)
  between operations  0.7 us (1%)
    all_to_all x1, blocking collectives, per_device(): parts = lax.all_to_all(chip, 'dp', 0, 0, axis_index_groups=groups)  21.4 us
    all_to_all x1, blocking collectives, per_device(): gathered = lax.all_to_all(copies, 'dp', 0, 0, axis_index_groups=groups)  18.4 us
    pallas_call x1, Pallas kernels, query_and_other(): pl.pallas_call(functools.partial(query_kernel, blocks), out_shape=(jax.Sh...  8.95 us
    pallas_call x1, Pallas kernels, own_rows(): pl.pallas_call(own_kernel, out_shape=jax.ShapeDtypeStruct(piece, jnp.bflo...  4.23 us
    dot_general x1, matrix products, dot(): return jnp.dot(left, right, preferred_element_type=jnp.float32)  3.26 us
    ppermute x3, starting transfers between devices, swap(): return lax.ppermute(array, 'dp', [(i, i ^ step) for i in range(count)])  3.17 us
    ppermute x3, waiting for transfers between devices, swap(): return lax.ppermute(array, 'dp', [(i, i ^ step) for i in range(count)])  2.65 us
    pallas_call x2, Pallas kernels, place(): pl.pallas_call(place_kernel if before is None else place_kernel_on, out_s...  2.05 us
  transfers between devices with their start and end apart: 3, of which 2 were waited for; matrix products, arithmetic and copies ran while one was open for 5% of the time, Pallas kernels for 8%

profile of v3, /device:TPU:0, one launch (start us, length us, event | category | flops | bytes accessed | tf_op | source)
XLA Modules:
  0.0 65.5 jit_solution(14997823288454428102)
XLA Ops:
  0.6 9.0 %shard_map.68 = (bf16[8,64,1024]{2,1,0:T(8,128)(2,1)S(1)}, bf16[256,128]{1,0:T(8,128)(2,1)S(1)}) custom-call(s32[1]{0:T(128)} %bitcast.core_ref, bf16[256,8192]{1,0:T(8,128)(2,1)} %hidden_hbm.3, bf16[128,8192]{1,0:T(8,128)(2,1)} %weight_hbm.1, bf16[64,256]{1,0:T(8,128)(2,1)} %bitcast.5, bf16[64,256]{1,0:T(8,128)(2,1)} %bitcast.6, bf16[256,128]{1,0:T(8,128)(2,1)} %grad_out_hbm.1), custom_call_target="tpu_custom_call" | custom-call | flops 805306368 | bytes 6291456 | tf_op jit(solution)/shard_map/pallas_call | solution.py:110
  9.6 0.5 collective-permute-start
  10.1 4.2 %shard_map.69 = bf16[8,64,1024]{2,1,0:T(8,128)(2,1)S(1)} custom-call(s32[1]{0:T(128)} %bitcast.core_ref, bf16[256,128]{1,0:T(8,128)(2,1)S(1)} %get-tuple-element.11.grad_query_hbm, bf16[256,8192]{1,0:T(8,128)(2,1)} %hidden_hbm.3), custom_call_target="tpu_custom_call" | custom-call | flops 268435456 | bytes 4194304 | tf_op jit(solution)/shard_map/pallas_call | solution.py:167
  14.3 0.0 collective-permute-done
  14.4 0.4 add_convert_fusion
  14.8 0.0 copy-start
  14.8 21.4 %all_to_all.10 = bf16[8,64,1024]{2,1,0:T(8,128)(2,1)S(1)} all-to-all(bf16[8,64,1024]{2,1,0:T(8,128)(2,1)S(1)} %add_convert_fusion), channel_id=1, replica_groups={{0,2,4,6,8,10,12,14},{1,3,5,7,9,11,13,15},{24,26,28,30,16,18,20,22},{25..., dimensions={0} | all-to-all | bytes 2097152 | tf_op jit(solution)/shard_map/all_to_all | solution.py:244
  36.2 0.2 reduce_sum.12
  36.4 2.7 %collective-permute-start.1 = (bf16[64,1024]{1,0:T(8,128)(2,1)S(1)}, bf16[64,1024]{1,0:T(8,128)(2,1)S(1)}, u32[]{:S(2)}, u32[]{:S(2)}) collective-permute-start(bf16[64,1024]{1,0:T(8,128)(2,1)S(1)} %reduce_sum.12), channel_id=1, source_target_pairs={{0,24},{1,25},{2,26},{3,27},{4,28},{5,29},{6,30},{7,31},{8,16},{9,... | collective-permute-start | bytes 393224 | tf_op jit(solution)/shard_map/ppermute | solution.py:219
  39.0 0.0 copy-done
  39.0 3.3 %convolution_convert_fusion = bf16[256,8192]{1,0:T(8,128)(2,1)} fusion(bf16[256,128]{1,0:T(8,128)(2,1)S(1)} %get-tuple-element.11.grad_query_hbm, bf16[128,8192]{1,0:T(8,128)(2,1)S(1)} %copy-done), kind=kOutput, calls=%fused_computation | convolution fusion | flops 538968064 | bytes 6356992 | tf_op jit(solution)/shard_map/dot_general | solution.py:16
  42.3 1.0 %collective-permute-done.1 = bf16[64,1024]{1,0:T(8,128)(2,1)S(1)} collective-permute-done((bf16[64,1024]{1,0:T(8,128)(2,1)S(1)}, bf16[64,1024]{1,0:T(8,128)(2,1)S(1)}, u32[]{:S(2)}, u32[]{:S(2)}) %collective-permute-start.1) | collective-permute-done | bytes 131104 | tf_op jit(solution)/shard_map/ppermute | solution.py:219
  43.3 0.1 broadcast_in_dim.2
  43.5 18.4 %all_to_all.11.piece_hbm = bf16[8,64,1024]{2,1,0:T(8,128)(2,1)S(1)} all-to-all(bf16[8,64,1024]{2,1,0:T(8,128)(2,1)S(1)} %broadcast_in_dim.2), channel_id=1, replica_groups={{0,2,4,6,8,10,12,14},{1,3,5,7,9,11,13,15},{24,26,28,30,16,18,20,22},{25..., dimensions={0} | all-to-all | bytes 2097152 | tf_op jit(solution)/shard_map/all_to_all | solution.py:257
  61.8 0.0 collective-permute-start.2
  61.8 1.0 %shard_map.70.before_hbm = bf16[128,8192]{1,0:T(8,128)(2,1)} custom-call(s32[1]{0:T(128)} %bitcast.core_ref, bf16[8,64,1024]{2,1,0:T(8,128)(2,1)S(1)} %all_to_all.11.piece_hbm), custom_call_target="tpu_custom_call" | custom-call | bytes 2097152 | tf_op jit(solution)/shard_map/pallas_call | solution.py:206
  62.9 1.6 %collective-permute-done.2.piece_hbm = bf16[8,64,1024]{2,1,0:T(8,128)(2,1)S(1)} collective-permute-done((bf16[8,64,1024]{2,1,0:T(8,128)(2,1)S(1)}, bf16[8,64,1024]{2,1,0:T(8,128)(2,1)S(1)}, u32[]{:S(2)}, u32[]{:S(2)}) %collective-permute-start.2) | collective-permute-done | bytes 1048608 | tf_op jit(solution)/shard_map/ppermute | solution.py:219
  64.5 1.0 %shard_map.71 = bf16[128,8192]{1,0:T(8,128)(2,1)} custom-call(s32[1]{0:T(128)S(6)} %sub.3.core_ref, bf16[8,64,1024]{2,1,0:T(8,128)(2,1)S(1)} %collective-permute-done.2.piece_hbm, bf16[128,8192]{1,0:T(8,128)(2,1)} %shard_map.70.before_hbm), custom_call_target="tpu_custom_call", output_to_operand_aliasing={{}: (2, {})} | custom-call | bytes 2097152 | tf_op jit(solution)/shard_map/pallas_call | solution.py:206
  (1 shorter events, 0.0 us)
Async XLA Ops:
  9.6 4.8 %collective-permute-start = (bf16[8,64,1024]{2,1,0:T(8,128)(2,1)S(1)}, bf16[8,64,1024]{2,1,0:T(8,128)(2,1)S(1)}, u32[]{:S(2)}, u32[]{:S(2)}) collective-permute-start(bf16[8,64,1024]{2,1,0:T(8,128)(2,1)S(1)} %get-tuple-element.9), channel_id=1, source_target_pairs={{0,1},{1,0},{2,3},{3,2},{4,5},{5,4},{6,7},{7,6},{8,9},{9,8},{10,11... | collective-permute-start | bytes 3145736 | tf_op jit(solution)/shard_map/ppermute | solution.py:219
  14.8 24.2 %copy-start = (bf16[128,8192]{1,0:T(8,128)(2,1)S(1)}, bf16[128,8192]{1,0:T(8,128)(2,1)}, u32[]{:S(2)}) copy-start(bf16[128,8192]{1,0:T(8,128)(2,1)} %weight_hbm.1) | copy-start | bytes 6291460
  36.4 6.9 %collective-permute-start.1 = (bf16[64,1024]{1,0:T(8,128)(2,1)S(1)}, bf16[64,1024]{1,0:T(8,128)(2,1)S(1)}, u32[]{:S(2)}, u32[]{:S(2)}) collective-permute-start(bf16[64,1024]{1,0:T(8,128)(2,1)S(1)} %reduce_sum.12), channel_id=1, source_target_pairs={{0,24},{1,25},{2,26},{3,27},{4,28},{5,29},{6,30},{7,31},{8,16},{9,... | collective-permute-start | bytes 393224 | tf_op jit(solution)/shard_map/ppermute | solution.py:219
  61.8 2.7 %collective-permute-start.2 = (bf16[8,64,1024]{2,1,0:T(8,128)(2,1)S(1)}, bf16[8,64,1024]{2,1,0:T(8,128)(2,1)S(1)}, u32[]{:S(2)}, u32[]{:S(2)}) collective-permute-start(bf16[8,64,1024]{2,1,0:T(8,128)(2,1)S(1)} %all_to_all.11.piece_hbm), channel_id=1, source_target_pairs={{0,1},{1,0},{2,3},{3,2},{4,5},{5,4},{6,7},{7,6},{8,9},{9,8},{10,11... | collective-permute-start | bytes 3145736 | tf_op jit(solution)/shard_map/ppermute | solution.py:219

commit v4 on v3

--- a/solution.py
+++ b/solution.py
@@ -223,15 +223,27 @@
     return (left.astype(jnp.float32) + right.astype(jnp.float32)).astype(jnp.bfloat16)
 
 
-def per_device(count, hidden_in, query_weight, saved_keys, saved_values, grad_out):
+def plan_of(count):
     bits = count.bit_length() - 1
     wide = min(3, bits - 1)
-    blocks = 1 << wide
-    groups = [
-        [high << (wide + 1) | (place ^ (high & 1) * (blocks >> 1)) << 1 | core for place in range(blocks)]
-        for high in range(count >> (wide + 1))
-        for core in range(2)
-    ]
+    group_bits = [list(range(1, wide + 1))] * 2
+    later = [list(range(wide + 1, bits))] * 2
+    if wide and later[1]:
+        group_bits[1] = group_bits[1][:-1] + [wide + 1]
+        later[1] = [wide] + later[1][1:]
+    places = list(range(1 << wide))
+    places = [places[half if way == 0 else -1 - half] for half in range(len(places) // 2) for way in range(2)] or places
+    groups = []
+    for core in range(2):
+        steps = [sum((place >> at & 1) << bit for at, bit in enumerate(group_bits[core])) for place in places]
+        firsts = [core + sum((rest >> at & 1) << bit for at, bit in enumerate(later[core])) for rest in range(count >> (wide + 1))]
+        groups += [[first + step for step in steps] for first in firsts]
+    return groups, [(1 << low, 1 << high) for low, high in zip(*later)]
+
+
+def per_device(count, hidden_in, query_weight, saved_keys, saved_values, grad_out):
+    groups, exchanges = plan_of(count)
+    blocks = len(groups[0])
     if hidden_in.shape[1] != query_weight.shape[1]:
         hidden_in = lax.all_gather(hidden_in, "tensor", axis=1, tiled=True)
     core = (lax.axis_index("dp") & 1).astype(jnp.int32).reshape(1)
@@ -248,9 +260,9 @@
     grad_hidden = lax.psum_scatter(
         input_terms.astype(jnp.bfloat16), "tensor", scatter_dimension=1, tiled=True
     )
-    for bit in range(wide + 1, bits):
-        arriving = swap(total, 3 << wide if bit == wide + 1 else 1 << bit, count)
-        if bit == wide + 1:
+    for at, steps in enumerate(exchanges):
+        arriving = lax.ppermute(total, "dp", [(i, i ^ steps[i & 1]) for i in range(count)])
+        if at == 0:
             arriving, grad_hidden = lax.optimization_barrier((arriving, grad_hidden))
         total = add(total, arriving)
     copies = jnp.broadcast_to(total[None], (blocks, *total.shape))

time: 65.7 us -> 65.9 us (level)
  waiting for transfers between devices: 2.65 us -> 1.93 us
  blocking collectives: 39.7 us -> 40.4 us
    ppermute x0 -> x1, starting transfers between devices: none -> 2.87 us  [per_device(): lax.ppermute(total, 'dp', [(i, i ^ steps[i & 1]) for i in range(count)])]
    ppermute x3 -> x2, starting transfers between devices: 3.17 us -> 0.52 us  [swap(): return lax.ppermute(array, 'dp', [(i, i ^ step) for i in range(count)])]
    ppermute x3 -> x2, waiting for transfers between devices: 2.65 us -> 1.63 us  [swap(): return lax.ppermute(array, 'dp', [(i, i ^ step) for i in range(count)])]
    all_to_all x1, blocking collectives: 18.4 us -> 19 us  [per_device(): gathered = lax.all_to_all(copies, 'dp', 0, 0, axis_index_groups=groups)]
where the time goes in v4:
time: 65.9 us; the launch traced here: 65.7 us
  blocking collectives  40.4 us (61%)
  Pallas kernels  15.2 us (23%)
  starting transfers between devices  3.39 us (5%)
  matrix products  3.25 us (5%)
  waiting for transfers between devices  1.93 us (3%)
  between operations  0.7 us (1%)
    all_to_all x1, blocking collectives, per_device(): parts = lax.all_to_all(chip, 'dp', 0, 0, axis_index_groups=groups)  21.4 us
    all_to_all x1, blocking collectives, per_device(): gathered = lax.all_to_all(copies, 'dp', 0, 0, axis_index_groups=groups)  19 us
    pallas_call x1, Pallas kernels, query_and_other(): pl.pallas_call(functools.partial(query_kernel, blocks), out_shape=(jax.Sh...  8.95 us
    pallas_call x1, Pallas kernels, own_rows(): pl.pallas_call(own_kernel, out_shape=jax.ShapeDtypeStruct(piece, jnp.bflo...  4.23 us
    dot_general x1, matrix products, dot(): return jnp.dot(left, right, preferred_element_type=jnp.float32)  3.25 us
    ppermute x1, starting transfers between devices, per_device(): lax.ppermute(total, 'dp', [(i, i ^ steps[i & 1]) for i in range(count)])  2.87 us
    pallas_call x2, Pallas kernels, place(): pl.pallas_call(place_kernel if before is None else place_kernel_on, out_s...  2.05 us
    ppermute x2, waiting for transfers between devices, swap(): return lax.ppermute(array, 'dp', [(i, i ^ step) for i in range(count)])  1.63 us
  transfers between devices with their start and end apart: 3, of which 2 were waited for; matrix products, arithmetic and copies ran while one was open for 5% of the time, Pallas kernels for 8%

profile of v4, /device:TPU:0, one launch (start us, length us, event | category | flops | bytes accessed | tf_op | source)
XLA Modules:
  0.0 65.7 jit_solution(8315432531412854467)
XLA Ops:
  0.6 9.0 %shard_map.68 = (bf16[8,64,1024]{2,1,0:T(8,128)(2,1)S(1)}, bf16[256,128]{1,0:T(8,128)(2,1)S(1)}) custom-call(s32[1]{0:T(128)} %bitcast.core_ref, bf16[256,8192]{1,0:T(8,128)(2,1)} %hidden_hbm.3, bf16[128,8192]{1,0:T(8,128)(2,1)} %weight_hbm.1, bf16[64,256]{1,0:T(8,128)(2,1)} %bitcast.5, bf16[64,256]{1,0:T(8,128)(2,1)} %bitcast.6, bf16[256,128]{1,0:T(8,128)(2,1)} %grad_out_hbm.1), custom_call_target="tpu_custom_call" | custom-call | flops 805306368 | bytes 6291456 | tf_op jit(solution)/shard_map/pallas_call | solution.py:110
  9.6 0.5 collective-permute-start
  10.1 4.2 %shard_map.69 = bf16[8,64,1024]{2,1,0:T(8,128)(2,1)S(1)} custom-call(s32[1]{0:T(128)} %bitcast.core_ref, bf16[256,128]{1,0:T(8,128)(2,1)S(1)} %get-tuple-element.11.grad_query_hbm, bf16[256,8192]{1,0:T(8,128)(2,1)} %hidden_hbm.3), custom_call_target="tpu_custom_call" | custom-call | flops 268435456 | bytes 4194304 | tf_op jit(solution)/shard_map/pallas_call | solution.py:167
  14.3 0.0 collective-permute-done
  14.4 0.4 add_convert_fusion
  14.8 0.0 copy-start
  14.8 21.4 %all_to_all.10 = bf16[8,64,1024]{2,1,0:T(8,128)(2,1)S(1)} all-to-all(bf16[8,64,1024]{2,1,0:T(8,128)(2,1)S(1)} %add_convert_fusion), channel_id=1, replica_groups={{0,14,2,12,4,10,6,8},{16,30,18,28,20,26,22,24},{1,23,3,21,5,19,7,17},{9..., dimensions={0} | all-to-all | bytes 2097152 | tf_op jit(solution)/shard_map/all_to_all | solution.py:256
  36.2 0.2 reduce_sum.12
  36.4 2.9 %collective-permute-start.1 = (bf16[64,1024]{1,0:T(8,128)(2,1)S(1)}, bf16[64,1024]{1,0:T(8,128)(2,1)S(1)}, u32[]{:S(2)}, u32[]{:S(2)}) collective-permute-start(bf16[64,1024]{1,0:T(8,128)(2,1)S(1)} %reduce_sum.12), channel_id=1, source_target_pairs={{0,16},{1,9},{2,18},{3,11},{4,20},{5,13},{6,22},{7,15},{8,24},{9,1... | collective-permute-start | bytes 393224 | tf_op jit(solution)/shard_map/ppermute | solution.py:264
  39.3 0.0 copy-done
  39.3 3.3 %convolution_convert_fusion = bf16[256,8192]{1,0:T(8,128)(2,1)} fusion(bf16[256,128]{1,0:T(8,128)(2,1)S(1)} %get-tuple-element.11.grad_query_hbm, bf16[128,8192]{1,0:T(8,128)(2,1)S(1)} %copy-done), kind=kOutput, calls=%fused_computation | convolution fusion | flops 538968064 | bytes 6356992 | tf_op jit(solution)/shard_map/dot_general | solution.py:16
  42.5 0.3 collective-permute-done.1
  42.8 0.1 broadcast_in_dim.2
  43.0 19.0 %all_to_all.11.piece_hbm = bf16[8,64,1024]{2,1,0:T(8,128)(2,1)S(1)} all-to-all(bf16[8,64,1024]{2,1,0:T(8,128)(2,1)S(1)} %broadcast_in_dim.2), channel_id=1, replica_groups={{0,14,2,12,4,10,6,8},{16,30,18,28,20,26,22,24},{1,23,3,21,5,19,7,17},{9..., dimensions={0} | all-to-all | bytes 2097152 | tf_op jit(solution)/shard_map/all_to_all | solution.py:269
  62.0 0.0 collective-permute-start.2
  62.0 1.0 %shard_map.70.before_hbm = bf16[128,8192]{1,0:T(8,128)(2,1)} custom-call(s32[1]{0:T(128)} %bitcast.core_ref, bf16[8,64,1024]{2,1,0:T(8,128)(2,1)S(1)} %all_to_all.11.piece_hbm), custom_call_target="tpu_custom_call" | custom-call | bytes 2097152 | tf_op jit(solution)/shard_map/pallas_call | solution.py:206
  63.0 1.6 %collective-permute-done.2.piece_hbm = bf16[8,64,1024]{2,1,0:T(8,128)(2,1)S(1)} collective-permute-done((bf16[8,64,1024]{2,1,0:T(8,128)(2,1)S(1)}, bf16[8,64,1024]{2,1,0:T(8,128)(2,1)S(1)}, u32[]{:S(2)}, u32[]{:S(2)}) %collective-permute-start.2) | collective-permute-done | bytes 1048608 | tf_op jit(solution)/shard_map/ppermute | solution.py:219
  64.7 1.0 %shard_map.71 = bf16[128,8192]{1,0:T(8,128)(2,1)} custom-call(s32[1]{0:T(128)S(6)} %sub.3.core_ref, bf16[8,64,1024]{2,1,0:T(8,128)(2,1)S(1)} %collective-permute-done.2.piece_hbm, bf16[128,8192]{1,0:T(8,128)(2,1)} %shard_map.70.before_hbm), custom_call_target="tpu_custom_call", output_to_operand_aliasing={{}: (2, {})} | custom-call | bytes 2097152 | tf_op jit(solution)/shard_map/pallas_call | solution.py:206
  (1 shorter events, 0.0 us)
Async XLA Ops:
  9.6 4.8 %collective-permute-start = (bf16[8,64,1024]{2,1,0:T(8,128)(2,1)S(1)}, bf16[8,64,1024]{2,1,0:T(8,128)(2,1)S(1)}, u32[]{:S(2)}, u32[]{:S(2)}) collective-permute-start(bf16[8,64,1024]{2,1,0:T(8,128)(2,1)S(1)} %get-tuple-element.9), channel_id=1, source_target_pairs={{0,1},{1,0},{2,3},{3,2},{4,5},{5,4},{6,7},{7,6},{8,9},{9,8},{10,11... | collective-permute-start | bytes 3145736 | tf_op jit(solution)/shard_map/ppermute | solution.py:219
  14.8 24.5 %copy-start = (bf16[128,8192]{1,0:T(8,128)(2,1)S(1)}, bf16[128,8192]{1,0:T(8,128)(2,1)}, u32[]{:S(2)}) copy-start(bf16[128,8192]{1,0:T(8,128)(2,1)} %weight_hbm.1) | copy-start | bytes 6291460
  36.4 6.4 %collective-permute-start.1 = (bf16[64,1024]{1,0:T(8,128)(2,1)S(1)}, bf16[64,1024]{1,0:T(8,128)(2,1)S(1)}, u32[]{:S(2)}, u32[]{:S(2)}) collective-permute-start(bf16[64,1024]{1,0:T(8,128)(2,1)S(1)} %reduce_sum.12), channel_id=1, source_target_pairs={{0,16},{1,9},{2,18},{3,11},{4,20},{5,13},{6,22},{7,15},{8,24},{9,1... | collective-permute-start | bytes 393224 | tf_op jit(solution)/shard_map/ppermute | solution.py:264
  62.0 2.7 %collective-permute-start.2 = (bf16[8,64,1024]{2,1,0:T(8,128)(2,1)S(1)}, bf16[8,64,1024]{2,1,0:T(8,128)(2,1)S(1)}, u32[]{:S(2)}, u32[]{:S(2)}) collective-permute-start(bf16[8,64,1024]{2,1,0:T(8,128)(2,1)S(1)} %all_to_all.11.piece_hbm), channel_id=1, source_target_pairs={{0,1},{1,0},{2,3},{3,2},{4,5},{5,4},{6,7},{7,6},{8,9},{9,8},{10,11... | collective-permute-start | bytes 3145736 | tf_op jit(solution)/shard_map/ppermute | solution.py:219

commit v5 on v3

v5 whole, which is shorter than its diff:
```python
import functools

import jax
import jax.numpy as jnp
from jax import lax
from jax.experimental import pallas as pl
from jax.experimental.pallas import tpu as pltpu
from jax.sharding import PartitionSpec as P

LOADS = 8
VMEM_LIMIT = 40 * 1024 * 1024
ANY = pl.BlockSpec(memory_space=pl.ANY)
WHOLE = pl.BlockSpec(memory_space=pltpu.VMEM)
SCALAR = pl.BlockSpec(memory_space=pltpu.SMEM)


def dot(left, right):
    return jnp.dot(left, right, preferred_element_type=jnp.float32)


def dot_tt(left, right):
    return lax.dot_general(left, right, (((1,), (1,)), ((), ())), preferred_element_type=jnp.float32)


def head_grad(query, keys, values, grad_out):
    head_size, length = keys.shape
    score_scale = head_size ** (-0.5)
    causal_mask = lax.broadcasted_iota(jnp.int32, (length, length), 1) <= lax.broadcasted_iota(
        jnp.int32, (length, length), 0
    )
    scores = jnp.where(causal_mask, dot(query, keys) * score_scale, -1e30)
    raised = jnp.exp(scores - jnp.max(scores, axis=1, keepdims=True))
    attn_weights = raised * (1.0 / jnp.sum(raised, axis=1, keepdims=True))
    grad_prob = dot(grad_out, values)
    row_delta = jnp.sum(attn_weights * grad_prob, axis=1, keepdims=True)
    grad_score = (attn_weights * (grad_prob - row_delta) * score_scale).astype(jnp.bfloat16)
    return dot_tt(grad_score, keys).astype(jnp.bfloat16)


def heads_grad(query, keys, values, grad_out):
    size = keys.shape[0]
    heads = [slice(low, low + size) for low in range(0, query.shape[1], size)]
    grads = [head_grad(query[:, head], keys, values, grad_out[:, head]) for head in heads]
    return grads[0] if len(grads) == 1 else jnp.concatenate(grads, axis=1)


def half_of(array, second):
    half = array.shape[1] // 2
    return jnp.where(second, array[:, half:], array[:, :half])


def add_rows(grads, hidden, out):
    turned = grads.T
    step = out.shape[2]
    for block in range(out.shape[0]):
        out[block] = dot(turned, hidden[:, pl.ds(block * step, step)]).astype(out.dtype)


def query_kernel(
    core_ref, hidden_hbm, weight_hbm, keys_hbm, values_hbm, grad_out_hbm,
    other, hidden, query, grads,
    weight, keys, values, grad_out, hidden_sem, weight_sem, small_sem,
):
    tokens, width = hidden.shape
    blocks = hidden_sem.shape[0]
    step = width // blocks
    copies = []
    for block in range(blocks):
        columns = pl.ds(block * step, step)
        pair = [
            pltpu.make_async_copy(weight_hbm.at[:, columns], weight.at[:, columns], weight_sem.at[block]),
            pltpu.make_async_copy(hidden_hbm.at[:, columns], hidden.at[:, columns], hidden_sem.at[block]),
        ]
        for copy in pair:
            copy.start()
        copies.append(pair)
    pairs = ((keys_hbm, keys), (values_hbm, values), (grad_out_hbm, grad_out))
    small = [pltpu.make_async_copy(*pair, small_sem.at[at]) for at, pair in enumerate(pairs)]
    for copy in small:
        copy.start()
    total = jnp.zeros((tokens, weight.shape[0]), jnp.float32)
    for block in range(blocks):
        for copy in copies[block]:
            copy.wait()
        columns = pl.ds(block * step, step)
        total += dot_tt(hidden[:, columns], weight[:, columns])
    rounded = total.astype(jnp.bfloat16)
    query[...] = rounded
    for copy in small:
        copy.wait()
    second = core_ref[0] == 0
    found = heads_grad(half_of(rounded, second), keys[...], values[...], half_of(grad_out[...], second))
    grads[...] = found
    add_rows(found, hidden, other)


def query_and_other(blocks, core, hidden_in, query_weight, keys, values, grad_out):
    tokens, width = hidden_in.shape
    rows = query_weight.shape[0]
    like = lambda array: pltpu.VMEM(array.shape, array.dtype)
    operands = (hidden_in, query_weight, keys, values, grad_out)
    return pl.pallas_call(
        query_kernel,
        out_shape=(
            jax.ShapeDtypeStruct((blocks, rows // 2, width // blocks), jnp.bfloat16),
            jax.ShapeDtypeStruct((tokens, width), jnp.bfloat16),
            jax.ShapeDtypeStruct((tokens, rows), jnp.bfloat16),
            jax.ShapeDtypeStruct((tokens, rows // 2), jnp.bfloat16),
        ),
        in_specs=[SCALAR] + [ANY] * 5,
        out_specs=(WHOLE,) * 4,
        scratch_shapes=[
            like(query_weight),
            like(keys),
            like(values),
            like(grad_out),
            pltpu.SemaphoreType.DMA((LOADS,)),
            pltpu.SemaphoreType.DMA((LOADS,)),
            pltpu.SemaphoreType.DMA((3,)),
        ],
        compiler_params=pltpu.CompilerParams(vmem_limit_bytes=VMEM_LIMIT),
        cost_estimate=pl.CostEstimate(
            flops=3 * tokens * width * rows,
            bytes_accessed=2 * (tokens * width + rows * width),
            transcendentals=tokens * tokens,
        ),
    )(core, *(pltpu.with_memory_space_constraint(operand, pltpu.HBM) for operand in operands))


def own_kernel(core_ref, hidden, query, others, keys, values, grad_out, own, grad_query):
    second = core_ref[0] == 1
    grads = heads_grad(half_of(query[...], second), keys[...], values[...], half_of(grad_out[...], second))
    add_rows(grads, hidden, own)
    before = others[...]
    grad_query[...] = jnp.concatenate(
        [jnp.where(second, before, grads), jnp.where(second, grads, before)], axis=1
    )


def own_part(blocks, core, hidden, query, others, keys, values, grad_out):
    tokens, width = hidden.shape
    rows = query.shape[1]
    return pl.pallas_call(
        own_kernel,
        out_shape=(
            jax.ShapeDtypeStruct((blocks, rows // 2, width // blocks), jnp.bfloat16),
            jax.ShapeDtypeStruct((tokens, rows), jnp.bfloat16),
        ),
        in_specs=[SCALAR] + [WHOLE] * 6,
        out_specs=(WHOLE,) * 2,
        compiler_params=pltpu.CompilerParams(vmem_limit_bytes=24 * 1024 * 1024),
        cost_estimate=pl.CostEstimate(
            flops=tokens * width * rows, bytes_accessed=2 * tokens * width, transcendentals=tokens * tokens
        ),
    )(core, hidden, query, others, keys, values, grad_out)


def place_kernel(core_ref, piece_hbm, out_hbm, sem):
    blocks, half, step = piece_hbm.shape
    rows = pl.ds(pl.multiple_of(core_ref[0] * half, half), half)
    copies = [
        pltpu.make_async_copy(piece_hbm.at[block], out_hbm.at[rows, pl.ds(block * step, step)], sem.at[block])
        for block in range(blocks)
    ]
    for copy in copies:
        copy.start()
    for copy in copies:
        copy.wait()


def place_kernel_on(core_ref, piece_hbm, before_hbm, out_hbm, sem):
    place_kernel(core_ref, piece_hbm, out_hbm, sem)


def place(core, piece, before=None):
    blocks, half, step = piece.shape
    return pl.pallas_call(
        place_kernel if before is None else place_kernel_on,
        out_shape=jax.ShapeDtypeStruct((2 * half, blocks * step), jnp.bfloat16),
        in_specs=[SCALAR, ANY] + [ANY] * (before is not None),
        out_specs=ANY,
        scratch_shapes=[pltpu.SemaphoreType.DMA((blocks,))],
        input_output_aliases={} if before is None else {2: 0},
        compiler_params=pltpu.CompilerParams(vmem_limit_bytes=VMEM_LIMIT),
        cost_estimate=pl.CostEstimate(flops=0, bytes_accessed=4 * half * blocks * step, transcendentals=0),
    )(core, piece, *(() if before is None else (before,)))


def swap(array, step, count):
    return lax.ppermute(array, "dp", [(i, i ^ step) for i in range(count)])


def add(left, right):
    return (left.astype(jnp.float32) + right.astype(jnp.float32)).astype(jnp.bfloat16)


def per_device(count, hidden_in, query_weight, saved_keys, saved_values, grad_out):
    bits = count.bit_length() - 1
    wide = min(3, bits - 1)
    blocks = 1 << wide
    groups = [
        [high << (wide + 1) | (place ^ (high & 1) * (blocks >> 1)) << 1 | core for place in range(blocks)]
        for high in range(count >> (wide + 1))
        for core in range(2)
    ]
    if hidden_in.shape[1] != query_weight.shape[1]:
        hidden_in = lax.all_gather(hidden_in, "tensor", axis=1, tiled=True)
    core = (lax.axis_index("dp") & 1).astype(jnp.int32).reshape(1)
    keys, values = saved_keys.T, saved_values.T
    other, hidden, query, grads = query_and_other(
        blocks, core, hidden_in, query_weight, keys, values, grad_out
    )
    arriving = swap(other, 1, count)
    own, grad_query = own_part(blocks, core, hidden, query, grads, keys, values, grad_out)
    chip = add(own, arriving)
    parts = lax.all_to_all(chip, "dp", 0, 0, axis_index_groups=groups)
    total = jnp.sum(parts.astype(jnp.float32), axis=0).astype(jnp.bfloat16)
    grad_query, total = lax.optimization_barrier((grad_query, total))
    input_terms = dot(grad_query, query_weight)
    grad_hidden = lax.psum_scatter(
        input_terms.astype(jnp.bfloat16), "tensor", scatter_dimension=1, tiled=True
    )
    for bit in range(wide + 1, bits):
        arriving = swap(total, 3 << wide if bit == wide + 1 else 1 << bit, count)
        if bit == wide + 1:
            arriving, grad_hidden = lax.optimization_barrier((arriving, grad_hidden))
        total = add(total, arriving)
    copies = jnp.broadcast_to(total[None], (blocks, *total.shape))
    gathered = lax.all_to_all(copies, "dp", 0, 0, axis_index_groups=groups)
    arriving = swap(gathered, 1, count)
    grad_query_weight = place(1 - core, arriving, place(core, gathered))
    return (grad_query_weight, grad_hidden)


def solution(mesh):
    count = mesh.shape["dp"]
    placed = (
        P("dp", "tensor"),
        P("tensor", None),
        P("dp", "tensor"),
        P("dp", "tensor"),
        P("dp", "tensor"),
    )
    return jax.shard_map(
        functools.partial(per_device, count),
        mesh=mesh,
        in_specs=placed,
        out_specs=(P("tensor", None), P("dp", "tensor")),
        check_vma=False,
    )
```

time: 65.7 us -> 61 us (0.928)
  Pallas kernels: 15.2 us -> 9.9 us
    pallas_call x2, Pallas kernels: 13.2 us -> 7.85 us  [the longest x1 6.13 us: query_and_other(): pl.pallas_call(query_kernel, out_shape=(jax.ShapeDtypeStruct((blocks, row...]
  transfers between devices with their start and end apart: 3 -> 3, of which waited for: 2 -> 3; matrix products, arithmetic and copies ran while one was open for 5% -> 5% of each run, Pallas kernels for 8% -> 5%
where the time goes in v5:
time: 61 us; the launch traced here: 60.8 us
  blocking collectives  39.8 us (65%)
  Pallas kernels  9.9 us (16%)
  matrix products  3.25 us (5%)
  waiting for transfers between devices  3.2 us (5%)
  starting transfers between devices  3.17 us (5%)
  between operations  0.72 us (1%)
  other arithmetic  0.62 us (1%)
    all_to_all x1, blocking collectives, per_device(): parts = lax.all_to_all(chip, 'dp', 0, 0, axis_index_groups=groups)  21.4 us
    all_to_all x1, blocking collectives, per_device(): gathered = lax.all_to_all(copies, 'dp', 0, 0, axis_index_groups=groups)  18.5 us
    pallas_call x1, Pallas kernels, query_and_other(): pl.pallas_call(query_kernel, out_shape=(jax.ShapeDtypeStruct((blocks, row...  6.13 us
    dot_general x1, matrix products, dot(): return jnp.dot(left, right, preferred_element_type=jnp.float32)  3.25 us
    ppermute x3, waiting for transfers between devices, swap(): return lax.ppermute(array, 'dp', [(i, i ^ step) for i in range(count)])  3.2 us
    ppermute x3, starting transfers between devices, swap(): return lax.ppermute(array, 'dp', [(i, i ^ step) for i in range(count)])  3.17 us
    pallas_call x2, Pallas kernels, place(): pl.pallas_call(place_kernel if before is None else place_kernel_on, out_s...  2.05 us
    pallas_call x1, Pallas kernels, own_part(): pl.pallas_call(own_kernel, out_shape=(jax.ShapeDtypeStruct((blocks, rows...  1.72 us
  transfers between devices with their start and end apart: 3, of which 3 were waited for; matrix products, arithmetic and copies ran while one was open for 5% of the time, Pallas kernels for 5%

profile of v5, /device:TPU:0, one launch (start us, length us, event | category | flops | bytes accessed | tf_op | source)
XLA Modules:
  0.0 60.8 jit_solution(16446772724414899934)
XLA Ops:
  0.6 0.0 copy-start
  0.6 0.0 copy-start.1
  0.7 0.0 copy-start.2
  0.7 6.1 %shard_map.68 = (bf16[8,64,1024]{2,1,0:T(8,128)(2,1)S(1)}, bf16[256,8192]{1,0:T(8,128)(2,1)S(1)}, bf16[256,128]{1,0:T(8,128)(2,1)S(1)}, bf16[256,64]{1,0:T(8,128)(2,1)S(1)}) custom-call(s32[1]{0:T(128)} %bitcast.core_ref, bf16[256,8192]{1,0:T(8,128)(2,1)} %hidden_hbm.1, bf16[128,8192]{1,0:T(8,128)(2,1)} %weight_hbm.1, bf16[64,256]{1,0:T(8,128)(2,1)} %bitcast.5, ...), custom_call_target="tpu_custom_call" | custom-call | flops 805306368 | bytes 6291456 | tf_op jit(solution)/shard_map/pallas_call | solution.py:102
  6.8 0.5 collective-permute-start
  7.3 0.0 copy-done
  7.3 0.0 copy-done.1
  7.3 0.0 copy-done.2
  7.3 1.7 %shard_map.69 = (bf16[8,64,1024]{2,1,0:T(8,128)(2,1)S(1)}, bf16[256,128]{1,0:T(8,128)(2,1)S(1)}) custom-call(s32[1]{0:T(128)} %bitcast.core_ref, bf16[256,8192]{1,0:T(8,128)(2,1)S(1)} %get-tuple-element.12.hidden, bf16[256,128]{1,0:T(8,128)(2,1)S(1)} %get-tuple-element.13.query, bf16[256,64]{1,0:T(8,128)(2,1)S(1)} %get-tuple-element.14.others, ...), custom_call_target="tpu_custom_call" | custom-call | flops 268435456 | bytes 4194304 | tf_op jit(solution)/shard_map/pallas_call | solution.py:143
  9.1 0.6 collective-permute-done
  9.6 0.4 add_convert_fusion
  10.0 0.0 copy-start.3
  10.0 21.4 %all_to_all.10 = bf16[8,64,1024]{2,1,0:T(8,128)(2,1)S(1)} all-to-all(bf16[8,64,1024]{2,1,0:T(8,128)(2,1)S(1)} %add_convert_fusion), channel_id=1, replica_groups={{0,2,4,6,8,10,12,14},{1,3,5,7,9,11,13,15},{24,26,28,30,16,18,20,22},{25..., dimensions={0} | all-to-all | bytes 2097152 | tf_op jit(solution)/shard_map/all_to_all | solution.py:216
  31.4 0.2 reduce_sum.12
  31.6 2.7 %collective-permute-start.1 = (bf16[64,1024]{1,0:T(8,128)(2,1)S(1)}, bf16[64,1024]{1,0:T(8,128)(2,1)S(1)}, u32[]{:S(2)}, u32[]{:S(2)}) collective-permute-start(bf16[64,1024]{1,0:T(8,128)(2,1)S(1)} %reduce_sum.12), channel_id=1, source_target_pairs={{0,24},{1,25},{2,26},{3,27},{4,28},{5,29},{6,30},{7,31},{8,16},{9,... | collective-permute-start | bytes 393224 | tf_op jit(solution)/shard_map/ppermute | solution.py:190
  34.2 0.0 copy-done.3
  34.3 3.3 %convolution_convert_fusion = bf16[256,8192]{1,0:T(8,128)(2,1)} fusion(bf16[256,128]{1,0:T(8,128)(2,1)S(1)} %get-tuple-element.19, bf16[128,8192]{1,0:T(8,128)(2,1)S(1)} %copy-done.3), kind=kOutput, calls=%fused_computation | convolution fusion | flops 538968064 | bytes 6356992 | tf_op jit(solution)/shard_map/dot_general | solution.py:18
  37.5 1.0 %collective-permute-done.1 = bf16[64,1024]{1,0:T(8,128)(2,1)S(1)} collective-permute-done((bf16[64,1024]{1,0:T(8,128)(2,1)S(1)}, bf16[64,1024]{1,0:T(8,128)(2,1)S(1)}, u32[]{:S(2)}, u32[]{:S(2)}) %collective-permute-start.1) | collective-permute-done | bytes 131104 | tf_op jit(solution)/shard_map/ppermute | solution.py:190
  38.6 0.1 broadcast_in_dim.2
  38.7 18.5 %all_to_all.11.piece_hbm = bf16[8,64,1024]{2,1,0:T(8,128)(2,1)S(1)} all-to-all(bf16[8,64,1024]{2,1,0:T(8,128)(2,1)S(1)} %broadcast_in_dim.2), channel_id=1, replica_groups={{0,2,4,6,8,10,12,14},{1,3,5,7,9,11,13,15},{24,26,28,30,16,18,20,22},{25..., dimensions={0} | all-to-all | bytes 2097152 | tf_op jit(solution)/shard_map/all_to_all | solution.py:229
  57.2 0.0 collective-permute-start.2
  57.2 1.0 %shard_map.70.before_hbm = bf16[128,8192]{1,0:T(8,128)(2,1)} custom-call(s32[1]{0:T(128)} %bitcast.core_ref, bf16[8,64,1024]{2,1,0:T(8,128)(2,1)S(1)} %all_to_all.11.piece_hbm), custom_call_target="tpu_custom_call" | custom-call | bytes 2097152 | tf_op jit(solution)/shard_map/pallas_call | solution.py:177
  58.2 1.6 %collective-permute-done.2.piece_hbm = bf16[8,64,1024]{2,1,0:T(8,128)(2,1)S(1)} collective-permute-done((bf16[8,64,1024]{2,1,0:T(8,128)(2,1)S(1)}, bf16[8,64,1024]{2,1,0:T(8,128)(2,1)S(1)}, u32[]{:S(2)}, u32[]{:S(2)}) %collective-permute-start.2) | collective-permute-done | bytes 1048608 | tf_op jit(solution)/shard_map/ppermute | solution.py:190
  59.8 1.0 %shard_map.71 = bf16[128,8192]{1,0:T(8,128)(2,1)} custom-call(s32[1]{0:T(128)S(6)} %sub.3.core_ref, bf16[8,64,1024]{2,1,0:T(8,128)(2,1)S(1)} %collective-permute-done.2.piece_hbm, bf16[128,8192]{1,0:T(8,128)(2,1)} %shard_map.70.before_hbm), custom_call_target="tpu_custom_call", output_to_operand_aliasing={{}: (2, {})} | custom-call | bytes 2097152 | tf_op jit(solution)/shard_map/pallas_call | solution.py:177
  (1 shorter events, 0.0 us)
Async XLA Ops:
  0.6 6.7 %copy-start = (bf16[256,128]{1,0:T(8,128)(2,1)S(1)}, bf16[256,128]{1,0:T(8,128)(2,1)}, u32[]{:S(2)}) copy-start(bf16[256,128]{1,0:T(8,128)(2,1)} %grad_out.1) | copy-start | bytes 196612
  0.6 6.7 %copy-start.1 = (bf16[256,64]{0,1:T(8,128)(2,1)S(1)}, bf16[256,64]{0,1:T(8,128)(2,1)}, u32[]{:S(2)}) copy-start(bf16[256,64]{0,1:T(8,128)(2,1)} %param.7) | copy-start | bytes 98308
  0.7 6.7 %copy-start.2 = (bf16[256,64]{0,1:T(8,128)(2,1)S(1)}, bf16[256,64]{0,1:T(8,128)(2,1)}, u32[]{:S(2)}) copy-start(bf16[256,64]{0,1:T(8,128)(2,1)} %param.8) | copy-start | bytes 98308
  6.8 2.8 %collective-permute-start = (bf16[8,64,1024]{2,1,0:T(8,128)(2,1)S(1)}, bf16[8,64,1024]{2,1,0:T(8,128)(2,1)S(1)}, u32[]{:S(2)}, u32[]{:S(2)}) collective-permute-start(bf16[8,64,1024]{2,1,0:T(8,128)(2,1)S(1)} %get-tuple-element.17), channel_id=1, source_target_pairs={{0,1},{1,0},{2,3},{3,2},{4,5},{5,4},{6,7},{7,6},{8,9},{9,8},{10,11... | collective-permute-start | bytes 3145736 | tf_op jit(solution)/shard_map/ppermute | solution.py:190
  10.0 24.2 %copy-start.3 = (bf16[128,8192]{1,0:T(8,128)(2,1)S(1)}, bf16[128,8192]{1,0:T(8,128)(2,1)}, u32[]{:S(2)}) copy-start(bf16[128,8192]{1,0:T(8,128)(2,1)} %weight_hbm.1) | copy-start | bytes 6291460
  31.6 6.9 %collective-permute-start.1 = (bf16[64,1024]{1,0:T(8,128)(2,1)S(1)}, bf16[64,1024]{1,0:T(8,128)(2,1)S(1)}, u32[]{:S(2)}, u32[]{:S(2)}) collective-permute-start(bf16[64,1024]{1,0:T(8,128)(2,1)S(1)} %reduce_sum.12), channel_id=1, source_target_pairs={{0,24},{1,25},{2,26},{3,27},{4,28},{5,29},{6,30},{7,31},{8,16},{9,... | collective-permute-start | bytes 393224 | tf_op jit(solution)/shard_map/ppermute | solution.py:190
  57.2 2.7 %collective-permute-start.2 = (bf16[8,64,1024]{2,1,0:T(8,128)(2,1)S(1)}, bf16[8,64,1024]{2,1,0:T(8,128)(2,1)S(1)}, u32[]{:S(2)}, u32[]{:S(2)}) collective-permute-start(bf16[8,64,1024]{2,1,0:T(8,128)(2,1)S(1)} %all_to_all.11.piece_hbm), channel_id=1, source_target_pairs={{0,1},{1,0},{2,3},{3,2},{4,5},{5,4},{6,7},{7,6},{8,9},{9,8},{10,11... | collective-permute-start | bytes 3145736 | tf_op jit(solution)/shard_map/ppermute | solution.py:190

commit v6 on v5

--- a/solution.py
+++ b/solution.py
@@ -155,6 +155,54 @@
     )(core, hidden, query, others, keys, values, grad_out)
 
 
+def hidden_kernel(core_ref, turn_ref, grad_query, weight_hbm, *refs):
+    out_hbm, weight, found, weight_sem, out_sem = refs[-5:]
+
+    @pl.when(core_ref[0] == turn_ref[0])
+    def _():
+        blocks, _, step = found.shape
+        copies = []
+        for block in range(blocks):
+            columns = pl.ds(block * step, step)
+            copies.append(
+                pltpu.make_async_copy(weight_hbm.at[:, columns], weight.at[:, columns], weight_sem.at[block])
+            )
+            copies[-1].start()
+        grads = grad_query[...]
+        sent = []
+        for block in range(blocks):
+            columns = pl.ds(block * step, step)
+            copies[block].wait()
+            found[block] = dot(grads, weight[:, columns]).astype(found.dtype)
+            sent.append(pltpu.make_async_copy(found.at[block], out_hbm.at[:, columns], out_sem.at[block]))
+            sent[-1].start()
+        for copy in sent:
+            copy.wait()
+
+
+def hidden_part(core, turn, grad_query, query_weight, before=None):
+    tokens, rows = grad_query.shape
+    width = query_weight.shape[1]
+    given = () if before is None else (before,)
+    return pl.pallas_call(
+        hidden_kernel,
+        out_shape=jax.ShapeDtypeStruct((tokens, width), jnp.bfloat16),
+        in_specs=[SCALAR, SCALAR, WHOLE, ANY] + [ANY] * len(given),
+        out_specs=ANY,
+        scratch_shapes=[
+            pltpu.VMEM((rows, width), jnp.bfloat16),
+            pltpu.VMEM((LOADS, tokens, width // LOADS), jnp.bfloat16),
+            pltpu.SemaphoreType.DMA((LOADS,)),
+            pltpu.SemaphoreType.DMA((LOADS,)),
+        ],
+        input_output_aliases={4: 0} if given else {},
+        compiler_params=pltpu.CompilerParams(vmem_limit_bytes=24 * 1024 * 1024),
+        cost_estimate=pl.CostEstimate(
+            flops=2 * tokens * width * rows, bytes_accessed=2 * width * (tokens + rows), transcendentals=0
+        ),
+    )(core, jnp.full((1,), turn, jnp.int32), grad_query, pltpu.with_memory_space_constraint(query_weight, pltpu.HBM), *given)
+
+
 def place_kernel(core_ref, piece_hbm, out_hbm, sem):
     blocks, half, step = piece_hbm.shape
     rows = pl.ds(pl.multiple_of(core_ref[0] * half, half), half)
@@ -203,7 +251,8 @@
         for high in range(count >> (wide + 1))
         for core in range(2)
     ]
-    if hidden_in.shape[1] != query_weight.shape[1]:
+    given_width = hidden_in.shape[1]
+    if given_width != query_weight.shape[1]:
         hidden_in = lax.all_gather(hidden_in, "tensor", axis=1, tiled=True)
     core = (lax.axis_index("dp") & 1).astype(jnp.int32).reshape(1)
     keys, values = saved_keys.T, saved_values.T
@@ -213,22 +262,25 @@
     arriving = swap(other, 1, count)
     own, grad_query = own_part(blocks, core, hidden, query, grads, keys, values, grad_out)
     chip = add(own, arriving)
+    input_terms = hidden_part(core, 0, grad_query, query_weight)
+    chip, input_terms = lax.optimization_barrier((chip, input_terms))
     parts = lax.all_to_all(chip, "dp", 0, 0, axis_index_groups=groups)
     total = jnp.sum(parts.astype(jnp.float32), axis=0).astype(jnp.bfloat16)
-    grad_query, total = lax.optimization_barrier((grad_query, total))
-    input_terms = dot(grad_query, query_weight)
-    grad_hidden = lax.psum_scatter(
-        input_terms.astype(jnp.bfloat16), "tensor", scatter_dimension=1, tiled=True
-    )
+    input_terms, total = lax.optimization_barrier((input_terms, total))
+    input_terms = hidden_part(core, 1, grad_query, query_weight, input_terms)
     for bit in range(wide + 1, bits):
         arriving = swap(total, 3 << wide if bit == wide + 1 else 1 << bit, count)
         if bit == wide + 1:
-            arriving, grad_hidden = lax.optimization_barrier((arriving, grad_hidden))
+            arriving, input_terms = lax.optimization_barrier((arriving, input_terms))
         total = add(total, arriving)
     copies = jnp.broadcast_to(total[None], (blocks, *total.shape))
     gathered = lax.all_to_all(copies, "dp", 0, 0, axis_index_groups=groups)
     arriving = swap(gathered, 1, count)
     grad_query_weight = place(1 - core, arriving, place(core, gathered))
+    if input_terms.shape[1] == given_width:
+        grad_hidden = input_terms
+    else:
+        grad_hidden = lax.psum_scatter(input_terms, "tensor", scatter_dimension=1, tiled=True)
     return (grad_query_weight, grad_hidden)
 
 

time: 61 us -> 55.6 us (0.911)
  blocking collectives: 39.8 us -> 30.9 us
  Pallas kernels: 9.9 us -> 14.2 us
  matrix products: 3.25 us -> 0 us
  waiting for transfers between devices: 3.2 us -> 5.65 us
    all_to_all x1, blocking collectives: 18.5 us -> 13.3 us  [per_device(): gathered = lax.all_to_all(copies, 'dp', 0, 0, axis_index_groups=groups)]
    pallas_call x0 -> x2, Pallas kernels: none -> 4.32 us  [hidden_part(): pl.pallas_call(hidden_kernel, out_shape=jax.ShapeDtypeStruct((tokens, wid...]
    all_to_all x1, blocking collectives: 21.4 us -> 17.6 us  [per_device(): parts = lax.all_to_all(chip, 'dp', 0, 0, axis_index_groups=groups)]
    dot_general x1 -> x0, matrix products: 3.25 us -> none  [dot(): return jnp.dot(left, right, preferred_element_type=jnp.float32)]
    ppermute x3, waiting for transfers between devices: 3.2 us -> 5.65 us  [swap(): return lax.ppermute(array, 'dp', [(i, i ^ step) for i in range(count)])]
  transfers between devices with their start and end apart: 3 -> 3, of which waited for: 3 -> 2; matrix products, arithmetic and copies ran while one was open for 5% -> 0% of each run, Pallas kernels for 5% -> 13%
where the time goes in v6:
time: 55.6 us; the launch traced here: 55.4 us
  blocking collectives  30.9 us (56%)
  Pallas kernels  14.2 us (26%)
  waiting for transfers between devices  5.65 us (10%)
  starting transfers between devices  3.17 us (6%)
  between operations  0.73 us (1%)
  other arithmetic  0.62 us (1%)
    all_to_all x1, blocking collectives, per_device(): parts = lax.all_to_all(chip, 'dp', 0, 0, axis_index_groups=groups)  17.6 us
    all_to_all x1, blocking collectives, per_device(): gathered = lax.all_to_all(copies, 'dp', 0, 0, axis_index_groups=groups)  13.3 us
    pallas_call x1, Pallas kernels, query_and_other(): pl.pallas_call(query_kernel, out_shape=(jax.ShapeDtypeStruct((blocks, row...  6.13 us
    ppermute x3, waiting for transfers between devices, swap(): return lax.ppermute(array, 'dp', [(i, i ^ step) for i in range(count)])  5.65 us
    pallas_call x2, Pallas kernels, hidden_part(): pl.pallas_call(hidden_kernel, out_shape=jax.ShapeDtypeStruct((tokens, wid...  4.32 us
    ppermute x3, starting transfers between devices, swap(): return lax.ppermute(array, 'dp', [(i, i ^ step) for i in range(count)])  3.17 us
    pallas_call x2, Pallas kernels, place(): pl.pallas_call(place_kernel if before is None else place_kernel_on, out_s...  2.05 us
    pallas_call x1, Pallas kernels, own_part(): pl.pallas_call(own_kernel, out_shape=(jax.ShapeDtypeStruct((blocks, rows...  1.72 us
  transfers between devices with their start and end apart: 3, of which 2 were waited for; matrix products, arithmetic and copies ran while one was open for 0% of the time, Pallas kernels for 13%

profile of v6, /device:TPU:0, one launch (start us, length us, event | category | flops | bytes accessed | tf_op | source)
XLA Modules:
  0.0 55.4 jit_solution(8083363864929102248)
XLA Ops:
  0.6 0.0 copy-start
  0.6 0.0 copy-start.1
  0.7 0.0 copy-start.2
  0.7 6.1 %shard_map.68 = (bf16[8,64,1024]{2,1,0:T(8,128)(2,1)S(1)}, bf16[256,8192]{1,0:T(8,128)(2,1)S(1)}, bf16[256,128]{1,0:T(8,128)(2,1)S(1)}, bf16[256,64]{1,0:T(8,128)(2,1)S(1)}) custom-call(s32[1]{0:T(128)} %bitcast.core_ref, bf16[256,8192]{1,0:T(8,128)(2,1)} %hidden_hbm.1, bf16[128,8192]{1,0:T(8,128)(2,1)} %weight_hbm.5, bf16[64,256]{1,0:T(8,128)(2,1)} %bitcast.3, ...), custom_call_target="tpu_custom_call" | custom-call | flops 805306368 | bytes 6291456 | tf_op jit(solution)/shard_map/pallas_call | solution.py:102
  6.8 0.5 collective-permute-start
  7.3 0.0 copy-done
  7.3 0.0 copy-done.1
  7.3 0.0 copy-done.2
  7.3 1.7 %shard_map.69 = (bf16[8,64,1024]{2,1,0:T(8,128)(2,1)S(1)}, bf16[256,128]{1,0:T(8,128)(2,1)S(1)}) custom-call(s32[1]{0:T(128)} %bitcast.core_ref, bf16[256,8192]{1,0:T(8,128)(2,1)S(1)} %get-tuple-element.14.hidden, bf16[256,128]{1,0:T(8,128)(2,1)S(1)} %get-tuple-element.15.query, bf16[256,64]{1,0:T(8,128)(2,1)S(1)} %get-tuple-element.16.others, ...), custom_call_target="tpu_custom_call" | custom-call | flops 268435456 | bytes 4194304 | tf_op jit(solution)/shard_map/pallas_call | solution.py:143
  9.1 4.2 %shard_map.70.refs_0_ = bf16[256,8192]{1,0:T(8,128)(2,1)} custom-call(s32[1]{0:T(128)} %bitcast.core_ref, s32[1]{0:T(128)} %constant.4.clone.1.turn_ref, bf16[256,128]{1,0:T(8,128)(2,1)S(1)} %get-tuple-element.19.grad_query, bf16[128,8192]{1,0:T(8,128)(2,1)} %weight_hbm.5), custom_call_target="tpu_custom_call" | custom-call | flops 536870912 | bytes 6291456 | tf_op jit(solution)/shard_map/pallas_call | solution.py:187
  13.2 0.0 collective-permute-done
  13.3 0.4 add_convert_fusion
  13.7 17.6 %all_to_all.10 = bf16[8,64,1024]{2,1,0:T(8,128)(2,1)S(1)} all-to-all(bf16[8,64,1024]{2,1,0:T(8,128)(2,1)S(1)} %add_convert_fusion), channel_id=1, replica_groups={{0,2,4,6,8,10,12,14},{1,3,5,7,9,11,13,15},{24,26,28,30,16,18,20,22},{25..., dimensions={0} | all-to-all | bytes 2097152 | tf_op jit(solution)/shard_map/all_to_all | solution.py:267
  31.3 0.2 reduce_sum.12
  31.4 2.7 %collective-permute-start.1 = (bf16[64,1024]{1,0:T(8,128)(2,1)S(1)}, bf16[64,1024]{1,0:T(8,128)(2,1)S(1)}, u32[]{:S(2)}, u32[]{:S(2)}) collective-permute-start(bf16[64,1024]{1,0:T(8,128)(2,1)S(1)} %reduce_sum.12), channel_id=1, source_target_pairs={{0,24},{1,25},{2,26},{3,27},{4,28},{5,29},{6,30},{7,31},{8,16},{9,... | collective-permute-start | bytes 393224 | tf_op jit(solution)/shard_map/ppermute | solution.py:238
  34.1 0.1 shard_map.71
  34.3 4.0 %collective-permute-done.1 = bf16[64,1024]{1,0:T(8,128)(2,1)S(1)} collective-permute-done((bf16[64,1024]{1,0:T(8,128)(2,1)S(1)}, bf16[64,1024]{1,0:T(8,128)(2,1)S(1)}, u32[]{:S(2)}, u32[]{:S(2)}) %collective-permute-start.1) | collective-permute-done | bytes 131104 | tf_op jit(solution)/shard_map/ppermute | solution.py:238
  38.3 0.1 broadcast_in_dim.2
  38.4 13.3 %all_to_all.11.piece_hbm = bf16[8,64,1024]{2,1,0:T(8,128)(2,1)S(1)} all-to-all(bf16[8,64,1024]{2,1,0:T(8,128)(2,1)S(1)} %broadcast_in_dim.2), channel_id=1, replica_groups={{0,2,4,6,8,10,12,14},{1,3,5,7,9,11,13,15},{24,26,28,30,16,18,20,22},{25..., dimensions={0} | all-to-all | bytes 2097152 | tf_op jit(solution)/shard_map/all_to_all | solution.py:277
  51.7 0.0 collective-permute-start.2
  51.7 1.0 %shard_map.72.before_hbm = bf16[128,8192]{1,0:T(8,128)(2,1)} custom-call(s32[1]{0:T(128)} %bitcast.core_ref, bf16[8,64,1024]{2,1,0:T(8,128)(2,1)S(1)} %all_to_all.11.piece_hbm), custom_call_target="tpu_custom_call" | custom-call | bytes 2097152 | tf_op jit(solution)/shard_map/pallas_call | solution.py:225
  52.7 1.6 %collective-permute-done.2.piece_hbm = bf16[8,64,1024]{2,1,0:T(8,128)(2,1)S(1)} collective-permute-done((bf16[8,64,1024]{2,1,0:T(8,128)(2,1)S(1)}, bf16[8,64,1024]{2,1,0:T(8,128)(2,1)S(1)}, u32[]{:S(2)}, u32[]{:S(2)}) %collective-permute-start.2) | collective-permute-done | bytes 1048608 | tf_op jit(solution)/shard_map/ppermute | solution.py:238
  54.4 1.0 %shard_map.73 = bf16[128,8192]{1,0:T(8,128)(2,1)} custom-call(s32[1]{0:T(128)S(6)} %sub.3.core_ref, bf16[8,64,1024]{2,1,0:T(8,128)(2,1)S(1)} %collective-permute-done.2.piece_hbm, bf16[128,8192]{1,0:T(8,128)(2,1)} %shard_map.72.before_hbm), custom_call_target="tpu_custom_call", output_to_operand_aliasing={{}: (2, {})} | custom-call | bytes 2097152 | tf_op jit(solution)/shard_map/pallas_call | solution.py:225
  (1 shorter events, 0.0 us)
Async XLA Ops:
  0.6 6.7 %copy-start = (bf16[256,128]{1,0:T(8,128)(2,1)S(1)}, bf16[256,128]{1,0:T(8,128)(2,1)}, u32[]{:S(2)}) copy-start(bf16[256,128]{1,0:T(8,128)(2,1)} %grad_out.1) | copy-start | bytes 196612
  0.6 6.7 %copy-start.1 = (bf16[256,64]{0,1:T(8,128)(2,1)S(1)}, bf16[256,64]{0,1:T(8,128)(2,1)}, u32[]{:S(2)}) copy-start(bf16[256,64]{0,1:T(8,128)(2,1)} %param.7) | copy-start | bytes 98308
  0.7 6.7 %copy-start.2 = (bf16[256,64]{0,1:T(8,128)(2,1)S(1)}, bf16[256,64]{0,1:T(8,128)(2,1)}, u32[]{:S(2)}) copy-start(bf16[256,64]{0,1:T(8,128)(2,1)} %param.8) | copy-start | bytes 98308
  6.8 6.4 %collective-permute-start = (bf16[8,64,1024]{2,1,0:T(8,128)(2,1)S(1)}, bf16[8,64,1024]{2,1,0:T(8,128)(2,1)S(1)}, u32[]{:S(2)}, u32[]{:S(2)}) collective-permute-start(bf16[8,64,1024]{2,1,0:T(8,128)(2,1)S(1)} %get-tuple-element.18), channel_id=1, source_target_pairs={{0,1},{1,0},{2,3},{3,2},{4,5},{5,4},{6,7},{7,6},{8,9},{9,8},{10,11... | collective-permute-start | bytes 3145736 | tf_op jit(solution)/shard_map/ppermute | solution.py:238
  31.4 6.8 %collective-permute-start.1 = (bf16[64,1024]{1,0:T(8,128)(2,1)S(1)}, bf16[64,1024]{1,0:T(8,128)(2,1)S(1)}, u32[]{:S(2)}, u32[]{:S(2)}) collective-permute-start(bf16[64,1024]{1,0:T(8,128)(2,1)S(1)} %reduce_sum.12), channel_id=1, source_target_pairs={{0,24},{1,25},{2,26},{3,27},{4,28},{5,29},{6,30},{7,31},{8,16},{9,... | collective-permute-start | bytes 393224 | tf_op jit(solution)/shard_map/ppermute | solution.py:238
  51.7 2.7 %collective-permute-start.2 = (bf16[8,64,1024]{2,1,0:T(8,128)(2,1)S(1)}, bf16[8,64,1024]{2,1,0:T(8,128)(2,1)S(1)}, u32[]{:S(2)}, u32[]{:S(2)}) collective-permute-start(bf16[8,64,1024]{2,1,0:T(8,128)(2,1)S(1)} %all_to_all.11.piece_hbm), channel_id=1, source_target_pairs={{0,1},{1,0},{2,3},{3,2},{4,5},{5,4},{6,7},{7,6},{8,9},{9,8},{10,11... | collective-permute-start | bytes 3145736 | tf_op jit(solution)/shard_map/ppermute | solution.py:238

commit v7 on v6

--- a/solution.py
+++ b/solution.py
@@ -11,7 +11,10 @@
 VMEM_LIMIT = 40 * 1024 * 1024
 ANY = pl.BlockSpec(memory_space=pl.ANY)
 WHOLE = pl.BlockSpec(memory_space=pltpu.VMEM)
-SCALAR = pl.BlockSpec(memory_space=pltpu.SMEM)
+
+
+def own_core():
+    return lax.axis_index("dp") & 1
 
 
 def dot(left, right):
@@ -57,7 +60,7 @@
 
 
 def query_kernel(
-    core_ref, hidden_hbm, weight_hbm, keys_hbm, values_hbm, grad_out_hbm,
+    hidden_hbm, weight_hbm, keys_hbm, values_hbm, grad_out_hbm,
     other, hidden, query, grads,
     weight, keys, values, grad_out, hidden_sem, weight_sem, small_sem,
 ):
@@ -88,13 +91,13 @@
     query[...] = rounded
     for copy in small:
         copy.wait()
-    second = core_ref[0] == 0
+    second = own_core() == 0
     found = heads_grad(half_of(rounded, second), keys[...], values[...], half_of(grad_out[...], second))
     grads[...] = found
     add_rows(found, hidden, other)
 
 
-def query_and_other(blocks, core, hidden_in, query_weight, keys, values, grad_out):
+def query_and_other(blocks, hidden_in, query_weight, keys, values, grad_out):
     tokens, width = hidden_in.shape
     rows = query_weight.shape[0]
     like = lambda array: pltpu.VMEM(array.shape, array.dtype)
@@ -107,7 +110,7 @@
             jax.ShapeDtypeStruct((tokens, rows), jnp.bfloat16),
             jax.ShapeDtypeStruct((tokens, rows // 2), jnp.bfloat16),
         ),
-        in_specs=[SCALAR] + [ANY] * 5,
+        in_specs=[ANY] * 5,
         out_specs=(WHOLE,) * 4,
         scratch_shapes=[
             like(query_weight),
@@ -124,11 +127,11 @@
             bytes_accessed=2 * (tokens * width + rows * width),
             transcendentals=tokens * tokens,
         ),
-    )(core, *(pltpu.with_memory_space_constraint(operand, pltpu.HBM) for operand in operands))
-
-
-def own_kernel(core_ref, hidden, query, others, keys, values, grad_out, own, grad_query):
-    second = core_ref[0] == 1
+    )(*(pltpu.with_memory_space_constraint(operand, pltpu.HBM) for operand in operands))
+
+
+def own_kernel(hidden, query, others, keys, values, grad_out, own, grad_query):
+    second = own_core() == 1
     grads = heads_grad(half_of(query[...], second), keys[...], values[...], half_of(grad_out[...], second))
     add_rows(grads, hidden, own)
     before = others[...]
@@ -137,7 +140,7 @@
     )
 
 
-def own_part(blocks, core, hidden, query, others, keys, values, grad_out):
+def own_part(blocks, hidden, query, others, keys, values, grad_out):
     tokens, width = hidden.shape
     rows = query.shape[1]
     return pl.pallas_call(
@@ -146,19 +149,19 @@
             jax.ShapeDtypeStruct((blocks, rows // 2, width // blocks), jnp.bfloat16),
             jax.ShapeDtypeStruct((tokens, rows), jnp.bfloat16),
         ),
-        in_specs=[SCALAR] + [WHOLE] * 6,
+        in_specs=[WHOLE] * 6,
         out_specs=(WHOLE,) * 2,
         compiler_params=pltpu.CompilerParams(vmem_limit_bytes=24 * 1024 * 1024),
         cost_estimate=pl.CostEstimate(
             flops=tokens * width * rows, bytes_accessed=2 * tokens * width, transcendentals=tokens * tokens
         ),
-    )(core, hidden, query, others, keys, values, grad_out)
-
-
-def hidden_kernel(core_ref, turn_ref, grad_query, weight_hbm, *refs):
+    )(hidden, query, others, keys, values, grad_out)
+
+
+def hidden_kernel(turn, grad_query, weight_hbm, *refs):
     out_hbm, weight, found, weight_sem, out_sem = refs[-5:]
 
-    @pl.when(core_ref[0] == turn_ref[0])
+    @pl.when(own_core() == turn)
     def _():
         blocks, _, step = found.shape
         copies = []
@@ -180,14 +183,14 @@
             copy.wait()
 
 
-def hidden_part(core, turn, grad_query, query_weight, before=None):
+def hidden_part(turn, grad_query, query_weight, before=None):
     tokens, rows = grad_query.shape
     width = query_weight.shape[1]
     given = () if before is None else (before,)
     return pl.pallas_call(
-        hidden_kernel,
+        functools.partial(hidden_kernel, turn),
         out_shape=jax.ShapeDtypeStruct((tokens, width), jnp.bfloat16),
-        in_specs=[SCALAR, SCALAR, WHOLE, ANY] + [ANY] * len(given),
+        in_specs=[WHOLE, ANY] + [ANY] * len(given),
         out_specs=ANY,
         scratch_shapes=[
             pltpu.VMEM((rows, width), jnp.bfloat16),
@@ -195,17 +198,18 @@
             pltpu.SemaphoreType.DMA((LOADS,)),
             pltpu.SemaphoreType.DMA((LOADS,)),
         ],
-        input_output_aliases={4: 0} if given else {},
+        input_output_aliases={2: 0} if given else {},
         compiler_params=pltpu.CompilerParams(vmem_limit_bytes=24 * 1024 * 1024),
         cost_estimate=pl.CostEstimate(
             flops=2 * tokens * width * rows, bytes_accessed=2 * width * (tokens + rows), transcendentals=0
         ),
-    )(core, jnp.full((1,), turn, jnp.int32), grad_query, pltpu.with_memory_space_constraint(query_weight, pltpu.HBM), *given)
-
-
-def place_kernel(core_ref, piece_hbm, out_hbm, sem):
+    )(grad_query, pltpu.with_memory_space_constraint(query_weight, pltpu.HBM), *given)
+
+
+def place_kernel(turned, piece_hbm, *refs):
+    out_hbm, sem = refs[-2:]
     blocks, half, step = piece_hbm.shape
-    rows = pl.ds(pl.multiple_of(core_ref[0] * half, half), half)
+    rows = pl.ds(pl.multiple_of((own_core() ^ turned) * half, half), half)
     copies = [
         pltpu.make_async_copy(piece_hbm.at[block], out_hbm.at[rows, pl.ds(block * step, step)], sem.at[block])
         for block in range(blocks)
@@ -216,22 +220,18 @@
         copy.wait()
 
 
-def place_kernel_on(core_ref, piece_hbm, before_hbm, out_hbm, sem):
-    place_kernel(core_ref, piece_hbm, out_hbm, sem)
-
-
-def place(core, piece, before=None):
+def place(turned, piece, before=None):
     blocks, half, step = piece.shape
     return pl.pallas_call(
-        place_kernel if before is None else place_kernel_on,
+        functools.partial(place_kernel, turned),
         out_shape=jax.ShapeDtypeStruct((2 * half, blocks * step), jnp.bfloat16),
-        in_specs=[SCALAR, ANY] + [ANY] * (before is not None),
+        in_specs=[ANY] + [ANY] * (before is not None),
         out_specs=ANY,
         scratch_shapes=[pltpu.SemaphoreType.DMA((blocks,))],
-        input_output_aliases={} if before is None else {2: 0},
+        input_output_aliases={} if before is None else {1: 0},
         compiler_params=pltpu.CompilerParams(vmem_limit_bytes=VMEM_LIMIT),
         cost_estimate=pl.CostEstimate(flops=0, bytes_accessed=4 * half * blocks * step, transcendentals=0),
-    )(core, piece, *(() if before is None else (before,)))
+    )(piece, *(() if before is None else (before,)))
 
 
 def swap(array, step, count):
@@ -254,29 +254,27 @@
     given_width = hidden_in.shape[1]
     if given_width != query_weight.shape[1]:
         hidden_in = lax.all_gather(hidden_in, "tensor", axis=1, tiled=True)
-    core = (lax.axis_index("dp") & 1).astype(jnp.int32).reshape(1)
     keys, values = saved_keys.T, saved_values.T
     other, hidden, query, grads = query_and_other(
-        blocks, core, hidden_in, query_weight, keys, values, grad_out
+        blocks, hidden_in, query_weight, keys, values, grad_out
     )
     arriving = swap(other, 1, count)
-    own, grad_query = own_part(blocks, core, hidden, query, grads, keys, values, grad_out)
+    own, grad_query = own_part(blocks, hidden, query, grads, keys, values, grad_out)
     chip = add(own, arriving)
-    input_terms = hidden_part(core, 0, grad_query, query_weight)
+    input_terms = hidden_part(0, grad_query, query_weight)
     chip, input_terms = lax.optimization_barrier((chip, input_terms))
     parts = lax.all_to_all(chip, "dp", 0, 0, axis_index_groups=groups)
     total = jnp.sum(parts.astype(jnp.float32), axis=0).astype(jnp.bfloat16)
-    input_terms, total = lax.optimization_barrier((input_terms, total))
-    input_terms = hidden_part(core, 1, grad_query, query_weight, input_terms)
     for bit in range(wide + 1, bits):
         arriving = swap(total, 3 << wide if bit == wide + 1 else 1 << bit, count)
-        if bit == wide + 1:
-            arriving, input_terms = lax.optimization_barrier((arriving, input_terms))
         total = add(total, arriving)
     copies = jnp.broadcast_to(total[None], (blocks, *total.shape))
     gathered = lax.all_to_all(copies, "dp", 0, 0, axis_index_groups=groups)
+    input_terms, gathered = lax.optimization_barrier((input_terms, gathered))
+    input_terms = hidden_part(1, grad_query, query_weight, input_terms)
+    input_terms, gathered = lax.optimization_barrier((input_terms, gathered))
     arriving = swap(gathered, 1, count)
-    grad_query_weight = place(1 - core, arriving, place(core, gathered))
+    grad_query_weight = place(1, arriving, place(0, gathered))
     if input_terms.shape[1] == given_width:
         grad_hidden = input_terms
     else:

time: 55.6 us -> 55.8 us (level)
  transfers between devices with their start and end apart: 3 -> 3, of which waited for: 2 -> 2; matrix products, arithmetic and copies ran while one was open for 0% -> 0% of each run, Pallas kernels for 13% -> 12%
where the time goes in v7:
time: 55.8 us; the launch traced here: 55.6 us
  blocking collectives  30.8 us (55%)
  Pallas kernels  14.2 us (25%)
  waiting for transfers between devices  5.78 us (10%)
  starting transfers between devices  3.25 us (6%)
  between operations  0.74 us (1%)
  other arithmetic  0.62 us (1%)
    all_to_all x1, blocking collectives, per_device(): parts = lax.all_to_all(chip, 'dp', 0, 0, axis_index_groups=groups)  17.6 us
    all_to_all x1, blocking collectives, per_device(): gathered = lax.all_to_all(copies, 'dp', 0, 0, axis_index_groups=groups)  13.3 us
    pallas_call x1, Pallas kernels, query_and_other(): pl.pallas_call(query_kernel, out_shape=(jax.ShapeDtypeStruct((blocks, row...  6.12 us
    ppermute x3, waiting for transfers between devices, swap(): return lax.ppermute(array, 'dp', [(i, i ^ step) for i in range(count)])  5.78 us
    pallas_call x2, Pallas kernels, hidden_part(): pl.pallas_call(functools.partial(hidden_kernel, turn), out_shape=jax.Shap...  4.32 us
    ppermute x3, starting transfers between devices, swap(): return lax.ppermute(array, 'dp', [(i, i ^ step) for i in range(count)])  3.25 us
    pallas_call x2, Pallas kernels, place(): pl.pallas_call(functools.partial(place_kernel, turned), out_shape=jax.Sha...  2.06 us
    pallas_call x1, Pallas kernels, own_part(): pl.pallas_call(own_kernel, out_shape=(jax.ShapeDtypeStruct((blocks, rows...  1.72 us
  transfers between devices with their start and end apart: 3, of which 2 were waited for; matrix products, arithmetic and copies ran while one was open for 0% of the time, Pallas kernels for 12%

profile of v7, /device:TPU:0, one launch (start us, length us, event | category | flops | bytes accessed | tf_op | source)
XLA Modules:
  0.0 55.6 jit_solution(2226898585521305885)
XLA Ops:
  0.6 0.0 copy-start
  0.6 0.0 copy-start.1
  0.7 0.0 copy-start.2
  0.7 6.1 %shard_map.68 = (bf16[8,64,1024]{2,1,0:T(8,128)(2,1)S(1)}, bf16[256,8192]{1,0:T(8,128)(2,1)S(1)}, bf16[256,128]{1,0:T(8,128)(2,1)S(1)}, bf16[256,64]{1,0:T(8,128)(2,1)S(1)}) custom-call(bf16[256,8192]{1,0:T(8,128)(2,1)} %hidden_hbm.1, bf16[128,8192]{1,0:T(8,128)(2,1)} %weight_hbm.5, bf16[64,256]{1,0:T(8,128)(2,1)} %bitcast.2, bf16[64,256]{1,0:T(8,128)(2,1)} %bitcast.4, ...), custom_call_target="tpu_custom_call" | custom-call | flops 805306368 | bytes 6291456 | tf_op jit(solution)/shard_map/pallas_call | solution.py:105
  6.8 0.5 collective-permute-start
  7.3 0.0 copy-done
  7.3 0.0 copy-done.1
  7.3 0.0 copy-done.2
  7.3 1.7 %shard_map.69 = (bf16[8,64,1024]{2,1,0:T(8,128)(2,1)S(1)}, bf16[256,128]{1,0:T(8,128)(2,1)S(1)}) custom-call(bf16[256,8192]{1,0:T(8,128)(2,1)S(1)} %get-tuple-element.14.hidden, bf16[256,128]{1,0:T(8,128)(2,1)S(1)} %get-tuple-element.15.query, bf16[256,64]{1,0:T(8,128)(2,1)S(1)} %get-tuple-element.16.others, bf16[64,256]{1,0:T(8,128)(2,1)S(1)} %bitcast.3, ...), custom_call_target="tpu_custom_call" | custom-call | flops 268435456 | bytes 4194304 | tf_op jit(solution)/shard_map/pallas_call | solution.py:146
  9.0 4.2 %shard_map.70.refs_0_ = bf16[256,8192]{1,0:T(8,128)(2,1)} custom-call(bf16[256,128]{1,0:T(8,128)(2,1)S(1)} %get-tuple-element.17.grad_query, bf16[128,8192]{1,0:T(8,128)(2,1)} %weight_hbm.5), custom_call_target="tpu_custom_call" | custom-call | flops 536870912 | bytes 6291456 | tf_op jit(solution)/shard_map/pallas_call | solution.py:190
  13.2 0.0 collective-permute-done
  13.2 0.4 add_convert_fusion
  13.7 17.6 %all_to_all.10 = bf16[8,64,1024]{2,1,0:T(8,128)(2,1)S(1)} all-to-all(bf16[8,64,1024]{2,1,0:T(8,128)(2,1)S(1)} %add_convert_fusion), channel_id=1, replica_groups={{0,2,4,6,8,10,12,14},{1,3,5,7,9,11,13,15},{24,26,28,30,16,18,20,22},{25..., dimensions={0} | all-to-all | bytes 2097152 | tf_op jit(solution)/shard_map/all_to_all | solution.py:266
  31.2 0.2 reduce_sum.12
  31.4 2.7 %collective-permute-start.1 = (bf16[64,1024]{1,0:T(8,128)(2,1)S(1)}, bf16[64,1024]{1,0:T(8,128)(2,1)S(1)}, u32[]{:S(2)}, u32[]{:S(2)}) collective-permute-start(bf16[64,1024]{1,0:T(8,128)(2,1)S(1)} %reduce_sum.12), channel_id=1, source_target_pairs={{0,24},{1,25},{2,26},{3,27},{4,28},{5,29},{6,30},{7,31},{8,16},{9,... | collective-permute-start | bytes 393224 | tf_op jit(solution)/shard_map/ppermute | solution.py:238
  34.1 4.2 %collective-permute-done.1 = bf16[64,1024]{1,0:T(8,128)(2,1)S(1)} collective-permute-done((bf16[64,1024]{1,0:T(8,128)(2,1)S(1)}, bf16[64,1024]{1,0:T(8,128)(2,1)S(1)}, u32[]{:S(2)}, u32[]{:S(2)}) %collective-permute-start.1) | collective-permute-done | bytes 131104 | tf_op jit(solution)/shard_map/ppermute | solution.py:238
  38.3 0.1 broadcast_in_dim.2
  38.4 13.3 %all_to_all.11.piece_hbm = bf16[8,64,1024]{2,1,0:T(8,128)(2,1)S(1)} all-to-all(bf16[8,64,1024]{2,1,0:T(8,128)(2,1)S(1)} %broadcast_in_dim.2), channel_id=1, replica_groups={{0,2,4,6,8,10,12,14},{1,3,5,7,9,11,13,15},{24,26,28,30,16,18,20,22},{25..., dimensions={0} | all-to-all | bytes 2097152 | tf_op jit(solution)/shard_map/all_to_all | solution.py:272
  51.7 0.1 shard_map.71
  51.8 0.1 collective-permute-start.2
  51.9 1.0 %shard_map.72.refs_0_ = bf16[128,8192]{1,0:T(8,128)(2,1)} custom-call(bf16[8,64,1024]{2,1,0:T(8,128)(2,1)S(1)} %all_to_all.11.piece_hbm), custom_call_target="tpu_custom_call" | custom-call | bytes 2097152 | tf_op jit(solution)/shard_map/pallas_call | solution.py:225
  53.0 1.6 %collective-permute-done.2.piece_hbm = bf16[8,64,1024]{2,1,0:T(8,128)(2,1)S(1)} collective-permute-done((bf16[8,64,1024]{2,1,0:T(8,128)(2,1)S(1)}, bf16[8,64,1024]{2,1,0:T(8,128)(2,1)S(1)}, u32[]{:S(2)}, u32[]{:S(2)}) %collective-permute-start.2) | collective-permute-done | bytes 1048608 | tf_op jit(solution)/shard_map/ppermute | solution.py:238
  54.6 1.0 %shard_map.73 = bf16[128,8192]{1,0:T(8,128)(2,1)} custom-call(bf16[8,64,1024]{2,1,0:T(8,128)(2,1)S(1)} %collective-permute-done.2.piece_hbm, bf16[128,8192]{1,0:T(8,128)(2,1)} %shard_map.72.refs_0_), custom_call_target="tpu_custom_call", output_to_operand_aliasing={{}: (1, {})} | custom-call | bytes 2097152 | tf_op jit(solution)/shard_map/pallas_call | solution.py:225
  (1 shorter events, 0.0 us)
Async XLA Ops:
  0.6 6.7 %copy-start = (bf16[256,128]{1,0:T(8,128)(2,1)S(1)}, bf16[256,128]{1,0:T(8,128)(2,1)}, u32[]{:S(2)}) copy-start(bf16[256,128]{1,0:T(8,128)(2,1)} %grad_out.1) | copy-start | bytes 196612
  0.6 6.7 %copy-start.1 = (bf16[256,64]{0,1:T(8,128)(2,1)S(1)}, bf16[256,64]{0,1:T(8,128)(2,1)}, u32[]{:S(2)}) copy-start(bf16[256,64]{0,1:T(8,128)(2,1)} %param.7) | copy-start | bytes 98308
  0.7 6.7 %copy-start.2 = (bf16[256,64]{0,1:T(8,128)(2,1)S(1)}, bf16[256,64]{0,1:T(8,128)(2,1)}, u32[]{:S(2)}) copy-start(bf16[256,64]{0,1:T(8,128)(2,1)} %param.8) | copy-start | bytes 98308
  6.8 6.4 %collective-permute-start = (bf16[8,64,1024]{2,1,0:T(8,128)(2,1)S(1)}, bf16[8,64,1024]{2,1,0:T(8,128)(2,1)S(1)}, u32[]{:S(2)}, u32[]{:S(2)}) collective-permute-start(bf16[8,64,1024]{2,1,0:T(8,128)(2,1)S(1)} %get-tuple-element.19), channel_id=1, source_target_pairs={{0,1},{1,0},{2,3},{3,2},{4,5},{5,4},{6,7},{7,6},{8,9},{9,8},{10,11... | collective-permute-start | bytes 3145736 | tf_op jit(solution)/shard_map/ppermute | solution.py:238
  31.4 6.8 %collective-permute-start.1 = (bf16[64,1024]{1,0:T(8,128)(2,1)S(1)}, bf16[64,1024]{1,0:T(8,128)(2,1)S(1)}, u32[]{:S(2)}, u32[]{:S(2)}) collective-permute-start(bf16[64,1024]{1,0:T(8,128)(2,1)S(1)} %reduce_sum.12), channel_id=1, source_target_pairs={{0,24},{1,25},{2,26},{3,27},{4,28},{5,29},{6,30},{7,31},{8,16},{9,... | collective-permute-start | bytes 393224 | tf_op jit(solution)/shard_map/ppermute | solution.py:238
  51.8 2.7 %collective-permute-start.2 = (bf16[8,64,1024]{2,1,0:T(8,128)(2,1)S(1)}, bf16[8,64,1024]{2,1,0:T(8,128)(2,1)S(1)}, u32[]{:S(2)}, u32[]{:S(2)}) collective-permute-start(bf16[8,64,1024]{2,1,0:T(8,128)(2,1)S(1)} %all_to_all.11.piece_hbm), channel_id=1, source_target_pairs={{0,1},{1,0},{2,3},{3,2},{4,5},{5,4},{6,7},{7,6},{8,9},{9,8},{10,11... | collective-permute-start | bytes 3145736 | tf_op jit(solution)/shard_map/ppermute | solution.py:238

commit v8 on v7

--- a/solution.py
+++ b/solution.py
@@ -7,7 +7,7 @@
 from jax.experimental.pallas import tpu as pltpu
 from jax.sharding import PartitionSpec as P
 
-LOADS = 8
+LOADS = 4
 VMEM_LIMIT = 40 * 1024 * 1024
 ANY = pl.BlockSpec(memory_space=pl.ANY)
 WHOLE = pl.BlockSpec(memory_space=pltpu.VMEM)
@@ -61,32 +61,30 @@
 
 def query_kernel(
     hidden_hbm, weight_hbm, keys_hbm, values_hbm, grad_out_hbm,
-    other, hidden, query, grads,
-    weight, keys, values, grad_out, hidden_sem, weight_sem, small_sem,
+    other, hidden, weight, query, grads,
+    turned, keys, values, grad_out, hidden_sem, weight_sem, small_sem,
 ):
     tokens, width = hidden.shape
-    blocks = hidden_sem.shape[0]
-    step = width // blocks
-    copies = []
-    for block in range(blocks):
-        columns = pl.ds(block * step, step)
-        pair = [
-            pltpu.make_async_copy(weight_hbm.at[:, columns], weight.at[:, columns], weight_sem.at[block]),
-            pltpu.make_async_copy(hidden_hbm.at[:, columns], hidden.at[:, columns], hidden_sem.at[block]),
-        ]
-        for copy in pair:
-            copy.start()
-        copies.append(pair)
+    step = width // LOADS
+    chunks = [pl.ds(at * step, step) for at in range(LOADS)]
+    weights = [
+        pltpu.make_async_copy(weight_hbm.at[:, columns], weight.at[:, columns], weight_sem.at[at])
+        for at, columns in enumerate(chunks)
+    ]
+    hiddens = [
+        pltpu.make_async_copy(hidden_hbm.at[:, columns], hidden.at[:, columns], hidden_sem.at[at])
+        for at, columns in enumerate(chunks)
+    ]
     pairs = ((keys_hbm, keys), (values_hbm, values), (grad_out_hbm, grad_out))
     small = [pltpu.make_async_copy(*pair, small_sem.at[at]) for at, pair in enumerate(pairs)]
-    for copy in small:
+    for copy in weights + hiddens + small:
         copy.start()
     total = jnp.zeros((tokens, weight.shape[0]), jnp.float32)
-    for block in range(blocks):
-        for copy in copies[block]:
-            copy.wait()
-        columns = pl.ds(block * step, step)
-        total += dot_tt(hidden[:, columns], weight[:, columns])
+    for at, columns in enumerate(chunks):
+        weights[at].wait()
+        turned[columns, :] = weight[:, columns].T
+        hiddens[at].wait()
+        total += dot(hidden[:, columns], turned[columns, :])
     rounded = total.astype(jnp.bfloat16)
     query[...] = rounded
     for copy in small:
@@ -107,13 +105,14 @@
         out_shape=(
             jax.ShapeDtypeStruct((blocks, rows // 2, width // blocks), jnp.bfloat16),
             jax.ShapeDtypeStruct((tokens, width), jnp.bfloat16),
+            jax.ShapeDtypeStruct((rows, width), jnp.bfloat16),
             jax.ShapeDtypeStruct((tokens, rows), jnp.bfloat16),
             jax.ShapeDtypeStruct((tokens, rows // 2), jnp.bfloat16),
         ),
         in_specs=[ANY] * 5,
-        out_specs=(WHOLE,) * 4,
+        out_specs=(WHOLE,) * 5,
         scratch_shapes=[
-            like(query_weight),
+            pltpu.VMEM((width, rows), jnp.bfloat16),
             like(keys),
             like(values),
             like(grad_out),
@@ -158,44 +157,34 @@
     )(hidden, query, others, keys, values, grad_out)
 
 
-def hidden_kernel(turn, grad_query, weight_hbm, *refs):
-    out_hbm, weight, found, weight_sem, out_sem = refs[-5:]
+def hidden_kernel(turn, grad_query, weight, *refs):
+    out_hbm, found, sem = refs[-3:]
 
     @pl.when(own_core() == turn)
     def _():
-        blocks, _, step = found.shape
-        copies = []
-        for block in range(blocks):
-            columns = pl.ds(block * step, step)
-            copies.append(
-                pltpu.make_async_copy(weight_hbm.at[:, columns], weight.at[:, columns], weight_sem.at[block])
-            )
-            copies[-1].start()
+        pieces, _, step = found.shape
         grads = grad_query[...]
         sent = []
-        for block in range(blocks):
-            columns = pl.ds(block * step, step)
-            copies[block].wait()
-            found[block] = dot(grads, weight[:, columns]).astype(found.dtype)
-            sent.append(pltpu.make_async_copy(found.at[block], out_hbm.at[:, columns], out_sem.at[block]))
+        for piece in range(pieces):
+            columns = pl.ds(piece * step, step)
+            found[piece] = dot(grads, weight[:, columns]).astype(found.dtype)
+            sent.append(pltpu.make_async_copy(found.at[piece], out_hbm.at[:, columns], sem.at[piece]))
             sent[-1].start()
         for copy in sent:
             copy.wait()
 
 
-def hidden_part(turn, grad_query, query_weight, before=None):
+def hidden_part(turn, grad_query, weight, before=None):
     tokens, rows = grad_query.shape
-    width = query_weight.shape[1]
+    width = weight.shape[1]
     given = () if before is None else (before,)
     return pl.pallas_call(
         functools.partial(hidden_kernel, turn),
         out_shape=jax.ShapeDtypeStruct((tokens, width), jnp.bfloat16),
-        in_specs=[WHOLE, ANY] + [ANY] * len(given),
+        in_specs=[WHOLE, WHOLE] + [ANY] * len(given),
         out_specs=ANY,
         scratch_shapes=[
-            pltpu.VMEM((rows, width), jnp.bfloat16),
             pltpu.VMEM((LOADS, tokens, width // LOADS), jnp.bfloat16),
-            pltpu.SemaphoreType.DMA((LOADS,)),
             pltpu.SemaphoreType.DMA((LOADS,)),
         ],
         input_output_aliases={2: 0} if given else {},
@@ -203,7 +192,7 @@
         cost_estimate=pl.CostEstimate(
             flops=2 * tokens * width * rows, bytes_accessed=2 * width * (tokens + rows), transcendentals=0
         ),
-    )(grad_query, pltpu.with_memory_space_constraint(query_weight, pltpu.HBM), *given)
+    )(grad_query, weight, *given)
 
 
 def place_kernel(turned, piece_hbm, *refs):
@@ -255,24 +244,25 @@
     if given_width != query_weight.shape[1]:
         hidden_in = lax.all_gather(hidden_in, "tensor", axis=1, tiled=True)
     keys, values = saved_keys.T, saved_values.T
-    other, hidden, query, grads = query_and_other(
+    other, hidden, weight, query, grads = query_and_other(
         blocks, hidden_in, query_weight, keys, values, grad_out
     )
     arriving = swap(other, 1, count)
     own, grad_query = own_part(blocks, hidden, query, grads, keys, values, grad_out)
     chip = add(own, arriving)
-    input_terms = hidden_part(0, grad_query, query_weight)
+    input_terms = hidden_part(0, grad_query, weight)
     chip, input_terms = lax.optimization_barrier((chip, input_terms))
     parts = lax.all_to_all(chip, "dp", 0, 0, axis_index_groups=groups)
     total = jnp.sum(parts.astype(jnp.float32), axis=0).astype(jnp.bfloat16)
+    input_terms, total = lax.optimization_barrier((input_terms, total))
+    input_terms = hidden_part(1, grad_query, weight, input_terms)
     for bit in range(wide + 1, bits):
         arriving = swap(total, 3 << wide if bit == wide + 1 else 1 << bit, count)
+        if bit == wide + 1:
+            arriving, input_terms = lax.optimization_barrier((arriving, input_terms))
         total = add(total, arriving)
     copies = jnp.broadcast_to(total[None], (blocks, *total.shape))
     gathered = lax.all_to_all(copies, "dp", 0, 0, axis_index_groups=groups)
-    input_terms, gathered = lax.optimization_barrier((input_terms, gathered))
-    input_terms = hidden_part(1, grad_query, query_weight, input_terms)
-    input_terms, gathered = lax.optimization_barrier((input_terms, gathered))
     arriving = swap(gathered, 1, count)
     grad_query_weight = place(1, arriving, place(0, gathered))
     if input_terms.shape[1] == given_width:

time: 55.8 us -> 55.5 us (level)
  Pallas kernels: 14.2 us -> 11.8 us
  blocking collectives: 30.8 us -> 33.1 us
    pallas_call x2, Pallas kernels: 4.32 us -> 2.51 us  [hidden_part(): pl.pallas_call(functools.partial(hidden_kernel, turn), out_shape=jax.Shap...]
    all_to_all x1, blocking collectives: 17.6 us -> 19.3 us  [per_device(): parts = lax.all_to_all(chip, 'dp', 0, 0, axis_index_groups=groups)]
  transfers between devices with their start and end apart: 3 -> 3, of which waited for: 2 -> 2; matrix products, arithmetic and copies ran while one was open for 0% -> 0% of each run, Pallas kernels for 12% -> 9%
where the time goes in v8:
time: 55.5 us; the launch traced here: 55.3 us
  blocking collectives  33.1 us (60%)
  Pallas kernels  11.8 us (21%)
  waiting for transfers between devices  5.76 us (10%)
  starting transfers between devices  3.18 us (6%)
  between operations  0.73 us (1%)
  other arithmetic  0.62 us (1%)
    all_to_all x1, blocking collectives, per_device(): parts = lax.all_to_all(chip, 'dp', 0, 0, axis_index_groups=groups)  19.3 us
    all_to_all x1, blocking collectives, per_device(): gathered = lax.all_to_all(copies, 'dp', 0, 0, axis_index_groups=groups)  13.8 us
    ppermute x3, waiting for transfers between devices, swap(): return lax.ppermute(array, 'dp', [(i, i ^ step) for i in range(count)])  5.76 us
    pallas_call x1, Pallas kernels, query_and_other(): pl.pallas_call(query_kernel, out_shape=(jax.ShapeDtypeStruct((blocks, row...  5.58 us
    ppermute x3, starting transfers between devices, swap(): return lax.ppermute(array, 'dp', [(i, i ^ step) for i in range(count)])  3.18 us
    pallas_call x2, Pallas kernels, hidden_part(): pl.pallas_call(functools.partial(hidden_kernel, turn), out_shape=jax.Shap...  2.51 us
    pallas_call x2, Pallas kernels, place(): pl.pallas_call(functools.partial(place_kernel, turned), out_shape=jax.Sha...  2.05 us
    pallas_call x1, Pallas kernels, own_part(): pl.pallas_call(own_kernel, out_shape=(jax.ShapeDtypeStruct((blocks, rows...  1.71 us
  transfers between devices with their start and end apart: 3, of which 2 were waited for; matrix products, arithmetic and copies ran while one was open for 0% of the time, Pallas kernels for 9%

profile of v8, /device:TPU:0, one launch (start us, length us, event | category | flops | bytes accessed | tf_op | source)
XLA Modules:
  0.0 55.3 jit_solution(8451610327771732344)
XLA Ops:
  0.6 0.0 copy-start
  0.6 0.0 copy-start.1
  0.7 0.0 copy-start.2
  0.7 5.6 %shard_map.68 = (bf16[8,64,1024]{2,1,0:T(8,128)(2,1)S(1)}, bf16[256,8192]{1,0:T(8,128)(2,1)S(1)}, bf16[128,8192]{1,0:T(8,128)(2,1)S(1)}, bf16[256,128]{1,0:T(8,128)(2,1)S(1)}, bf16[256,64]{1,0:T(8,128)(2,1)S(1)}) custom-call(bf16[256,8192]{1,0:T(8,128)(2,1)} %hidden_hbm.1, bf16[128,8192]{1,0:T(8,128)(2,1)} %weight_hbm.1, bf16[64,256]{1,0:T(8,128)(2,1)} %bitcast.2, ...), custom_call_target="tpu_custom_call" | custom-call | flops 805306368 | bytes 6291456 | tf_op jit(solution)/shard_map/pallas_call | solution.py:103
  6.2 0.5 collective-permute-start
  6.8 0.0 copy-done
  6.8 0.0 copy-done.1
  6.8 0.0 copy-done.2
  6.8 1.7 %shard_map.69 = (bf16[8,64,1024]{2,1,0:T(8,128)(2,1)S(1)}, bf16[256,128]{1,0:T(8,128)(2,1)S(1)}) custom-call(bf16[256,8192]{1,0:T(8,128)(2,1)S(1)} %get-tuple-element.15.hidden, bf16[256,128]{1,0:T(8,128)(2,1)S(1)} %get-tuple-element.16.query, bf16[256,64]{1,0:T(8,128)(2,1)S(1)} %get-tuple-element.17.others, bf16[64,256]{1,0:T(8,128)(2,1)S(1)} %bitcast.3, ...), custom_call_target="tpu_custom_call" | custom-call | flops 268435456 | bytes 4194304 | tf_op jit(solution)/shard_map/pallas_call | solution.py:145
  8.5 2.5 %shard_map.70.refs_0_ = bf16[256,8192]{1,0:T(8,128)(2,1)} custom-call(bf16[256,128]{1,0:T(8,128)(2,1)S(1)} %get-tuple-element.20.grad_query, bf16[128,8192]{1,0:T(8,128)(2,1)S(1)} %get-tuple-element.21.weight), custom_call_target="tpu_custom_call" | custom-call | flops 536870912 | bytes 6291456 | tf_op jit(solution)/shard_map/pallas_call | solution.py:181
  11.0 0.0 collective-permute-done
  11.0 0.4 add_convert_fusion
  11.4 19.3 %all_to_all.10 = bf16[8,64,1024]{2,1,0:T(8,128)(2,1)S(1)} all-to-all(bf16[8,64,1024]{2,1,0:T(8,128)(2,1)S(1)} %add_convert_fusion), channel_id=1, replica_groups={{0,2,4,6,8,10,12,14},{1,3,5,7,9,11,13,15},{24,26,28,30,16,18,20,22},{25..., dimensions={0} | all-to-all | bytes 2097152 | tf_op jit(solution)/shard_map/all_to_all | solution.py:255
  30.7 0.2 reduce_sum.12
  30.9 2.7 %collective-permute-start.1 = (bf16[64,1024]{1,0:T(8,128)(2,1)S(1)}, bf16[64,1024]{1,0:T(8,128)(2,1)S(1)}, u32[]{:S(2)}, u32[]{:S(2)}) collective-permute-start(bf16[64,1024]{1,0:T(8,128)(2,1)S(1)} %reduce_sum.12), channel_id=1, source_target_pairs={{0,24},{1,25},{2,26},{3,27},{4,28},{5,29},{6,30},{7,31},{8,16},{9,... | collective-permute-start | bytes 393224 | tf_op jit(solution)/shard_map/ppermute | solution.py:227
  33.6 4.1 %collective-permute-done.1 = bf16[64,1024]{1,0:T(8,128)(2,1)S(1)} collective-permute-done((bf16[64,1024]{1,0:T(8,128)(2,1)S(1)}, bf16[64,1024]{1,0:T(8,128)(2,1)S(1)}, u32[]{:S(2)}, u32[]{:S(2)}) %collective-permute-start.1) | collective-permute-done | bytes 131104 | tf_op jit(solution)/shard_map/ppermute | solution.py:227
  37.8 0.1 broadcast_in_dim.2
  37.9 13.8 %all_to_all.11.piece_hbm = bf16[8,64,1024]{2,1,0:T(8,128)(2,1)S(1)} all-to-all(bf16[8,64,1024]{2,1,0:T(8,128)(2,1)S(1)} %broadcast_in_dim.2), channel_id=1, replica_groups={{0,2,4,6,8,10,12,14},{1,3,5,7,9,11,13,15},{24,26,28,30,16,18,20,22},{25..., dimensions={0} | all-to-all | bytes 2097152 | tf_op jit(solution)/shard_map/all_to_all | solution.py:265
  51.7 0.0 collective-permute-start.2
  51.7 1.0 %shard_map.72.refs_0_ = bf16[128,8192]{1,0:T(8,128)(2,1)} custom-call(bf16[8,64,1024]{2,1,0:T(8,128)(2,1)S(1)} %all_to_all.11.piece_hbm), custom_call_target="tpu_custom_call" | custom-call | bytes 2097152 | tf_op jit(solution)/shard_map/pallas_call | solution.py:214
  52.7 1.6 %collective-permute-done.2.piece_hbm = bf16[8,64,1024]{2,1,0:T(8,128)(2,1)S(1)} collective-permute-done((bf16[8,64,1024]{2,1,0:T(8,128)(2,1)S(1)}, bf16[8,64,1024]{2,1,0:T(8,128)(2,1)S(1)}, u32[]{:S(2)}, u32[]{:S(2)}) %collective-permute-start.2) | collective-permute-done | bytes 1048608 | tf_op jit(solution)/shard_map/ppermute | solution.py:227
  54.3 1.0 %shard_map.73 = bf16[128,8192]{1,0:T(8,128)(2,1)} custom-call(bf16[8,64,1024]{2,1,0:T(8,128)(2,1)S(1)} %collective-permute-done.2.piece_hbm, bf16[128,8192]{1,0:T(8,128)(2,1)} %shard_map.72.refs_0_), custom_call_target="tpu_custom_call", output_to_operand_aliasing={{}: (1, {})} | custom-call | bytes 2097152 | tf_op jit(solution)/shard_map/pallas_call | solution.py:214
  (2 shorter events, 0.1 us)
Async XLA Ops:
  0.6 6.1 %copy-start = (bf16[256,128]{1,0:T(8,128)(2,1)S(1)}, bf16[256,128]{1,0:T(8,128)(2,1)}, u32[]{:S(2)}) copy-start(bf16[256,128]{1,0:T(8,128)(2,1)} %grad_out.1) | copy-start | bytes 196612
  0.6 6.1 %copy-start.1 = (bf16[256,64]{0,1:T(8,128)(2,1)S(1)}, bf16[256,64]{0,1:T(8,128)(2,1)}, u32[]{:S(2)}) copy-start(bf16[256,64]{0,1:T(8,128)(2,1)} %param.7) | copy-start | bytes 98308
  0.7 6.1 %copy-start.2 = (bf16[256,64]{0,1:T(8,128)(2,1)S(1)}, bf16[256,64]{0,1:T(8,128)(2,1)}, u32[]{:S(2)}) copy-start(bf16[256,64]{0,1:T(8,128)(2,1)} %param.8) | copy-start | bytes 98308
  6.2 4.7 %collective-permute-start = (bf16[8,64,1024]{2,1,0:T(8,128)(2,1)S(1)}, bf16[8,64,1024]{2,1,0:T(8,128)(2,1)S(1)}, u32[]{:S(2)}, u32[]{:S(2)}) collective-permute-start(bf16[8,64,1024]{2,1,0:T(8,128)(2,1)S(1)} %get-tuple-element.19), channel_id=1, source_target_pairs={{0,1},{1,0},{2,3},{3,2},{4,5},{5,4},{6,7},{7,6},{8,9},{9,8},{10,11... | collective-permute-start | bytes 3145736 | tf_op jit(solution)/shard_map/ppermute | solution.py:227
  30.9 6.8 %collective-permute-start.1 = (bf16[64,1024]{1,0:T(8,128)(2,1)S(1)}, bf16[64,1024]{1,0:T(8,128)(2,1)S(1)}, u32[]{:S(2)}, u32[]{:S(2)}) collective-permute-start(bf16[64,1024]{1,0:T(8,128)(2,1)S(1)} %reduce_sum.12), channel_id=1, source_target_pairs={{0,24},{1,25},{2,26},{3,27},{4,28},{5,29},{6,30},{7,31},{8,16},{9,... | collective-permute-start | bytes 393224 | tf_op jit(solution)/shard_map/ppermute | solution.py:227
  51.7 2.7 %collective-permute-start.2 = (bf16[8,64,1024]{2,1,0:T(8,128)(2,1)S(1)}, bf16[8,64,1024]{2,1,0:T(8,128)(2,1)S(1)}, u32[]{:S(2)}, u32[]{:S(2)}) collective-permute-start(bf16[8,64,1024]{2,1,0:T(8,128)(2,1)S(1)} %all_to_all.11.piece_hbm), channel_id=1, source_target_pairs={{0,1},{1,0},{2,3},{3,2},{4,5},{5,4},{6,7},{7,6},{8,9},{9,8},{10,11... | collective-permute-start | bytes 3145736 | tf_op jit(solution)/shard_map/ppermute | solution.py:227

commit v9 on v8

--- a/solution.py
+++ b/solution.py
@@ -8,6 +8,7 @@
 from jax.sharding import PartitionSpec as P
 
 LOADS = 4
+LAST = 2
 VMEM_LIMIT = 40 * 1024 * 1024
 ANY = pl.BlockSpec(memory_space=pl.ANY)
 WHOLE = pl.BlockSpec(memory_space=pltpu.VMEM)
@@ -15,6 +16,11 @@
 
 def own_core():
     return lax.axis_index("dp") & 1
+
+
+def own_place(blocks):
+    index = lax.axis_index("dp") >> 1
+    return (index & (blocks - 1)) ^ ((index >> (blocks.bit_length() - 1) & 1) * (blocks >> 1))
 
 
 def dot(left, right):
@@ -195,32 +201,33 @@
     )(grad_query, weight, *given)
 
 
-def place_kernel(turned, piece_hbm, *refs):
+def place_kernel(blocks, plan, *refs):
     out_hbm, sem = refs[-2:]
-    blocks, half, step = piece_hbm.shape
-    rows = pl.ds(pl.multiple_of((own_core() ^ turned) * half, half), half)
-    copies = [
-        pltpu.make_async_copy(piece_hbm.at[block], out_hbm.at[rows, pl.ds(block * step, step)], sem.at[block])
-        for block in range(blocks)
-    ]
-    for copy in copies:
-        copy.start()
+    half, step = refs[0].shape
+    own = own_place(blocks)
+    copies = []
+    for at, (distance, turned) in enumerate(plan):
+        rows = pl.ds(pl.multiple_of((own_core() ^ turned) * half, half), half)
+        columns = pl.ds(pl.multiple_of((own ^ distance) * step, step), step)
+        copies.append(pltpu.make_async_copy(refs[at], out_hbm.at[rows, columns], sem.at[at]))
+        copies[-1].start()
     for copy in copies:
         copy.wait()
 
 
-def place(turned, piece, before=None):
-    blocks, half, step = piece.shape
+def place(blocks, plan, pieces, before=None):
+    half, step = pieces[0].shape
+    given = () if before is None else (before,)
     return pl.pallas_call(
-        functools.partial(place_kernel, turned),
+        functools.partial(place_kernel, blocks, plan),
         out_shape=jax.ShapeDtypeStruct((2 * half, blocks * step), jnp.bfloat16),
-        in_specs=[ANY] + [ANY] * (before is not None),
+        in_specs=[ANY] * (len(pieces) + len(given)),
         out_specs=ANY,
-        scratch_shapes=[pltpu.SemaphoreType.DMA((blocks,))],
-        input_output_aliases={} if before is None else {1: 0},
+        scratch_shapes=[pltpu.SemaphoreType.DMA((len(pieces),))],
+        input_output_aliases={len(pieces): 0} if given else {},
         compiler_params=pltpu.CompilerParams(vmem_limit_bytes=VMEM_LIMIT),
-        cost_estimate=pl.CostEstimate(flops=0, bytes_accessed=4 * half * blocks * step, transcendentals=0),
-    )(piece, *(() if before is None else (before,)))
+        cost_estimate=pl.CostEstimate(flops=0, bytes_accessed=4 * half * step * len(pieces), transcendentals=0),
+    )(*pieces, *given)
 
 
 def swap(array, step, count):
@@ -229,6 +236,24 @@
 
 def add(left, right):
     return (left.astype(jnp.float32) + right.astype(jnp.float32)).astype(jnp.bfloat16)
+
+
+def gather(blocks, groups, total):
+    count = len(groups) * blocks
+    pieces = {0: total}
+    for distance in sorted(range(1, blocks), key=lambda distance: -distance.bit_count()):
+        pairs = [(group[at], group[at ^ distance]) for group in groups for at in range(blocks)]
+        pieces[distance] = lax.ppermute(total, "dp", pairs)
+    order = list(pieces)
+    cut = max(len(order) - LAST, 1)
+    result, turned = None, []
+    for part in filter(None, (order[:cut], order[cut:])):
+        held = lax.optimization_barrier([pieces[distance] for distance in part])
+        arriving = [swap(piece, 1, count) for piece in held]
+        plan = tuple((distance, 0) for distance in part) + tuple((distance, 1) for distance, _ in turned)
+        result = place(blocks, plan, held + [piece for _, piece in turned], result)
+        turned = list(zip(part, arriving))
+    return place(blocks, tuple((distance, 1) for distance, _ in turned), [piece for _, piece in turned], result)
 
 
 def per_device(count, hidden_in, query_weight, saved_keys, saved_values, grad_out):
@@ -261,10 +286,7 @@
         if bit == wide + 1:
             arriving, input_terms = lax.optimization_barrier((arriving, input_terms))
         total = add(total, arriving)
-    copies = jnp.broadcast_to(total[None], (blocks, *total.shape))
-    gathered = lax.all_to_all(copies, "dp", 0, 0, axis_index_groups=groups)
-    arriving = swap(gathered, 1, count)
-    grad_query_weight = place(1, arriving, place(0, gathered))
+    grad_query_weight = gather(blocks, groups, total)
     if input_terms.shape[1] == given_width:
         grad_hidden = input_terms
     else:

time: 55.5 us -> 55.4 us (level)
  blocking collectives: 33.1 us -> 19.3 us
  starting transfers between devices: 3.18 us -> 13.9 us
  waiting for transfers between devices: 5.76 us -> 8.14 us
  Pallas kernels: 11.8 us -> 12.5 us
    all_to_all x1 -> x0, blocking collectives: 13.8 us -> none  [per_device(): gathered = lax.all_to_all(copies, 'dp', 0, 0, axis_index_groups=groups)]
    ppermute x0 -> x7, starting transfers between devices: none -> 8.63 us  [gather(): pieces[distance] = lax.ppermute(total, 'dp', pairs)]
    ppermute x0 -> x7, waiting for transfers between devices: none -> 3.94 us  [gather(): pieces[distance] = lax.ppermute(total, 'dp', pairs)]
    ppermute x3 -> x10, starting transfers between devices: 3.18 us -> 5.22 us  [swap(): return lax.ppermute(array, 'dp', [(i, i ^ step) for i in range(count)])]
    ppermute x3 -> x10, waiting for transfers between devices: 5.76 us -> 4.2 us  [swap(): return lax.ppermute(array, 'dp', [(i, i ^ step) for i in range(count)])]
    pallas_call x2 -> x3, Pallas kernels: 2.05 us -> 2.69 us  [place(): pl.pallas_call(functools.partial(place_kernel, blocks, plan), out_shape=j...]
  transfers between devices with their start and end apart: 3 -> 17, of which waited for: 2 -> 5; matrix products, arithmetic and copies ran while one was open for 0% -> 0% of each run, Pallas kernels for 9% -> 11%
where the time goes in v9:
time: 55.4 us; the launch traced here: 55.2 us
  blocking collectives  19.3 us (35%)
  starting transfers between devices  13.9 us (25%)
  Pallas kernels  12.5 us (23%)
  waiting for transfers between devices  8.14 us (15%)
  between operations  0.78 us (1%)
  other arithmetic  0.62 us (1%)
    all_to_all x1, blocking collectives, per_device(): parts = lax.all_to_all(chip, 'dp', 0, 0, axis_index_groups=groups)  19.3 us
    ppermute x7, starting transfers between devices, gather(): pieces[distance] = lax.ppermute(total, 'dp', pairs)  8.63 us
    pallas_call x1, Pallas kernels, query_and_other(): pl.pallas_call(query_kernel, out_shape=(jax.ShapeDtypeStruct((blocks, row...  5.58 us
    ppermute x10, starting transfers between devices, swap(): return lax.ppermute(array, 'dp', [(i, i ^ step) for i in range(count)])  5.22 us
    ppermute x10, waiting for transfers between devices, swap(): return lax.ppermute(array, 'dp', [(i, i ^ step) for i in range(count)])  4.2 us
    ppermute x7, waiting for transfers between devices, gather(): pieces[distance] = lax.ppermute(total, 'dp', pairs)  3.94 us
    pallas_call x3, Pallas kernels, place(): pl.pallas_call(functools.partial(place_kernel, blocks, plan), out_shape=j...  2.69 us
    pallas_call x2, Pallas kernels, hidden_part(): pl.pallas_call(functools.partial(hidden_kernel, turn), out_shape=jax.Shap...  2.51 us
  transfers between devices with their start and end apart: 17, of which 5 were waited for; matrix products, arithmetic and copies ran while one was open for 0% of the time, Pallas kernels for 11%

profile of v9, /device:TPU:0, one launch (start us, length us, event | category | flops | bytes accessed | tf_op | source)
XLA Modules:
  0.0 55.2 jit_solution(8205872378429118815)
XLA Ops:
  0.6 0.0 copy-start
  0.6 0.0 copy-start.1
  0.7 0.0 copy-start.2
  0.7 5.6 %shard_map.68 = (bf16[8,64,1024]{2,1,0:T(8,128)(2,1)S(1)}, bf16[256,8192]{1,0:T(8,128)(2,1)S(1)}, bf16[128,8192]{1,0:T(8,128)(2,1)S(1)}, bf16[256,128]{1,0:T(8,128)(2,1)S(1)}, bf16[256,64]{1,0:T(8,128)(2,1)S(1)}) custom-call(bf16[256,8192]{1,0:T(8,128)(2,1)} %hidden_hbm.1, bf16[128,8192]{1,0:T(8,128)(2,1)} %weight_hbm.1, bf16[64,256]{1,0:T(8,128)(2,1)} %bitcast.2, ...), custom_call_target="tpu_custom_call" | custom-call | flops 805306368 | bytes 6291456 | tf_op jit(solution)/shard_map/pallas_call | solution.py:109
  6.2 0.5 collective-permute-start
  6.8 0.0 copy-done
  6.8 0.0 copy-done.1
  6.8 0.0 copy-done.2
  6.8 1.7 %shard_map.69 = (bf16[8,64,1024]{2,1,0:T(8,128)(2,1)S(1)}, bf16[256,128]{1,0:T(8,128)(2,1)S(1)}) custom-call(bf16[256,8192]{1,0:T(8,128)(2,1)S(1)} %get-tuple-element.23.hidden, bf16[256,128]{1,0:T(8,128)(2,1)S(1)} %get-tuple-element.24.query, bf16[256,64]{1,0:T(8,128)(2,1)S(1)} %get-tuple-element.25.others, bf16[64,256]{1,0:T(8,128)(2,1)S(1)} %bitcast.3, ...), custom_call_target="tpu_custom_call" | custom-call | flops 268435456 | bytes 4194304 | tf_op jit(solution)/shard_map/pallas_call | solution.py:151
  8.5 2.5 %shard_map.70.refs_0_ = bf16[256,8192]{1,0:T(8,128)(2,1)} custom-call(bf16[256,128]{1,0:T(8,128)(2,1)S(1)} %get-tuple-element.28.grad_query, bf16[128,8192]{1,0:T(8,128)(2,1)S(1)} %get-tuple-element.29.weight), custom_call_target="tpu_custom_call" | custom-call | flops 536870912 | bytes 6291456 | tf_op jit(solution)/shard_map/pallas_call | solution.py:187
  11.0 0.0 collective-permute-done
  11.0 0.4 add_convert_fusion
  11.4 19.3 %all_to_all.5 = bf16[8,64,1024]{2,1,0:T(8,128)(2,1)S(1)} all-to-all(bf16[8,64,1024]{2,1,0:T(8,128)(2,1)S(1)} %add_convert_fusion), channel_id=1, replica_groups={{0,2,4,6,8,10,12,14},{1,3,5,7,9,11,13,15},{24,26,28,30,16,18,20,22},{25..., dimensions={0} | all-to-all | bytes 2097152 | tf_op jit(solution)/shard_map/all_to_all | solution.py:280
  30.7 0.2 reduce_sum.12
  30.9 2.7 %collective-permute-start.1 = (bf16[64,1024]{1,0:T(8,128)(2,1)S(1)}, bf16[64,1024]{1,0:T(8,128)(2,1)S(1)}, u32[]{:S(2)}, u32[]{:S(2)}) collective-permute-start(bf16[64,1024]{1,0:T(8,128)(2,1)S(1)} %reduce_sum.12), channel_id=1, source_target_pairs={{0,24},{1,25},{2,26},{3,27},{4,28},{5,29},{6,30},{7,31},{8,16},{9,... | collective-permute-start | bytes 393224 | tf_op jit(solution)/shard_map/ppermute | solution.py:234
  33.6 4.2 %collective-permute-done.1 = bf16[64,1024]{1,0:T(8,128)(2,1)S(1)} collective-permute-done((bf16[64,1024]{1,0:T(8,128)(2,1)S(1)}, bf16[64,1024]{1,0:T(8,128)(2,1)S(1)}, u32[]{:S(2)}, u32[]{:S(2)}) %collective-permute-start.1) | collective-permute-done | bytes 131104 | tf_op jit(solution)/shard_map/ppermute | solution.py:234
  37.8 0.3 collective-permute-start.10
  38.1 0.0 collective-permute-start.9
  38.1 3.2 %collective-permute-start.8 = (bf16[64,1024]{1,0:T(8,128)(2,1)S(1)}, bf16[64,1024]{1,0:T(8,128)(2,1)S(1)}, u32[]{:S(2)}, u32[]{:S(2)}) collective-permute-start(bf16[64,1024]{1,0:T(8,128)(2,1)S(1)} %add_convert_fusion.1.refs_0_), channel_id=1, source_target_pairs={{0,10},{2,8},{4,14},{6,12},{8,2},{10,0},{12,6},{14,4},{1,11},{3,9}... | collective-permute-start | bytes 393224 | tf_op jit(solution)/shard_map/ppermute | solution.py:246
  41.3 1.2 %collective-permute-start.7 = (bf16[64,1024]{1,0:T(8,128)(2,1)S(1)}, bf16[64,1024]{1,0:T(8,128)(2,1)S(1)}, u32[]{:S(2)}, u32[]{:S(2)}) collective-permute-start(bf16[64,1024]{1,0:T(8,128)(2,1)S(1)} %add_convert_fusion.1.refs_0_), channel_id=1, source_target_pairs={{0,6},{2,4},{4,2},{6,0},{8,14},{10,12},{12,10},{14,8},{1,7},{3,5},... | collective-permute-start | bytes 393224 | tf_op jit(solution)/shard_map/ppermute | solution.py:246
  42.5 1.2 %collective-permute-start.6 = (bf16[64,1024]{1,0:T(8,128)(2,1)S(1)}, bf16[64,1024]{1,0:T(8,128)(2,1)S(1)}, u32[]{:S(2)}, u32[]{:S(2)}) collective-permute-start(bf16[64,1024]{1,0:T(8,128)(2,1)S(1)} %add_convert_fusion.1.refs_0_), channel_id=1, source_target_pairs={{0,14},{2,12},{4,10},{6,8},{8,6},{10,4},{12,2},{14,0},{1,15},{3,13... | collective-permute-start | bytes 393224 | tf_op jit(solution)/shard_map/ppermute | solution.py:246
  43.7 0.8 %collective-permute-done.10.refs_5_ = bf16[64,1024]{1,0:T(8,128)(2,1)S(1)} collective-permute-done((bf16[64,1024]{1,0:T(8,128)(2,1)S(1)}, bf16[64,1024]{1,0:T(8,128)(2,1)S(1)}, u32[]{:S(2)}, u32[]{:S(2)}) %collective-permute-start.10) | collective-permute-done | bytes 131104 | tf_op jit(solution)/shard_map/ppermute | solution.py:246
  44.5 1.4 %collective-permute-start.3 = (bf16[64,1024]{1,0:T(8,128)(2,1)S(1)}, bf16[64,1024]{1,0:T(8,128)(2,1)S(1)}, u32[]{:S(2)}, u32[]{:S(2)}) collective-permute-start(bf16[64,1024]{1,0:T(8,128)(2,1)S(1)} %add_convert_fusion.1.refs_0_), channel_id=1, source_target_pairs={{0,8},{2,10},{4,12},{6,14},{8,0},{10,2},{12,4},{14,6},{1,9},{3,11}... | collective-permute-start | bytes 393224 | tf_op jit(solution)/shard_map/ppermute | solution.py:246
  45.9 0.0 collective-permute-done.9.refs_4_
  45.9 1.3 %collective-permute-start.2 = (bf16[64,1024]{1,0:T(8,128)(2,1)S(1)}, bf16[64,1024]{1,0:T(8,128)(2,1)S(1)}, u32[]{:S(2)}, u32[]{:S(2)}) collective-permute-start(bf16[64,1024]{1,0:T(8,128)(2,1)S(1)} %add_convert_fusion.1.refs_0_), channel_id=1, source_target_pairs={{0,4},{2,6},{4,0},{6,2},{8,12},{10,14},{12,8},{14,10},{1,5},{3,7},... | collective-permute-start | bytes 393224 | tf_op jit(solution)/shard_map/ppermute | solution.py:246
  47.2 0.2 collective-permute-done.8.refs_3_
  47.4 2.6 %collective-permute-done.7.refs_2_ = bf16[64,1024]{1,0:T(8,128)(2,1)S(1)} collective-permute-done((bf16[64,1024]{1,0:T(8,128)(2,1)S(1)}, bf16[64,1024]{1,0:T(8,128)(2,1)S(1)}, u32[]{:S(2)}, u32[]{:S(2)}) %collective-permute-start.7) | collective-permute-done | bytes 131104 | tf_op jit(solution)/shard_map/ppermute | solution.py:246
  50.1 0.0 collective-permute-done.6.refs_1_
  50.1 0.0 collective-permute-start.11
  50.1 0.5 collective-permute-start.12
  50.6 0.0 collective-permute-start.13
  50.6 0.0 collective-permute-done.3.refs_1_
  50.6 0.5 collective-permute-start.14
  51.1 0.3 collective-permute-done.2.refs_0_
  51.4 0.0 collective-permute-start.15
  51.4 0.0 collective-permute-done.11.refs_2_
  51.4 0.5 collective-permute-start.16
  51.9 0.0 collective-permute-done.12.refs_3_
  51.9 0.1 collective-permute-start.4
  52.0 0.0 collective-permute-done.13.refs_4_
  52.0 0.4 collective-permute-start.5
  52.4 0.9 %shard_map.72.refs_8_ = bf16[128,8192]{1,0:T(8,128)(2,1)} custom-call(bf16[64,1024]{1,0:T(8,128)(2,1)S(1)} %add_convert_fusion.1.refs_0_, bf16[64,1024]{1,0:T(8,128)(2,1)S(1)} %collective-permute-done.6.refs_1_, bf16[64,1024]{1,0:T(8,128)(2,1)S(1)} %collective-permute-done.7.refs_2_, bf16[64,1024]{1,0:T(8,128)(2,1)S(1)} %collective-permute-done.8.refs_3_, ...), custom_call_target="tpu_custom_call" | custom-call | bytes 1572864 | tf_op jit(solution)/shard_map/pallas_call | solution.py:221
  53.4 0.0 collective-permute-done.14.refs_5_
  53.4 0.0 collective-permute-done.15.refs_6_
  53.4 0.0 collective-permute-done.16.refs_7_
  53.4 1.0 %shard_map.73.refs_2_ = bf16[128,8192]{1,0:T(8,128)(2,1)} custom-call(bf16[64,1024]{1,0:T(8,128)(2,1)S(1)} %collective-permute-done.2.refs_0_, bf16[64,1024]{1,0:T(8,128)(2,1)S(1)} %collective-permute-done.3.refs_1_, bf16[64,1024]{1,0:T(8,128)(2,1)S(1)} %collective-permute-done.11.refs_2_, ...), custom_call_target="tpu_custom_call", output_to_operand_aliasing={{}: (8, {})} | custom-call | bytes 2097152 | tf_op jit(solution)/shard_map/pallas_call | solution.py:221
  54.5 0.0 collective-permute-done.4.refs_0_
  54.5 0.0 collective-permute-done.5.refs_1_
  54.5 0.7 %shard_map.74 = bf16[128,8192]{1,0:T(8,128)(2,1)} custom-call(bf16[64,1024]{1,0:T(8,128)(2,1)S(1)} %collective-permute-done.4.refs_0_, bf16[64,1024]{1,0:T(8,128)(2,1)S(1)} %collective-permute-done.5.refs_1_, bf16[128,8192]{1,0:T(8,128)(2,1)} %shard_map.73.refs_2_), custom_call_target="tpu_custom_call", output_to_operand_aliasing={{}: (2, {})} | custom-call | bytes 524288 | tf_op jit(solution)/shard_map/pallas_call | solution.py:221
  (2 shorter events, 0.1 us)
Async XLA Ops:
  0.6 6.1 %copy-start = (bf16[256,128]{1,0:T(8,128)(2,1)S(1)}, bf16[256,128]{1,0:T(8,128)(2,1)}, u32[]{:S(2)}) copy-start(bf16[256,128]{1,0:T(8,128)(2,1)} %grad_out.1) | copy-start | bytes 196612
  0.6 6.1 %copy-start.1 = (bf16[256,64]{0,1:T(8,128)(2,1)S(1)}, bf16[256,64]{0,1:T(8,128)(2,1)}, u32[]{:S(2)}) copy-start(bf16[256,64]{0,1:T(8,128)(2,1)} %param.7) | copy-start | bytes 98308
  0.7 6.1 %copy-start.2 = (bf16[256,64]{0,1:T(8,128)(2,1)S(1)}, bf16[256,64]{0,1:T(8,128)(2,1)}, u32[]{:S(2)}) copy-start(bf16[256,64]{0,1:T(8,128)(2,1)} %param.8) | copy-start | bytes 98308
  6.2 4.7 %collective-permute-start = (bf16[8,64,1024]{2,1,0:T(8,128)(2,1)S(1)}, bf16[8,64,1024]{2,1,0:T(8,128)(2,1)S(1)}, u32[]{:S(2)}, u32[]{:S(2)}) collective-permute-start(bf16[8,64,1024]{2,1,0:T(8,128)(2,1)S(1)} %get-tuple-element.27), channel_id=1, source_target_pairs={{0,1},{1,0},{2,3},{3,2},{4,5},{5,4},{6,7},{7,6},{8,9},{9,8},{10,11... | collective-permute-start | bytes 3145736 | tf_op jit(solution)/shard_map/ppermute | solution.py:234
  30.9 6.9 %collective-permute-start.1 = (bf16[64,1024]{1,0:T(8,128)(2,1)S(1)}, bf16[64,1024]{1,0:T(8,128)(2,1)S(1)}, u32[]{:S(2)}, u32[]{:S(2)}) collective-permute-start(bf16[64,1024]{1,0:T(8,128)(2,1)S(1)} %reduce_sum.12), channel_id=1, source_target_pairs={{0,24},{1,25},{2,26},{3,27},{4,28},{5,29},{6,30},{7,31},{8,16},{9,... | collective-permute-start | bytes 393224 | tf_op jit(solution)/shard_map/ppermute | solution.py:234
  37.8 6.7 %collective-permute-start.10 = (bf16[64,1024]{1,0:T(8,128)(2,1)S(1)}, bf16[64,1024]{1,0:T(8,128)(2,1)S(1)}, u32[]{:S(2)}, u32[]{:S(2)}) collective-permute-start(bf16[64,1024]{1,0:T(8,128)(2,1)S(1)} %add_convert_fusion.1.refs_0_), channel_id=1, source_target_pairs={{0,2},{2,0},{4,6},{6,4},{8,10},{10,8},{12,14},{14,12},{1,3},{3,1},... | collective-permute-start | bytes 393224 | tf_op jit(solution)/shard_map/ppermute | solution.py:246
  38.1 7.7 %collective-permute-start.9 = (bf16[64,1024]{1,0:T(8,128)(2,1)S(1)}, bf16[64,1024]{1,0:T(8,128)(2,1)S(1)}, u32[]{:S(2)}, u32[]{:S(2)}) collective-permute-start(bf16[64,1024]{1,0:T(8,128)(2,1)S(1)} %add_convert_fusion.1.refs_0_), channel_id=1, source_target_pairs={{0,12},{2,14},{4,8},{6,10},{8,4},{10,6},{12,0},{14,2},{1,13},{3,15... | collective-permute-start | bytes 393224 | tf_op jit(solution)/shard_map/ppermute | solution.py:246
  38.1 9.3 %collective-permute-start.8 = (bf16[64,1024]{1,0:T(8,128)(2,1)S(1)}, bf16[64,1024]{1,0:T(8,128)(2,1)S(1)}, u32[]{:S(2)}, u32[]{:S(2)}) collective-permute-start(bf16[64,1024]{1,0:T(8,128)(2,1)S(1)} %add_convert_fusion.1.refs_0_), channel_id=1, source_target_pairs={{0,10},{2,8},{4,14},{6,12},{8,2},{10,0},{12,6},{14,4},{1,11},{3,9}... | collective-permute-start | bytes 393224 | tf_op jit(solution)/shard_map/ppermute | solution.py:246
  41.3 8.7 %collective-permute-start.7 = (bf16[64,1024]{1,0:T(8,128)(2,1)S(1)}, bf16[64,1024]{1,0:T(8,128)(2,1)S(1)}, u32[]{:S(2)}, u32[]{:S(2)}) collective-permute-start(bf16[64,1024]{1,0:T(8,128)(2,1)S(1)} %add_convert_fusion.1.refs_0_), channel_id=1, source_target_pairs={{0,6},{2,4},{4,2},{6,0},{8,14},{10,12},{12,10},{14,8},{1,7},{3,5},... | collective-permute-start | bytes 393224 | tf_op jit(solution)/shard_map/ppermute | solution.py:246
  42.5 7.5 %collective-permute-start.6 = (bf16[64,1024]{1,0:T(8,128)(2,1)S(1)}, bf16[64,1024]{1,0:T(8,128)(2,1)S(1)}, u32[]{:S(2)}, u32[]{:S(2)}) collective-permute-start(bf16[64,1024]{1,0:T(8,128)(2,1)S(1)} %add_convert_fusion.1.refs_0_), channel_id=1, source_target_pairs={{0,14},{2,12},{4,10},{6,8},{8,6},{10,4},{12,2},{14,0},{1,15},{3,13... | collective-permute-start | bytes 393224 | tf_op jit(solution)/shard_map/ppermute | solution.py:246
  44.5 6.1 %collective-permute-start.3 = (bf16[64,1024]{1,0:T(8,128)(2,1)S(1)}, bf16[64,1024]{1,0:T(8,128)(2,1)S(1)}, u32[]{:S(2)}, u32[]{:S(2)}) collective-permute-start(bf16[64,1024]{1,0:T(8,128)(2,1)S(1)} %add_convert_fusion.1.refs_0_), channel_id=1, source_target_pairs={{0,8},{2,10},{4,12},{6,14},{8,0},{10,2},{12,4},{14,6},{1,9},{3,11}... | collective-permute-start | bytes 393224 | tf_op jit(solution)/shard_map/ppermute | solution.py:246
  45.9 5.5 %collective-permute-start.2 = (bf16[64,1024]{1,0:T(8,128)(2,1)S(1)}, bf16[64,1024]{1,0:T(8,128)(2,1)S(1)}, u32[]{:S(2)}, u32[]{:S(2)}) collective-permute-start(bf16[64,1024]{1,0:T(8,128)(2,1)S(1)} %add_convert_fusion.1.refs_0_), channel_id=1, source_target_pairs={{0,4},{2,6},{4,0},{6,2},{8,12},{10,14},{12,8},{14,10},{1,5},{3,7},... | collective-permute-start | bytes 393224 | tf_op jit(solution)/shard_map/ppermute | solution.py:246
  50.1 1.4 %collective-permute-start.11 = (bf16[64,1024]{1,0:T(8,128)(2,1)S(1)}, bf16[64,1024]{1,0:T(8,128)(2,1)S(1)}, u32[]{:S(2)}, u32[]{:S(2)}) collective-permute-start(bf16[64,1024]{1,0:T(8,128)(2,1)S(1)} %add_convert_fusion.1.refs_0_), channel_id=1, source_target_pairs={{0,1},{1,0},{2,3},{3,2},{4,5},{5,4},{6,7},{7,6},{8,9},{9,8},{10,11... | collective-permute-start | bytes 393224 | tf_op jit(solution)/shard_map/ppermute | solution.py:234
  50.1 1.9 %collective-permute-start.12 = (bf16[64,1024]{1,0:T(8,128)(2,1)S(1)}, bf16[64,1024]{1,0:T(8,128)(2,1)S(1)}, u32[]{:S(2)}, u32[]{:S(2)}) collective-permute-start(bf16[64,1024]{1,0:T(8,128)(2,1)S(1)} %collective-permute-done.6.refs_1_), channel_id=1, source_target_pairs={{0,1},{1,0},{2,3},{3,2},{4,5},{5,4},{6,7},{7,6},{8,9},{9,8},{10,11... | collective-permute-start | bytes 393224 | tf_op jit(solution)/shard_map/ppermute | solution.py:234
  50.6 1.4 %collective-permute-start.13 = (bf16[64,1024]{1,0:T(8,128)(2,1)S(1)}, bf16[64,1024]{1,0:T(8,128)(2,1)S(1)}, u32[]{:S(2)}, u32[]{:S(2)}) collective-permute-start(bf16[64,1024]{1,0:T(8,128)(2,1)S(1)} %collective-permute-done.7.refs_2_), channel_id=1, source_target_pairs={{0,1},{1,0},{2,3},{3,2},{4,5},{5,4},{6,7},{7,6},{8,9},{9,8},{10,11... | collective-permute-start | bytes 393224 | tf_op jit(solution)/shard_map/ppermute | solution.py:234
  50.6 2.8 %collective-permute-start.14 = (bf16[64,1024]{1,0:T(8,128)(2,1)S(1)}, bf16[64,1024]{1,0:T(8,128)(2,1)S(1)}, u32[]{:S(2)}, u32[]{:S(2)}) collective-permute-start(bf16[64,1024]{1,0:T(8,128)(2,1)S(1)} %collective-permute-done.8.refs_3_), channel_id=1, source_target_pairs={{0,1},{1,0},{2,3},{3,2},{4,5},{5,4},{6,7},{7,6},{8,9},{9,8},{10,11... | collective-permute-start | bytes 393224 | tf_op jit(solution)/shard_map/ppermute | solution.py:234
  51.4 2.0 %collective-permute-start.15 = (bf16[64,1024]{1,0:T(8,128)(2,1)S(1)}, bf16[64,1024]{1,0:T(8,128)(2,1)S(1)}, u32[]{:S(2)}, u32[]{:S(2)}) collective-permute-start(bf16[64,1024]{1,0:T(8,128)(2,1)S(1)} %collective-permute-done.9.refs_4_), channel_id=1, source_target_pairs={{0,1},{1,0},{2,3},{3,2},{4,5},{5,4},{6,7},{7,6},{8,9},{9,8},{10,11... | collective-permute-start | bytes 393224 | tf_op jit(solution)/shard_map/ppermute | solution.py:234
  51.4 2.0 %collective-permute-start.16 = (bf16[64,1024]{1,0:T(8,128)(2,1)S(1)}, bf16[64,1024]{1,0:T(8,128)(2,1)S(1)}, u32[]{:S(2)}, u32[]{:S(2)}) collective-permute-start(bf16[64,1024]{1,0:T(8,128)(2,1)S(1)} %collective-permute-done.10.refs_5_), channel_id=1, source_target_pairs={{0,1},{1,0},{2,3},{3,2},{4,5},{5,4},{6,7},{7,6},{8,9},{9,8},{10,11... | collective-permute-start | bytes 393224 | tf_op jit(solution)/shard_map/ppermute | solution.py:234
  51.9 2.5 %collective-permute-start.4 = (bf16[64,1024]{1,0:T(8,128)(2,1)S(1)}, bf16[64,1024]{1,0:T(8,128)(2,1)S(1)}, u32[]{:S(2)}, u32[]{:S(2)}) collective-permute-start(bf16[64,1024]{1,0:T(8,128)(2,1)S(1)} %collective-permute-done.2.refs_0_), channel_id=1, source_target_pairs={{0,1},{1,0},{2,3},{3,2},{4,5},{5,4},{6,7},{7,6},{8,9},{9,8},{10,11... | collective-permute-start | bytes 393224 | tf_op jit(solution)/shard_map/ppermute | solution.py:234
  52.0 2.5 %collective-permute-start.5 = (bf16[64,1024]{1,0:T(8,128)(2,1)S(1)}, bf16[64,1024]{1,0:T(8,128)(2,1)S(1)}, u32[]{:S(2)}, u32[]{:S(2)}) collective-permute-start(bf16[64,1024]{1,0:T(8,128)(2,1)S(1)} %collective-permute-done.3.refs_1_), channel_id=1, source_target_pairs={{0,1},{1,0},{2,3},{3,2},{4,5},{5,4},{6,7},{7,6},{8,9},{9,8},{10,11... | collective-permute-start | bytes 393224 | tf_op jit(solution)/shard_map/ppermute | solution.py:234

commit v10 on v9

--- a/solution.py
+++ b/solution.py
@@ -8,7 +8,8 @@
 from jax.sharding import PartitionSpec as P
 
 LOADS = 4
-LAST = 2
+STORES = 8
+EARLY = (0, 4, 3, 5)
 VMEM_LIMIT = 40 * 1024 * 1024
 ANY = pl.BlockSpec(memory_space=pl.ANY)
 WHOLE = pl.BlockSpec(memory_space=pltpu.VMEM)
@@ -190,8 +191,8 @@
         in_specs=[WHOLE, WHOLE] + [ANY] * len(given),
         out_specs=ANY,
         scratch_shapes=[
-            pltpu.VMEM((LOADS, tokens, width // LOADS), jnp.bfloat16),
-            pltpu.SemaphoreType.DMA((LOADS,)),
+            pltpu.VMEM((STORES, tokens, width // STORES), jnp.bfloat16),
+            pltpu.SemaphoreType.DMA((STORES,)),
         ],
         input_output_aliases={2: 0} if given else {},
         compiler_params=pltpu.CompilerParams(vmem_limit_bytes=24 * 1024 * 1024),
@@ -244,16 +245,19 @@
     for distance in sorted(range(1, blocks), key=lambda distance: -distance.bit_count()):
         pairs = [(group[at], group[at ^ distance]) for group in groups for at in range(blocks)]
         pieces[distance] = lax.ppermute(total, "dp", pairs)
-    order = list(pieces)
-    cut = max(len(order) - LAST, 1)
-    result, turned = None, []
-    for part in filter(None, (order[:cut], order[cut:])):
-        held = lax.optimization_barrier([pieces[distance] for distance in part])
-        arriving = [swap(piece, 1, count) for piece in held]
-        plan = tuple((distance, 0) for distance in part) + tuple((distance, 1) for distance, _ in turned)
-        result = place(blocks, plan, held + [piece for _, piece in turned], result)
-        turned = list(zip(part, arriving))
-    return place(blocks, tuple((distance, 1) for distance, _ in turned), [piece for _, piece in turned], result)
+    early = [distance for distance in EARLY if distance < blocks]
+    late = [distance for distance in pieces if distance not in early]
+    result = place(blocks, tuple((distance, 0) for distance in early), [pieces[distance] for distance in early])
+    result, held = lax.optimization_barrier((result, [pieces[distance] for distance in early]))
+    pieces.update(zip(early, held))
+    turned = {distance: swap(pieces[distance], 1, count) for distance in early + late}
+    for own, other in ((late, early), ([], late)):
+        plan = tuple((distance, 0) for distance in own) + tuple((distance, 1) for distance in other)
+        if plan:
+            result = place(
+                blocks, plan, [pieces[distance] for distance in own] + [turned[distance] for distance in other], result
+            )
+    return result
 
 
 def per_device(count, hidden_in, query_weight, saved_keys, saved_values, grad_out):

time: 55.4 us -> 55.6 us (level)
  waiting for transfers between devices: 8.14 us -> 9.7 us
  starting transfers between devices: 13.9 us -> 12.5 us
    ppermute x7, waiting for transfers between devices: 3.94 us -> 5.48 us  [gather(): pieces[distance] = lax.ppermute(total, 'dp', pairs)]
    ppermute x7, starting transfers between devices: 8.63 us -> 7.62 us  [gather(): pieces[distance] = lax.ppermute(total, 'dp', pairs)]
where the time goes in v10:
time: 55.6 us; the launch traced here: 55.4 us
  blocking collectives  19.4 us (35%)
  starting transfers between devices  12.5 us (22%)
  Pallas kernels  12.4 us (22%)
  waiting for transfers between devices  9.7 us (17%)
  between operations  0.79 us (1%)
  other arithmetic  0.62 us (1%)
    all_to_all x1, blocking collectives, per_device(): parts = lax.all_to_all(chip, 'dp', 0, 0, axis_index_groups=groups)  19.4 us
    ppermute x7, starting transfers between devices, gather(): pieces[distance] = lax.ppermute(total, 'dp', pairs)  7.62 us
    pallas_call x1, Pallas kernels, query_and_other(): pl.pallas_call(query_kernel, out_shape=(jax.ShapeDtypeStruct((blocks, row...  5.58 us
    ppermute x7, waiting for transfers between devices, gather(): pieces[distance] = lax.ppermute(total, 'dp', pairs)  5.48 us
    ppermute x10, starting transfers between devices, swap(): return lax.ppermute(array, 'dp', [(i, i ^ step) for i in range(count)])  4.84 us
    ppermute x10, waiting for transfers between devices, swap(): return lax.ppermute(array, 'dp', [(i, i ^ step) for i in range(count)])  4.22 us
    pallas_call x3, Pallas kernels, place(): pl.pallas_call(functools.partial(place_kernel, blocks, plan), out_shape=j...  2.68 us
    pallas_call x2, Pallas kernels, hidden_part(): pl.pallas_call(functools.partial(hidden_kernel, turn), out_shape=jax.Shap...  2.44 us
  transfers between devices with their start and end apart: 17, of which 5 were waited for; matrix products, arithmetic and copies ran while one was open for 0% of the time, Pallas kernels for 11%

profile of v10, /device:TPU:0, one launch (start us, length us, event | category | flops | bytes accessed | tf_op | source)
XLA Modules:
  0.0 55.4 jit_solution(13280895668243225711)
XLA Ops:
  0.6 0.0 copy-start
  0.6 0.0 copy-start.1
  0.7 0.0 copy-start.2
  0.7 5.6 %shard_map.68 = (bf16[8,64,1024]{2,1,0:T(8,128)(2,1)S(1)}, bf16[256,8192]{1,0:T(8,128)(2,1)S(1)}, bf16[128,8192]{1,0:T(8,128)(2,1)S(1)}, bf16[256,128]{1,0:T(8,128)(2,1)S(1)}, bf16[256,64]{1,0:T(8,128)(2,1)S(1)}) custom-call(bf16[256,8192]{1,0:T(8,128)(2,1)} %hidden_hbm.1, bf16[128,8192]{1,0:T(8,128)(2,1)} %weight_hbm.1, bf16[64,256]{1,0:T(8,128)(2,1)} %bitcast.2, ...), custom_call_target="tpu_custom_call" | custom-call | flops 805306368 | bytes 6291456 | tf_op jit(solution)/shard_map/pallas_call | solution.py:110
  6.2 0.5 collective-permute-start
  6.8 0.0 copy-done
  6.8 0.0 copy-done.1
  6.8 0.0 copy-done.2
  6.8 1.7 %shard_map.69 = (bf16[8,64,1024]{2,1,0:T(8,128)(2,1)S(1)}, bf16[256,128]{1,0:T(8,128)(2,1)S(1)}) custom-call(bf16[256,8192]{1,0:T(8,128)(2,1)S(1)} %get-tuple-element.20.hidden, bf16[256,128]{1,0:T(8,128)(2,1)S(1)} %get-tuple-element.21.query, bf16[256,64]{1,0:T(8,128)(2,1)S(1)} %get-tuple-element.22.others, bf16[64,256]{1,0:T(8,128)(2,1)S(1)} %bitcast.3, ...), custom_call_target="tpu_custom_call" | custom-call | flops 268435456 | bytes 4194304 | tf_op jit(solution)/shard_map/pallas_call | solution.py:152
  8.5 2.4 %shard_map.70.refs_0_ = bf16[256,8192]{1,0:T(8,128)(2,1)} custom-call(bf16[256,128]{1,0:T(8,128)(2,1)S(1)} %get-tuple-element.25.grad_query, bf16[128,8192]{1,0:T(8,128)(2,1)S(1)} %get-tuple-element.26.weight), custom_call_target="tpu_custom_call" | custom-call | flops 536870912 | bytes 6291456 | tf_op jit(solution)/shard_map/pallas_call | solution.py:188
  10.9 0.0 collective-permute-done
  10.9 0.4 add_convert_fusion
  11.3 19.4 %all_to_all.5 = bf16[8,64,1024]{2,1,0:T(8,128)(2,1)S(1)} all-to-all(bf16[8,64,1024]{2,1,0:T(8,128)(2,1)S(1)} %add_convert_fusion), channel_id=1, replica_groups={{0,2,4,6,8,10,12,14},{1,3,5,7,9,11,13,15},{24,26,28,30,16,18,20,22},{25..., dimensions={0} | all-to-all | bytes 2097152 | tf_op jit(solution)/shard_map/all_to_all | solution.py:284
  30.7 0.2 reduce_sum.12
  30.9 2.7 %collective-permute-start.1 = (bf16[64,1024]{1,0:T(8,128)(2,1)S(1)}, bf16[64,1024]{1,0:T(8,128)(2,1)S(1)}, u32[]{:S(2)}, u32[]{:S(2)}) collective-permute-start(bf16[64,1024]{1,0:T(8,128)(2,1)S(1)} %reduce_sum.12), channel_id=1, source_target_pairs={{0,24},{1,25},{2,26},{3,27},{4,28},{5,29},{6,30},{7,31},{8,16},{9,... | collective-permute-start | bytes 393224 | tf_op jit(solution)/shard_map/ppermute | solution.py:235
  33.5 0.1 shard_map.71
  33.6 4.2 %collective-permute-done.1 = bf16[64,1024]{1,0:T(8,128)(2,1)S(1)} collective-permute-done((bf16[64,1024]{1,0:T(8,128)(2,1)S(1)}, bf16[64,1024]{1,0:T(8,128)(2,1)S(1)}, u32[]{:S(2)}, u32[]{:S(2)}) %collective-permute-start.1) | collective-permute-done | bytes 131104 | tf_op jit(solution)/shard_map/ppermute | solution.py:235
  37.8 0.7 %collective-permute-start.12 = (bf16[64,1024]{1,0:T(8,128)(2,1)S(1)}, bf16[64,1024]{1,0:T(8,128)(2,1)S(1)}, u32[]{:S(2)}, u32[]{:S(2)}) collective-permute-start(bf16[64,1024]{1,0:T(8,128)(2,1)S(1)} %add_convert_fusion.1.refs_0_), channel_id=1, source_target_pairs={{0,10},{2,8},{4,14},{6,12},{8,2},{10,0},{12,6},{14,4},{1,11},{3,9}... | collective-permute-start | bytes 393224 | tf_op jit(solution)/shard_map/ppermute | solution.py:247
  38.5 0.4 collective-permute-start.11
  38.9 2.5 %collective-permute-start.10 = (bf16[64,1024]{1,0:T(8,128)(2,1)S(1)}, bf16[64,1024]{1,0:T(8,128)(2,1)S(1)}, u32[]{:S(2)}, u32[]{:S(2)}) collective-permute-start(bf16[64,1024]{1,0:T(8,128)(2,1)S(1)} %add_convert_fusion.1.refs_0_), channel_id=1, source_target_pairs={{0,8},{2,10},{4,12},{6,14},{8,0},{10,2},{12,4},{14,6},{1,9},{3,11}... | collective-permute-start | bytes 393224 | tf_op jit(solution)/shard_map/ppermute | solution.py:247
  41.4 1.5 %collective-permute-start.8 = (bf16[64,1024]{1,0:T(8,128)(2,1)S(1)}, bf16[64,1024]{1,0:T(8,128)(2,1)S(1)}, u32[]{:S(2)}, u32[]{:S(2)}) collective-permute-start(bf16[64,1024]{1,0:T(8,128)(2,1)S(1)} %add_convert_fusion.1.refs_0_), channel_id=1, source_target_pairs={{0,4},{2,6},{4,0},{6,2},{8,12},{10,14},{12,8},{14,10},{1,5},{3,7},... | collective-permute-start | bytes 393224 | tf_op jit(solution)/shard_map/ppermute | solution.py:247
  42.9 0.3 collective-permute-start.6
  43.1 1.9 %collective-permute-done.12.refs_3_ = bf16[64,1024]{1,0:T(8,128)(2,1)S(1)} collective-permute-done((bf16[64,1024]{1,0:T(8,128)(2,1)S(1)}, bf16[64,1024]{1,0:T(8,128)(2,1)S(1)}, u32[]{:S(2)}, u32[]{:S(2)}) %collective-permute-start.12) | collective-permute-done | bytes 131104 | tf_op jit(solution)/shard_map/ppermute | solution.py:247
  45.0 0.0 collective-permute-start.4
  45.0 0.6 %collective-permute-done.11.refs_2_ = bf16[64,1024]{1,0:T(8,128)(2,1)S(1)} collective-permute-done((bf16[64,1024]{1,0:T(8,128)(2,1)S(1)}, bf16[64,1024]{1,0:T(8,128)(2,1)S(1)}, u32[]{:S(2)}, u32[]{:S(2)}) %collective-permute-start.11) | collective-permute-done | bytes 131104 | tf_op jit(solution)/shard_map/ppermute | solution.py:247
  45.7 2.3 %collective-permute-start.2 = (bf16[64,1024]{1,0:T(8,128)(2,1)S(1)}, bf16[64,1024]{1,0:T(8,128)(2,1)S(1)}, u32[]{:S(2)}, u32[]{:S(2)}) collective-permute-start(bf16[64,1024]{1,0:T(8,128)(2,1)S(1)} %add_convert_fusion.1.refs_0_), channel_id=1, source_target_pairs={{0,14},{2,12},{4,10},{6,8},{8,6},{10,4},{12,2},{14,0},{1,15},{3,13... | collective-permute-start | bytes 393224 | tf_op jit(solution)/shard_map/ppermute | solution.py:247
  48.0 0.0 collective-permute-done.10.refs_1_
  48.0 0.8 %shard_map.72.refs_8_ = bf16[128,8192]{1,0:T(8,128)(2,1)} custom-call(bf16[64,1024]{1,0:T(8,128)(2,1)S(1)} %add_convert_fusion.1.refs_0_, bf16[64,1024]{1,0:T(8,128)(2,1)S(1)} %collective-permute-done.10.refs_1_, bf16[64,1024]{1,0:T(8,128)(2,1)S(1)} %collective-permute-done.11.refs_2_, bf16[64,1024]{1,0:T(8,128)(2,1)S(1)} %collective-permute-done.12.refs_3_), custom_call_target="tpu_custom_call" | custom-call | bytes 1048576 | tf_op jit(solution)/shard_map/pallas_call | solution.py:222
  48.9 0.1 collective-permute-start.13
  48.9 0.0 collective-permute-done.8.refs_3_
  48.9 0.5 collective-permute-start.14
  49.4 0.0 collective-permute-done.6.refs_2_
  49.4 0.1 collective-permute-start.15
  49.5 1.4 %collective-permute-done.4.refs_1_ = bf16[64,1024]{1,0:T(8,128)(2,1)S(1)} collective-permute-done((bf16[64,1024]{1,0:T(8,128)(2,1)S(1)}, bf16[64,1024]{1,0:T(8,128)(2,1)S(1)}, u32[]{:S(2)}, u32[]{:S(2)}) %collective-permute-start.4) | collective-permute-done | bytes 131104 | tf_op jit(solution)/shard_map/ppermute | solution.py:247
  50.9 0.0 collective-permute-start.16
  50.9 1.5 %collective-permute-done.2.refs_0_ = bf16[64,1024]{1,0:T(8,128)(2,1)S(1)} collective-permute-done((bf16[64,1024]{1,0:T(8,128)(2,1)S(1)}, bf16[64,1024]{1,0:T(8,128)(2,1)S(1)}, u32[]{:S(2)}, u32[]{:S(2)}) %collective-permute-start.2) | collective-permute-done | bytes 131104 | tf_op jit(solution)/shard_map/ppermute | solution.py:247
  52.4 0.0 collective-permute-start.9
  52.4 0.0 collective-permute-done.13.refs_4_
  52.5 0.5 collective-permute-start.7
  53.0 0.0 collective-permute-done.14.refs_5_
  53.0 0.1 collective-permute-start.5
  53.0 0.0 collective-permute-done.15.refs_6_
  53.0 0.4 collective-permute-start.3
  53.5 0.0 collective-permute-done.16.refs_7_
  53.5 1.0 %shard_map.73.refs_4_ = bf16[128,8192]{1,0:T(8,128)(2,1)} custom-call(bf16[64,1024]{1,0:T(8,128)(2,1)S(1)} %collective-permute-done.2.refs_0_, bf16[64,1024]{1,0:T(8,128)(2,1)S(1)} %collective-permute-done.4.refs_1_, bf16[64,1024]{1,0:T(8,128)(2,1)S(1)} %collective-permute-done.6.refs_2_, ...), custom_call_target="tpu_custom_call", output_to_operand_aliasing={{}: (8, {})} | custom-call | bytes 2097152 | tf_op jit(solution)/shard_map/pallas_call | solution.py:222
  54.5 0.0 collective-permute-done.9.refs_3_
  54.5 0.0 collective-permute-done.7.refs_2_
  54.5 0.0 collective-permute-done.5.refs_1_
  54.5 0.0 collective-permute-done.3.refs_0_
  54.6 0.8 %shard_map.74 = bf16[128,8192]{1,0:T(8,128)(2,1)} custom-call(bf16[64,1024]{1,0:T(8,128)(2,1)S(1)} %collective-permute-done.3.refs_0_, bf16[64,1024]{1,0:T(8,128)(2,1)S(1)} %collective-permute-done.5.refs_1_, bf16[64,1024]{1,0:T(8,128)(2,1)S(1)} %collective-permute-done.7.refs_2_, ...), custom_call_target="tpu_custom_call", output_to_operand_aliasing={{}: (4, {})} | custom-call | bytes 1048576 | tf_op jit(solution)/shard_map/pallas_call | solution.py:222
  (1 shorter events, 0.0 us)
Async XLA Ops:
  0.6 6.1 %copy-start = (bf16[256,128]{1,0:T(8,128)(2,1)S(1)}, bf16[256,128]{1,0:T(8,128)(2,1)}, u32[]{:S(2)}) copy-start(bf16[256,128]{1,0:T(8,128)(2,1)} %grad_out.1) | copy-start | bytes 196612
  0.6 6.1 %copy-start.1 = (bf16[256,64]{0,1:T(8,128)(2,1)S(1)}, bf16[256,64]{0,1:T(8,128)(2,1)}, u32[]{:S(2)}) copy-start(bf16[256,64]{0,1:T(8,128)(2,1)} %param.7) | copy-start | bytes 98308
  0.7 6.1 %copy-start.2 = (bf16[256,64]{0,1:T(8,128)(2,1)S(1)}, bf16[256,64]{0,1:T(8,128)(2,1)}, u32[]{:S(2)}) copy-start(bf16[256,64]{0,1:T(8,128)(2,1)} %param.8) | copy-start | bytes 98308
  6.2 4.6 %collective-permute-start = (bf16[8,64,1024]{2,1,0:T(8,128)(2,1)S(1)}, bf16[8,64,1024]{2,1,0:T(8,128)(2,1)S(1)}, u32[]{:S(2)}, u32[]{:S(2)}) collective-permute-start(bf16[8,64,1024]{2,1,0:T(8,128)(2,1)S(1)} %get-tuple-element.24), channel_id=1, source_target_pairs={{0,1},{1,0},{2,3},{3,2},{4,5},{5,4},{6,7},{7,6},{8,9},{9,8},{10,11... | collective-permute-start | bytes 3145736 | tf_op jit(solution)/shard_map/ppermute | solution.py:235
  30.9 6.9 %collective-permute-start.1 = (bf16[64,1024]{1,0:T(8,128)(2,1)S(1)}, bf16[64,1024]{1,0:T(8,128)(2,1)S(1)}, u32[]{:S(2)}, u32[]{:S(2)}) collective-permute-start(bf16[64,1024]{1,0:T(8,128)(2,1)S(1)} %reduce_sum.12), channel_id=1, source_target_pairs={{0,24},{1,25},{2,26},{3,27},{4,28},{5,29},{6,30},{7,31},{8,16},{9,... | collective-permute-start | bytes 393224 | tf_op jit(solution)/shard_map/ppermute | solution.py:235
  37.8 7.2 %collective-permute-start.12 = (bf16[64,1024]{1,0:T(8,128)(2,1)S(1)}, bf16[64,1024]{1,0:T(8,128)(2,1)S(1)}, u32[]{:S(2)}, u32[]{:S(2)}) collective-permute-start(bf16[64,1024]{1,0:T(8,128)(2,1)S(1)} %add_convert_fusion.1.refs_0_), channel_id=1, source_target_pairs={{0,10},{2,8},{4,14},{6,12},{8,2},{10,0},{12,6},{14,4},{1,11},{3,9}... | collective-permute-start | bytes 393224 | tf_op jit(solution)/shard_map/ppermute | solution.py:247
  38.5 7.2 %collective-permute-start.11 = (bf16[64,1024]{1,0:T(8,128)(2,1)S(1)}, bf16[64,1024]{1,0:T(8,128)(2,1)S(1)}, u32[]{:S(2)}, u32[]{:S(2)}) collective-permute-start(bf16[64,1024]{1,0:T(8,128)(2,1)S(1)} %add_convert_fusion.1.refs_0_), channel_id=1, source_target_pairs={{0,6},{2,4},{4,2},{6,0},{8,14},{10,12},{12,10},{14,8},{1,7},{3,5},... | collective-permute-start | bytes 393224 | tf_op jit(solution)/shard_map/ppermute | solution.py:247
  38.9 9.1 %collective-permute-start.10 = (bf16[64,1024]{1,0:T(8,128)(2,1)S(1)}, bf16[64,1024]{1,0:T(8,128)(2,1)S(1)}, u32[]{:S(2)}, u32[]{:S(2)}) collective-permute-start(bf16[64,1024]{1,0:T(8,128)(2,1)S(1)} %add_convert_fusion.1.refs_0_), channel_id=1, source_target_pairs={{0,8},{2,10},{4,12},{6,14},{8,0},{10,2},{12,4},{14,6},{1,9},{3,11}... | collective-permute-start | bytes 393224 | tf_op jit(solution)/shard_map/ppermute | solution.py:247
  41.4 7.6 %collective-permute-start.8 = (bf16[64,1024]{1,0:T(8,128)(2,1)S(1)}, bf16[64,1024]{1,0:T(8,128)(2,1)S(1)}, u32[]{:S(2)}, u32[]{:S(2)}) collective-permute-start(bf16[64,1024]{1,0:T(8,128)(2,1)S(1)} %add_convert_fusion.1.refs_0_), channel_id=1, source_target_pairs={{0,4},{2,6},{4,0},{6,2},{8,12},{10,14},{12,8},{14,10},{1,5},{3,7},... | collective-permute-start | bytes 393224 | tf_op jit(solution)/shard_map/ppermute | solution.py:247
  42.9 6.6 %collective-permute-start.6 = (bf16[64,1024]{1,0:T(8,128)(2,1)S(1)}, bf16[64,1024]{1,0:T(8,128)(2,1)S(1)}, u32[]{:S(2)}, u32[]{:S(2)}) collective-permute-start(bf16[64,1024]{1,0:T(8,128)(2,1)S(1)} %add_convert_fusion.1.refs_0_), channel_id=1, source_target_pairs={{0,2},{2,0},{4,6},{6,4},{8,10},{10,8},{12,14},{14,12},{1,3},{3,1},... | collective-permute-start | bytes 393224 | tf_op jit(solution)/shard_map/ppermute | solution.py:247
  45.0 5.9 %collective-permute-start.4 = (bf16[64,1024]{1,0:T(8,128)(2,1)S(1)}, bf16[64,1024]{1,0:T(8,128)(2,1)S(1)}, u32[]{:S(2)}, u32[]{:S(2)}) collective-permute-start(bf16[64,1024]{1,0:T(8,128)(2,1)S(1)} %add_convert_fusion.1.refs_0_), channel_id=1, source_target_pairs={{0,12},{2,14},{4,8},{6,10},{8,4},{10,6},{12,0},{14,2},{1,13},{3,15... | collective-permute-start | bytes 393224 | tf_op jit(solution)/shard_map/ppermute | solution.py:247
  45.7 6.8 %collective-permute-start.2 = (bf16[64,1024]{1,0:T(8,128)(2,1)S(1)}, bf16[64,1024]{1,0:T(8,128)(2,1)S(1)}, u32[]{:S(2)}, u32[]{:S(2)}) collective-permute-start(bf16[64,1024]{1,0:T(8,128)(2,1)S(1)} %add_convert_fusion.1.refs_0_), channel_id=1, source_target_pairs={{0,14},{2,12},{4,10},{6,8},{8,6},{10,4},{12,2},{14,0},{1,15},{3,13... | collective-permute-start | bytes 393224 | tf_op jit(solution)/shard_map/ppermute | solution.py:247
  48.9 3.6 %collective-permute-start.13 = (bf16[64,1024]{1,0:T(8,128)(2,1)S(1)}, bf16[64,1024]{1,0:T(8,128)(2,1)S(1)}, u32[]{:S(2)}, u32[]{:S(2)}) collective-permute-start(bf16[64,1024]{1,0:T(8,128)(2,1)S(1)} %add_convert_fusion.1.refs_0_), channel_id=1, source_target_pairs={{0,1},{1,0},{2,3},{3,2},{4,5},{5,4},{6,7},{7,6},{8,9},{9,8},{10,11... | collective-permute-start | bytes 393224 | tf_op jit(solution)/shard_map/ppermute | solution.py:235
  48.9 4.0 %collective-permute-start.14 = (bf16[64,1024]{1,0:T(8,128)(2,1)S(1)}, bf16[64,1024]{1,0:T(8,128)(2,1)S(1)}, u32[]{:S(2)}, u32[]{:S(2)}) collective-permute-start(bf16[64,1024]{1,0:T(8,128)(2,1)S(1)} %collective-permute-done.10.refs_1_), channel_id=1, source_target_pairs={{0,1},{1,0},{2,3},{3,2},{4,5},{5,4},{6,7},{7,6},{8,9},{9,8},{10,11... | collective-permute-start | bytes 393224 | tf_op jit(solution)/shard_map/ppermute | solution.py:235
  49.4 3.6 %collective-permute-start.15 = (bf16[64,1024]{1,0:T(8,128)(2,1)S(1)}, bf16[64,1024]{1,0:T(8,128)(2,1)S(1)}, u32[]{:S(2)}, u32[]{:S(2)}) collective-permute-start(bf16[64,1024]{1,0:T(8,128)(2,1)S(1)} %collective-permute-done.11.refs_2_), channel_id=1, source_target_pairs={{0,1},{1,0},{2,3},{3,2},{4,5},{5,4},{6,7},{7,6},{8,9},{9,8},{10,11... | collective-permute-start | bytes 393224 | tf_op jit(solution)/shard_map/ppermute | solution.py:235
  50.9 2.6 %collective-permute-start.16 = (bf16[64,1024]{1,0:T(8,128)(2,1)S(1)}, bf16[64,1024]{1,0:T(8,128)(2,1)S(1)}, u32[]{:S(2)}, u32[]{:S(2)}) collective-permute-start(bf16[64,1024]{1,0:T(8,128)(2,1)S(1)} %collective-permute-done.12.refs_3_), channel_id=1, source_target_pairs={{0,1},{1,0},{2,3},{3,2},{4,5},{5,4},{6,7},{7,6},{8,9},{9,8},{10,11... | collective-permute-start | bytes 393224 | tf_op jit(solution)/shard_map/ppermute | solution.py:235
  52.4 2.1 %collective-permute-start.9 = (bf16[64,1024]{1,0:T(8,128)(2,1)S(1)}, bf16[64,1024]{1,0:T(8,128)(2,1)S(1)}, u32[]{:S(2)}, u32[]{:S(2)}) collective-permute-start(bf16[64,1024]{1,0:T(8,128)(2,1)S(1)} %collective-permute-done.8.refs_3_), channel_id=1, source_target_pairs={{0,1},{1,0},{2,3},{3,2},{4,5},{5,4},{6,7},{7,6},{8,9},{9,8},{10,11... | collective-permute-start | bytes 393224 | tf_op jit(solution)/shard_map/ppermute | solution.py:235
  52.5 2.1 %collective-permute-start.7 = (bf16[64,1024]{1,0:T(8,128)(2,1)S(1)}, bf16[64,1024]{1,0:T(8,128)(2,1)S(1)}, u32[]{:S(2)}, u32[]{:S(2)}) collective-permute-start(bf16[64,1024]{1,0:T(8,128)(2,1)S(1)} %collective-permute-done.6.refs_2_), channel_id=1, source_target_pairs={{0,1},{1,0},{2,3},{3,2},{4,5},{5,4},{6,7},{7,6},{8,9},{9,8},{10,11... | collective-permute-start | bytes 393224 | tf_op jit(solution)/shard_map/ppermute | solution.py:235
  53.0 1.6 %collective-permute-start.5 = (bf16[64,1024]{1,0:T(8,128)(2,1)S(1)}, bf16[64,1024]{1,0:T(8,128)(2,1)S(1)}, u32[]{:S(2)}, u32[]{:S(2)}) collective-permute-start(bf16[64,1024]{1,0:T(8,128)(2,1)S(1)} %collective-permute-done.4.refs_1_), channel_id=1, source_target_pairs={{0,1},{1,0},{2,3},{3,2},{4,5},{5,4},{6,7},{7,6},{8,9},{9,8},{10,11... | collective-permute-start | bytes 393224 | tf_op jit(solution)/shard_map/ppermute | solution.py:235
  53.0 1.5 %collective-permute-start.3 = (bf16[64,1024]{1,0:T(8,128)(2,1)S(1)}, bf16[64,1024]{1,0:T(8,128)(2,1)S(1)}, u32[]{:S(2)}, u32[]{:S(2)}) collective-permute-start(bf16[64,1024]{1,0:T(8,128)(2,1)S(1)} %collective-permute-done.2.refs_0_), channel_id=1, source_target_pairs={{0,1},{1,0},{2,3},{3,2},{4,5},{5,4},{6,7},{7,6},{8,9},{9,8},{10,11... | collective-permute-start | bytes 393224 | tf_op jit(solution)/shard_map/ppermute | solution.py:235

commit v11 on v8

--- a/solution.py
+++ b/solution.py
@@ -8,6 +8,7 @@
 from jax.sharding import PartitionSpec as P
 
 LOADS = 4
+HIDDEN_PIECES = 4
 VMEM_LIMIT = 40 * 1024 * 1024
 ANY = pl.BlockSpec(memory_space=pl.ANY)
 WHOLE = pl.BlockSpec(memory_space=pltpu.VMEM)
@@ -157,42 +158,50 @@
     )(hidden, query, others, keys, values, grad_out)
 
 
-def hidden_kernel(turn, grad_query, weight, *refs):
-    out_hbm, found, sem = refs[-3:]
+def hidden_kernel(turn, grad_query, weight_hbm, *refs):
+    out_hbm, weight, found, load_sem, store_sem = refs[-5:]
 
     @pl.when(own_core() == turn)
     def _():
-        pieces, _, step = found.shape
+        width = weight.shape[1]
+        loads = []
+        for at in range(HIDDEN_PIECES):
+            columns = pl.ds(at * (width // HIDDEN_PIECES), width // HIDDEN_PIECES)
+            loads.append(pltpu.make_async_copy(weight_hbm.at[:, columns], weight.at[:, columns], load_sem.at[at]))
+            loads[-1].start()
         grads = grad_query[...]
         sent = []
-        for piece in range(pieces):
-            columns = pl.ds(piece * step, step)
-            found[piece] = dot(grads, weight[:, columns]).astype(found.dtype)
-            sent.append(pltpu.make_async_copy(found.at[piece], out_hbm.at[:, columns], sem.at[piece]))
+        for at in range(HIDDEN_PIECES):
+            columns = pl.ds(at * (width // HIDDEN_PIECES), width // HIDDEN_PIECES)
+            loads[at].wait()
+            found[at] = dot(grads, weight[:, columns]).astype(found.dtype)
+            sent.append(pltpu.make_async_copy(found.at[at], out_hbm.at[:, columns], store_sem.at[at]))
             sent[-1].start()
         for copy in sent:
             copy.wait()
 
 
-def hidden_part(turn, grad_query, weight, before=None):
+def hidden_part(turn, grad_query, query_weight, before=None):
     tokens, rows = grad_query.shape
-    width = weight.shape[1]
+    width = query_weight.shape[1]
     given = () if before is None else (before,)
     return pl.pallas_call(
         functools.partial(hidden_kernel, turn),
         out_shape=jax.ShapeDtypeStruct((tokens, width), jnp.bfloat16),
-        in_specs=[WHOLE, WHOLE] + [ANY] * len(given),
+        in_specs=[WHOLE, ANY] + [ANY] * len(given),
         out_specs=ANY,
         scratch_shapes=[
-            pltpu.VMEM((LOADS, tokens, width // LOADS), jnp.bfloat16),
-            pltpu.SemaphoreType.DMA((LOADS,)),
+            pltpu.VMEM((rows, width), jnp.bfloat16),
+            pltpu.VMEM((HIDDEN_PIECES, tokens, width // HIDDEN_PIECES), jnp.bfloat16),
+            pltpu.SemaphoreType.DMA((HIDDEN_PIECES,)),
+            pltpu.SemaphoreType.DMA((HIDDEN_PIECES,)),
         ],
         input_output_aliases={2: 0} if given else {},
         compiler_params=pltpu.CompilerParams(vmem_limit_bytes=24 * 1024 * 1024),
         cost_estimate=pl.CostEstimate(
             flops=2 * tokens * width * rows, bytes_accessed=2 * width * (tokens + rows), transcendentals=0
         ),
-    )(grad_query, weight, *given)
+    )(grad_query, pltpu.with_memory_space_constraint(query_weight, pltpu.HBM), *given)
 
 
 def place_kernel(turned, piece_hbm, *refs):
@@ -236,7 +245,7 @@
     wide = min(3, bits - 1)
     blocks = 1 << wide
     groups = [
-        [high << (wide + 1) | (place ^ (high & 1) * (blocks >> 1)) << 1 | core for place in range(blocks)]
+        [high << (wide + 1) | (place ^ (high & 1) * (blocks >> 1)) << 1 | core for place in reversed(range(blocks))]
         for high in range(count >> (wide + 1))
         for core in range(2)
     ]
@@ -250,12 +259,12 @@
     arriving = swap(other, 1, count)
     own, grad_query = own_part(blocks, hidden, query, grads, keys, values, grad_out)
     chip = add(own, arriving)
-    input_terms = hidden_part(0, grad_query, weight)
+    input_terms = hidden_part(0, grad_query, query_weight)
     chip, input_terms = lax.optimization_barrier((chip, input_terms))
     parts = lax.all_to_all(chip, "dp", 0, 0, axis_index_groups=groups)
     total = jnp.sum(parts.astype(jnp.float32), axis=0).astype(jnp.bfloat16)
     input_terms, total = lax.optimization_barrier((input_terms, total))
-    input_terms = hidden_part(1, grad_query, weight, input_terms)
+    input_terms = hidden_part(1, grad_query, query_weight, input_terms)
     for bit in range(wide + 1, bits):
         arriving = swap(total, 3 << wide if bit == wide + 1 else 1 << bit, count)
         if bit == wide + 1:

time: 55.5 us -> 54 us (0.973)
  blocking collectives: 33.1 us -> 30.1 us
  Pallas kernels: 11.8 us -> 13.2 us
    all_to_all x1, blocking collectives: 19.3 us -> 16.7 us  [per_device(): parts = lax.all_to_all(chip, 'dp', 0, 0, axis_index_groups=groups)]
    pallas_call x2, Pallas kernels: 2.51 us -> 3.84 us  [hidden_part(): pl.pallas_call(functools.partial(hidden_kernel, turn), out_shape=jax.Shap...]
  transfers between devices with their start and end apart: 3 -> 3, of which waited for: 2 -> 2; matrix products, arithmetic and copies ran while one was open for 0% -> 0% of each run, Pallas kernels for 9% -> 12%
where the time goes in v11:
time: 54 us; the launch traced here: 53.8 us
  blocking collectives  30.1 us (56%)
  Pallas kernels  13.2 us (24%)
  waiting for transfers between devices  5.94 us (11%)
  starting transfers between devices  3.06 us (6%)
  between operations  0.73 us (1%)
  other arithmetic  0.62 us (1%)
    all_to_all x1, blocking collectives, per_device(): parts = lax.all_to_all(chip, 'dp', 0, 0, axis_index_groups=groups)  16.7 us
    all_to_all x1, blocking collectives, per_device(): gathered = lax.all_to_all(copies, 'dp', 0, 0, axis_index_groups=groups)  13.4 us
    ppermute x3, waiting for transfers between devices, swap(): return lax.ppermute(array, 'dp', [(i, i ^ step) for i in range(count)])  5.94 us
    pallas_call x1, Pallas kernels, query_and_other(): pl.pallas_call(query_kernel, out_shape=(jax.ShapeDtypeStruct((blocks, row...  5.57 us
    pallas_call x2, Pallas kernels, hidden_part(): pl.pallas_call(functools.partial(hidden_kernel, turn), out_shape=jax.Shap...  3.84 us
    ppermute x3, starting transfers between devices, swap(): return lax.ppermute(array, 'dp', [(i, i ^ step) for i in range(count)])  3.06 us
    pallas_call x2, Pallas kernels, place(): pl.pallas_call(functools.partial(place_kernel, turned), out_shape=jax.Sha...  2.05 us
    pallas_call x1, Pallas kernels, own_part(): pl.pallas_call(own_kernel, out_shape=(jax.ShapeDtypeStruct((blocks, rows...  1.72 us
  transfers between devices with their start and end apart: 3, of which 2 were waited for; matrix products, arithmetic and copies ran while one was open for 0% of the time, Pallas kernels for 12%

profile of v11, /device:TPU:0, one launch (start us, length us, event | category | flops | bytes accessed | tf_op | source)
XLA Modules:
  0.0 53.8 jit_solution(17579229730639373042)
XLA Ops:
  0.6 0.0 copy-start
  0.6 0.0 copy-start.1
  0.7 0.0 copy-start.2
  0.7 5.6 %shard_map.68 = (bf16[8,64,1024]{2,1,0:T(8,128)(2,1)S(1)}, bf16[256,8192]{1,0:T(8,128)(2,1)S(1)}, bf16[128,8192]{1,0:T(8,128)(2,1)}, bf16[256,128]{1,0:T(8,128)(2,1)S(1)}, bf16[256,64]{1,0:T(8,128)(2,1)S(1)}) custom-call(bf16[256,8192]{1,0:T(8,128)(2,1)} %hidden_hbm.1, bf16[128,8192]{1,0:T(8,128)(2,1)} %weight_hbm.5, bf16[64,256]{1,0:T(8,128)(2,1)} %bitcast.2, ...), custom_call_target="tpu_custom_call" | custom-call | flops 805306368 | bytes 6291456 | tf_op jit(solution)/shard_map/pallas_call | solution.py:104
  6.2 0.5 collective-permute-start
  6.8 0.0 copy-done
  6.8 0.0 copy-done.1
  6.8 0.0 copy-done.2
  6.8 1.7 %shard_map.69 = (bf16[8,64,1024]{2,1,0:T(8,128)(2,1)S(1)}, bf16[256,128]{1,0:T(8,128)(2,1)S(1)}) custom-call(bf16[256,8192]{1,0:T(8,128)(2,1)S(1)} %get-tuple-element.14.hidden, bf16[256,128]{1,0:T(8,128)(2,1)S(1)} %get-tuple-element.15.query, bf16[256,64]{1,0:T(8,128)(2,1)S(1)} %get-tuple-element.16.others, bf16[64,256]{1,0:T(8,128)(2,1)S(1)} %bitcast.3, ...), custom_call_target="tpu_custom_call" | custom-call | flops 268435456 | bytes 4194304 | tf_op jit(solution)/shard_map/pallas_call | solution.py:146
  8.5 3.8 %shard_map.70.refs_0_ = bf16[256,8192]{1,0:T(8,128)(2,1)} custom-call(bf16[256,128]{1,0:T(8,128)(2,1)S(1)} %get-tuple-element.19.grad_query, bf16[128,8192]{1,0:T(8,128)(2,1)} %weight_hbm.5), custom_call_target="tpu_custom_call" | custom-call | flops 536870912 | bytes 6291456 | tf_op jit(solution)/shard_map/pallas_call | solution.py:188
  12.3 0.0 collective-permute-done
  12.3 0.4 add_convert_fusion
  12.7 16.7 %all_to_all.10 = bf16[8,64,1024]{2,1,0:T(8,128)(2,1)S(1)} all-to-all(bf16[8,64,1024]{2,1,0:T(8,128)(2,1)S(1)} %add_convert_fusion), channel_id=1, replica_groups={{14,12,10,8,6,4,2,0},{15,13,11,9,7,5,3,1},{22,20,18,16,30,28,26,24},{23..., dimensions={0} | all-to-all | bytes 2097152 | tf_op jit(solution)/shard_map/all_to_all | solution.py:264
  29.4 0.2 reduce_sum.12
  29.6 2.5 %collective-permute-start.1 = (bf16[64,1024]{1,0:T(8,128)(2,1)S(1)}, bf16[64,1024]{1,0:T(8,128)(2,1)S(1)}, u32[]{:S(2)}, u32[]{:S(2)}) collective-permute-start(bf16[64,1024]{1,0:T(8,128)(2,1)S(1)} %reduce_sum.12), channel_id=1, source_target_pairs={{0,24},{1,25},{2,26},{3,27},{4,28},{5,29},{6,30},{7,31},{8,16},{9,... | collective-permute-start | bytes 393224 | tf_op jit(solution)/shard_map/ppermute | solution.py:236
  32.1 0.1 shard_map.71
  32.2 4.3 %collective-permute-done.1 = bf16[64,1024]{1,0:T(8,128)(2,1)S(1)} collective-permute-done((bf16[64,1024]{1,0:T(8,128)(2,1)S(1)}, bf16[64,1024]{1,0:T(8,128)(2,1)S(1)}, u32[]{:S(2)}, u32[]{:S(2)}) %collective-permute-start.1) | collective-permute-done | bytes 131104 | tf_op jit(solution)/shard_map/ppermute | solution.py:236
  36.6 0.1 broadcast_in_dim.2
  36.7 13.4 %all_to_all.11.piece_hbm = bf16[8,64,1024]{2,1,0:T(8,128)(2,1)S(1)} all-to-all(bf16[8,64,1024]{2,1,0:T(8,128)(2,1)S(1)} %broadcast_in_dim.2), channel_id=1, replica_groups={{14,12,10,8,6,4,2,0},{15,13,11,9,7,5,3,1},{22,20,18,16,30,28,26,24},{23..., dimensions={0} | all-to-all | bytes 2097152 | tf_op jit(solution)/shard_map/all_to_all | solution.py:274
  50.1 0.0 collective-permute-start.2
  50.1 1.0 %shard_map.72.refs_0_ = bf16[128,8192]{1,0:T(8,128)(2,1)} custom-call(bf16[8,64,1024]{2,1,0:T(8,128)(2,1)S(1)} %all_to_all.11.piece_hbm), custom_call_target="tpu_custom_call" | custom-call | bytes 2097152 | tf_op jit(solution)/shard_map/pallas_call | solution.py:223
  51.1 1.6 %collective-permute-done.2.piece_hbm = bf16[8,64,1024]{2,1,0:T(8,128)(2,1)S(1)} collective-permute-done((bf16[8,64,1024]{2,1,0:T(8,128)(2,1)S(1)}, bf16[8,64,1024]{2,1,0:T(8,128)(2,1)S(1)}, u32[]{:S(2)}, u32[]{:S(2)}) %collective-permute-start.2) | collective-permute-done | bytes 1048608 | tf_op jit(solution)/shard_map/ppermute | solution.py:236
  52.8 1.0 %shard_map.73 = bf16[128,8192]{1,0:T(8,128)(2,1)} custom-call(bf16[8,64,1024]{2,1,0:T(8,128)(2,1)S(1)} %collective-permute-done.2.piece_hbm, bf16[128,8192]{1,0:T(8,128)(2,1)} %shard_map.72.refs_0_), custom_call_target="tpu_custom_call", output_to_operand_aliasing={{}: (1, {})} | custom-call | bytes 2097152 | tf_op jit(solution)/shard_map/pallas_call | solution.py:223
  (1 shorter events, 0.0 us)
Async XLA Ops:
  0.6 6.1 %copy-start = (bf16[256,128]{1,0:T(8,128)(2,1)S(1)}, bf16[256,128]{1,0:T(8,128)(2,1)}, u32[]{:S(2)}) copy-start(bf16[256,128]{1,0:T(8,128)(2,1)} %grad_out.1) | copy-start | bytes 196612
  0.6 6.1 %copy-start.1 = (bf16[256,64]{0,1:T(8,128)(2,1)S(1)}, bf16[256,64]{0,1:T(8,128)(2,1)}, u32[]{:S(2)}) copy-start(bf16[256,64]{0,1:T(8,128)(2,1)} %param.7) | copy-start | bytes 98308
  0.7 6.1 %copy-start.2 = (bf16[256,64]{0,1:T(8,128)(2,1)S(1)}, bf16[256,64]{0,1:T(8,128)(2,1)}, u32[]{:S(2)}) copy-start(bf16[256,64]{0,1:T(8,128)(2,1)} %param.8) | copy-start | bytes 98308
  6.2 6.0 %collective-permute-start = (bf16[8,64,1024]{2,1,0:T(8,128)(2,1)S(1)}, bf16[8,64,1024]{2,1,0:T(8,128)(2,1)S(1)}, u32[]{:S(2)}, u32[]{:S(2)}) collective-permute-start(bf16[8,64,1024]{2,1,0:T(8,128)(2,1)S(1)} %get-tuple-element.18), channel_id=1, source_target_pairs={{0,1},{1,0},{2,3},{3,2},{4,5},{5,4},{6,7},{7,6},{8,9},{9,8},{10,11... | collective-permute-start | bytes 3145736 | tf_op jit(solution)/shard_map/ppermute | solution.py:236
  29.6 6.9 %collective-permute-start.1 = (bf16[64,1024]{1,0:T(8,128)(2,1)S(1)}, bf16[64,1024]{1,0:T(8,128)(2,1)S(1)}, u32[]{:S(2)}, u32[]{:S(2)}) collective-permute-start(bf16[64,1024]{1,0:T(8,128)(2,1)S(1)} %reduce_sum.12), channel_id=1, source_target_pairs={{0,24},{1,25},{2,26},{3,27},{4,28},{5,29},{6,30},{7,31},{8,16},{9,... | collective-permute-start | bytes 393224 | tf_op jit(solution)/shard_map/ppermute | solution.py:236
  50.1 2.7 %collective-permute-start.2 = (bf16[8,64,1024]{2,1,0:T(8,128)(2,1)S(1)}, bf16[8,64,1024]{2,1,0:T(8,128)(2,1)S(1)}, u32[]{:S(2)}, u32[]{:S(2)}) collective-permute-start(bf16[8,64,1024]{2,1,0:T(8,128)(2,1)S(1)} %all_to_all.11.piece_hbm), channel_id=1, source_target_pairs={{0,1},{1,0},{2,3},{3,2},{4,5},{5,4},{6,7},{7,6},{8,9},{9,8},{10,11... | collective-permute-start | bytes 3145736 | tf_op jit(solution)/shard_map/ppermute | solution.py:236

commit v12 on v11

--- a/solution.py
+++ b/solution.py
@@ -8,6 +8,7 @@
 from jax.sharding import PartitionSpec as P
 
 LOADS = 4
+PARTS = 4
 HIDDEN_PIECES = 4
 VMEM_LIMIT = 40 * 1024 * 1024
 ANY = pl.BlockSpec(memory_space=pl.ANY)
@@ -55,9 +56,10 @@
 
 def add_rows(grads, hidden, out):
     turned = grads.T
-    step = out.shape[2]
-    for block in range(out.shape[0]):
-        out[block] = dot(turned, hidden[:, pl.ds(block * step, step)]).astype(out.dtype)
+    step = out.shape[1] // PARTS
+    for part in range(PARTS):
+        columns = pl.ds(part * step, step)
+        out[:, columns] = dot(turned, hidden[:, columns]).astype(out.dtype)
 
 
 def query_kernel(
@@ -96,7 +98,7 @@
     add_rows(found, hidden, other)
 
 
-def query_and_other(blocks, hidden_in, query_weight, keys, values, grad_out):
+def query_and_other(hidden_in, query_weight, keys, values, grad_out):
     tokens, width = hidden_in.shape
     rows = query_weight.shape[0]
     like = lambda array: pltpu.VMEM(array.shape, array.dtype)
@@ -104,7 +106,7 @@
     return pl.pallas_call(
         query_kernel,
         out_shape=(
-            jax.ShapeDtypeStruct((blocks, rows // 2, width // blocks), jnp.bfloat16),
+            jax.ShapeDtypeStruct((rows // 2, width), jnp.bfloat16),
             jax.ShapeDtypeStruct((tokens, width), jnp.bfloat16),
             jax.ShapeDtypeStruct((rows, width), jnp.bfloat16),
             jax.ShapeDtypeStruct((tokens, rows), jnp.bfloat16),
@@ -140,13 +142,13 @@
     )
 
 
-def own_part(blocks, hidden, query, others, keys, values, grad_out):
+def own_part(hidden, query, others, keys, values, grad_out):
     tokens, width = hidden.shape
     rows = query.shape[1]
     return pl.pallas_call(
         own_kernel,
         out_shape=(
-            jax.ShapeDtypeStruct((blocks, rows // 2, width // blocks), jnp.bfloat16),
+            jax.ShapeDtypeStruct((rows // 2, width), jnp.bfloat16),
             jax.ShapeDtypeStruct((tokens, rows), jnp.bfloat16),
         ),
         in_specs=[WHOLE] * 6,
@@ -206,29 +208,24 @@
 
 def place_kernel(turned, piece_hbm, *refs):
     out_hbm, sem = refs[-2:]
-    blocks, half, step = piece_hbm.shape
+    half = piece_hbm.shape[0]
     rows = pl.ds(pl.multiple_of((own_core() ^ turned) * half, half), half)
-    copies = [
-        pltpu.make_async_copy(piece_hbm.at[block], out_hbm.at[rows, pl.ds(block * step, step)], sem.at[block])
-        for block in range(blocks)
-    ]
-    for copy in copies:
-        copy.start()
-    for copy in copies:
-        copy.wait()
+    copy = pltpu.make_async_copy(piece_hbm, out_hbm.at[rows], sem)
+    copy.start()
+    copy.wait()
 
 
 def place(turned, piece, before=None):
-    blocks, half, step = piece.shape
+    half, width = piece.shape
     return pl.pallas_call(
         functools.partial(place_kernel, turned),
-        out_shape=jax.ShapeDtypeStruct((2 * half, blocks * step), jnp.bfloat16),
+        out_shape=jax.ShapeDtypeStruct((2 * half, width), jnp.bfloat16),
         in_specs=[ANY] + [ANY] * (before is not None),
         out_specs=ANY,
-        scratch_shapes=[pltpu.SemaphoreType.DMA((blocks,))],
+        scratch_shapes=[pltpu.SemaphoreType.DMA(())],
         input_output_aliases={} if before is None else {1: 0},
         compiler_params=pltpu.CompilerParams(vmem_limit_bytes=VMEM_LIMIT),
-        cost_estimate=pl.CostEstimate(flops=0, bytes_accessed=4 * half * blocks * step, transcendentals=0),
+        cost_estimate=pl.CostEstimate(flops=0, bytes_accessed=4 * half * width, transcendentals=0),
     )(piece, *(() if before is None else (before,)))
 
 
@@ -254,11 +251,13 @@
         hidden_in = lax.all_gather(hidden_in, "tensor", axis=1, tiled=True)
     keys, values = saved_keys.T, saved_values.T
     other, hidden, weight, query, grads = query_and_other(
-        blocks, hidden_in, query_weight, keys, values, grad_out
+        hidden_in, query_weight, keys, values, grad_out
     )
     arriving = swap(other, 1, count)
-    own, grad_query = own_part(blocks, hidden, query, grads, keys, values, grad_out)
+    own, grad_query = own_part(hidden, query, grads, keys, values, grad_out)
     chip = add(own, arriving)
+    half, width = chip.shape
+    chip = chip.reshape(blocks, half // blocks, width)
     input_terms = hidden_part(0, grad_query, query_weight)
     chip, input_terms = lax.optimization_barrier((chip, input_terms))
     parts = lax.all_to_all(chip, "dp", 0, 0, axis_index_groups=groups)
@@ -271,7 +270,7 @@
             arriving, input_terms = lax.optimization_barrier((arriving, input_terms))
         total = add(total, arriving)
     copies = jnp.broadcast_to(total[None], (blocks, *total.shape))
-    gathered = lax.all_to_all(copies, "dp", 0, 0, axis_index_groups=groups)
+    gathered = lax.all_to_all(copies, "dp", 0, 0, axis_index_groups=groups).reshape(half, width)
     arriving = swap(gathered, 1, count)
     grad_query_weight = place(1, arriving, place(0, gathered))
     if input_terms.shape[1] == given_width:

time: 54 us -> 53.7 us (level)
  no operation moved by 1% of the time
where the time goes in v12:
time: 53.7 us; the launch traced here: 53.5 us
  blocking collectives  30.1 us (56%)
  Pallas kernels  13.1 us (24%)
  waiting for transfers between devices  5.99 us (11%)
  starting transfers between devices  3.06 us (6%)
  between operations  0.73 us (1%)
    all_to_all x1, blocking collectives, per_device(): parts = lax.all_to_all(chip, 'dp', 0, 0, axis_index_groups=groups)  16.7 us
    all_to_all x1, blocking collectives, per_device(): lax.all_to_all(copies, 'dp', 0, 0, axis_index_groups=groups)  13.4 us
    ppermute x3, waiting for transfers between devices, swap(): return lax.ppermute(array, 'dp', [(i, i ^ step) for i in range(count)])  5.99 us
    pallas_call x1, Pallas kernels, query_and_other(): pl.pallas_call(query_kernel, out_shape=(jax.ShapeDtypeStruct((rows // 2,...  5.57 us
    pallas_call x2, Pallas kernels, hidden_part(): pl.pallas_call(functools.partial(hidden_kernel, turn), out_shape=jax.Shap...  3.84 us
    ppermute x3, starting transfers between devices, swap(): return lax.ppermute(array, 'dp', [(i, i ^ step) for i in range(count)])  3.06 us
    pallas_call x2, Pallas kernels, place(): pl.pallas_call(functools.partial(place_kernel, turned), out_shape=jax.Sha...  1.96 us
    pallas_call x1, Pallas kernels, own_part(): pl.pallas_call(own_kernel, out_shape=(jax.ShapeDtypeStruct((rows // 2, wi...  1.72 us
  transfers between devices with their start and end apart: 3, of which 2 were waited for; matrix products, arithmetic and copies ran while one was open for 0% of the time, Pallas kernels for 12%

profile of v12, /device:TPU:0, one launch (start us, length us, event | category | flops | bytes accessed | tf_op | source)
XLA Modules:
  0.0 53.5 jit_solution(12964962794830522679)
XLA Ops:
  0.6 0.0 copy-start
  0.6 0.0 copy-start.1
  0.7 0.0 copy-start.2
  0.7 5.6 %shard_map.68 = (bf16[64,8192]{1,0:T(8,128)(2,1)S(1)}, bf16[256,8192]{1,0:T(8,128)(2,1)S(1)}, bf16[128,8192]{1,0:T(8,128)(2,1)}, bf16[256,128]{1,0:T(8,128)(2,1)S(1)}, bf16[256,64]{1,0:T(8,128)(2,1)S(1)}) custom-call(bf16[256,8192]{1,0:T(8,128)(2,1)} %hidden_hbm.1, bf16[128,8192]{1,0:T(8,128)(2,1)} %weight_hbm.5, bf16[64,256]{1,0:T(8,128)(2,1)} %bitcast.7, ...), custom_call_target="tpu_custom_call" | custom-call | flops 805306368 | bytes 6291456 | tf_op jit(solution)/shard_map/pallas_call | solution.py:106
  6.2 0.5 collective-permute-start
  6.8 0.0 copy-done
  6.8 0.0 copy-done.1
  6.8 0.0 copy-done.2
  6.8 1.7 %shard_map.69 = (bf16[64,8192]{1,0:T(8,128)(2,1)S(1)}, bf16[256,128]{1,0:T(8,128)(2,1)S(1)}) custom-call(bf16[256,8192]{1,0:T(8,128)(2,1)S(1)} %get-tuple-element.14.hidden, bf16[256,128]{1,0:T(8,128)(2,1)S(1)} %get-tuple-element.15.query, bf16[256,64]{1,0:T(8,128)(2,1)S(1)} %get-tuple-element.16.others, bf16[64,256]{1,0:T(8,128)(2,1)S(1)} %bitcast.8, ...), custom_call_target="tpu_custom_call" | custom-call | flops 268435456 | bytes 4194304 | tf_op jit(solution)/shard_map/pallas_call | solution.py:148
  8.5 3.8 %shard_map.70.refs_0_ = bf16[256,8192]{1,0:T(8,128)(2,1)} custom-call(bf16[256,128]{1,0:T(8,128)(2,1)S(1)} %get-tuple-element.19.grad_query, bf16[128,8192]{1,0:T(8,128)(2,1)} %weight_hbm.5), custom_call_target="tpu_custom_call" | custom-call | flops 536870912 | bytes 6291456 | tf_op jit(solution)/shard_map/pallas_call | solution.py:190
  12.3 0.0 collective-permute-done
  12.3 0.2 fusion
  12.5 16.7 %all_to_all.10 = bf16[8,8,8192]{2,1,0:T(8,128)(2,1)S(1)} all-to-all(bf16[8,8,8192]{2,1,0:T(8,128)(2,1)S(1)} %fusion), channel_id=1, replica_groups={{14,12,10,8,6,4,2,0},{15,13,11,9,7,5,3,1},{22,20,18,16,30,28,26,24},{23..., dimensions={0} | all-to-all | bytes 2097152 | tf_op jit(solution)/shard_map/all_to_all | solution.py:263
  29.2 0.1 reduce_sum.12
  29.4 2.5 %collective-permute-start.1 = (bf16[8,8192]{1,0:T(8,128)(2,1)S(1)}, bf16[8,8192]{1,0:T(8,128)(2,1)S(1)}, u32[]{:S(2)}, u32[]{:S(2)}) collective-permute-start(bf16[8,8192]{1,0:T(8,128)(2,1)S(1)} %reduce_sum.12), channel_id=1, source_target_pairs={{0,24},{1,25},{2,26},{3,27},{4,28},{5,29},{6,30},{7,31},{8,16},{9,... | collective-permute-start | bytes 393224 | tf_op jit(solution)/shard_map/ppermute | solution.py:233
  31.9 0.1 shard_map.71
  32.0 4.3 %collective-permute-done.1 = bf16[8,8192]{1,0:T(8,128)(2,1)S(1)} collective-permute-done((bf16[8,8192]{1,0:T(8,128)(2,1)S(1)}, bf16[8,8192]{1,0:T(8,128)(2,1)S(1)}, u32[]{:S(2)}, u32[]{:S(2)}) %collective-permute-start.1) | collective-permute-done | bytes 131104 | tf_op jit(solution)/shard_map/ppermute | solution.py:233
  36.4 0.1 broadcast_in_dim.2
  36.4 13.4 %all_to_all.11 = bf16[8,8,8192]{2,1,0:T(8,128)(2,1)S(1)} all-to-all(bf16[8,8,8192]{2,1,0:T(8,128)(2,1)S(1)} %broadcast_in_dim.2), channel_id=1, replica_groups={{14,12,10,8,6,4,2,0},{15,13,11,9,7,5,3,1},{22,20,18,16,30,28,26,24},{23..., dimensions={0} | all-to-all | bytes 2097152 | tf_op jit(solution)/shard_map/all_to_all | solution.py:273
  49.9 0.0 collective-permute-start.2
  49.9 1.0 %shard_map.72.refs_0_ = bf16[128,8192]{1,0:T(8,128)(2,1)} custom-call(bf16[64,8192]{1,0:T(8,128)(2,1)S(1)} %bitcast.6), custom_call_target="tpu_custom_call" | custom-call | bytes 2097152 | tf_op jit(solution)/shard_map/pallas_call | solution.py:220
  50.8 1.7 %collective-permute-done.2.piece_hbm = bf16[64,8192]{1,0:T(8,128)(2,1)S(1)} collective-permute-done((bf16[64,8192]{1,0:T(8,128)(2,1)S(1)}, bf16[64,8192]{1,0:T(8,128)(2,1)S(1)}, u32[]{:S(2)}, u32[]{:S(2)}) %collective-permute-start.2) | collective-permute-done | bytes 1048608 | tf_op jit(solution)/shard_map/ppermute | solution.py:233
  52.5 1.0 %shard_map.73 = bf16[128,8192]{1,0:T(8,128)(2,1)} custom-call(bf16[64,8192]{1,0:T(8,128)(2,1)S(1)} %collective-permute-done.2.piece_hbm, bf16[128,8192]{1,0:T(8,128)(2,1)} %shard_map.72.refs_0_), custom_call_target="tpu_custom_call", output_to_operand_aliasing={{}: (1, {})} | custom-call | bytes 2097152 | tf_op jit(solution)/shard_map/pallas_call | solution.py:220
  (1 shorter events, 0.0 us)
Async XLA Ops:
  0.6 6.1 %copy-start = (bf16[256,128]{1,0:T(8,128)(2,1)S(1)}, bf16[256,128]{1,0:T(8,128)(2,1)}, u32[]{:S(2)}) copy-start(bf16[256,128]{1,0:T(8,128)(2,1)} %grad_out.1) | copy-start | bytes 196612
  0.6 6.1 %copy-start.1 = (bf16[256,64]{0,1:T(8,128)(2,1)S(1)}, bf16[256,64]{0,1:T(8,128)(2,1)}, u32[]{:S(2)}) copy-start(bf16[256,64]{0,1:T(8,128)(2,1)} %param.7) | copy-start | bytes 98308
  0.7 6.1 %copy-start.2 = (bf16[256,64]{0,1:T(8,128)(2,1)S(1)}, bf16[256,64]{0,1:T(8,128)(2,1)}, u32[]{:S(2)}) copy-start(bf16[256,64]{0,1:T(8,128)(2,1)} %param.8) | copy-start | bytes 98308
  6.2 6.0 %collective-permute-start = (bf16[64,8192]{1,0:T(8,128)(2,1)S(1)}, bf16[64,8192]{1,0:T(8,128)(2,1)S(1)}, u32[]{:S(2)}, u32[]{:S(2)}) collective-permute-start(bf16[64,8192]{1,0:T(8,128)(2,1)S(1)} %get-tuple-element.18), channel_id=1, source_target_pairs={{0,1},{1,0},{2,3},{3,2},{4,5},{5,4},{6,7},{7,6},{8,9},{9,8},{10,11... | collective-permute-start | bytes 3145736 | tf_op jit(solution)/shard_map/ppermute | solution.py:233
  29.4 6.9 %collective-permute-start.1 = (bf16[8,8192]{1,0:T(8,128)(2,1)S(1)}, bf16[8,8192]{1,0:T(8,128)(2,1)S(1)}, u32[]{:S(2)}, u32[]{:S(2)}) collective-permute-start(bf16[8,8192]{1,0:T(8,128)(2,1)S(1)} %reduce_sum.12), channel_id=1, source_target_pairs={{0,24},{1,25},{2,26},{3,27},{4,28},{5,29},{6,30},{7,31},{8,16},{9,... | collective-permute-start | bytes 393224 | tf_op jit(solution)/shard_map/ppermute | solution.py:233
  49.9 2.7 %collective-permute-start.2 = (bf16[64,8192]{1,0:T(8,128)(2,1)S(1)}, bf16[64,8192]{1,0:T(8,128)(2,1)S(1)}, u32[]{:S(2)}, u32[]{:S(2)}) collective-permute-start(bf16[64,8192]{1,0:T(8,128)(2,1)S(1)} %bitcast.5), channel_id=1, source_target_pairs={{0,1},{1,0},{2,3},{3,2},{4,5},{5,4},{6,7},{7,6},{8,9},{9,8},{10,11... | collective-permute-start | bytes 3145736 | tf_op jit(solution)/shard_map/ppermute | solution.py:233

commit v13 on v12

--- a/solution.py
+++ b/solution.py
@@ -64,8 +64,8 @@
 
 def query_kernel(
     hidden_hbm, weight_hbm, keys_hbm, values_hbm, grad_out_hbm,
-    other, hidden, weight, query, grads,
-    turned, keys, values, grad_out, hidden_sem, weight_sem, small_sem,
+    other, hidden, query, grads,
+    weight, turned, keys, values, grad_out, hidden_sem, weight_sem, small_sem,
 ):
     tokens, width = hidden.shape
     step = width // LOADS
@@ -108,13 +108,13 @@
         out_shape=(
             jax.ShapeDtypeStruct((rows // 2, width), jnp.bfloat16),
             jax.ShapeDtypeStruct((tokens, width), jnp.bfloat16),
-            jax.ShapeDtypeStruct((rows, width), jnp.bfloat16),
             jax.ShapeDtypeStruct((tokens, rows), jnp.bfloat16),
             jax.ShapeDtypeStruct((tokens, rows // 2), jnp.bfloat16),
         ),
         in_specs=[ANY] * 5,
-        out_specs=(WHOLE,) * 5,
+        out_specs=(WHOLE,) * 4,
         scratch_shapes=[
+            like(query_weight),
             pltpu.VMEM((width, rows), jnp.bfloat16),
             like(keys),
             like(values),
@@ -250,9 +250,7 @@
     if given_width != query_weight.shape[1]:
         hidden_in = lax.all_gather(hidden_in, "tensor", axis=1, tiled=True)
     keys, values = saved_keys.T, saved_values.T
-    other, hidden, weight, query, grads = query_and_other(
-        hidden_in, query_weight, keys, values, grad_out
-    )
+    other, hidden, query, grads = query_and_other(hidden_in, query_weight, keys, values, grad_out)
     arriving = swap(other, 1, count)
     own, grad_query = own_part(hidden, query, grads, keys, values, grad_out)
     chip = add(own, arriving)

time: 53.7 us -> 53.7 us (level)
  no operation moved by 1% of the time
where the time goes in v13:
time: 53.7 us; the launch traced here: 53.5 us
  blocking collectives  30.1 us (56%)
  Pallas kernels  13.1 us (24%)
  waiting for transfers between devices  5.99 us (11%)
  starting transfers between devices  3.06 us (6%)
  between operations  0.73 us (1%)
    all_to_all x1, blocking collectives, per_device(): parts = lax.all_to_all(chip, 'dp', 0, 0, axis_index_groups=groups)  16.7 us
    all_to_all x1, blocking collectives, per_device(): lax.all_to_all(copies, 'dp', 0, 0, axis_index_groups=groups)  13.4 us
    ppermute x3, waiting for transfers between devices, swap(): return lax.ppermute(array, 'dp', [(i, i ^ step) for i in range(count)])  5.99 us
    pallas_call x1, Pallas kernels, query_and_other(): pl.pallas_call(query_kernel, out_shape=(jax.ShapeDtypeStruct((rows // 2,...  5.57 us
    pallas_call x2, Pallas kernels, hidden_part(): pl.pallas_call(functools.partial(hidden_kernel, turn), out_shape=jax.Shap...  3.84 us
    ppermute x3, starting transfers between devices, swap(): return lax.ppermute(array, 'dp', [(i, i ^ step) for i in range(count)])  3.06 us
    pallas_call x2, Pallas kernels, place(): pl.pallas_call(functools.partial(place_kernel, turned), out_shape=jax.Sha...  1.96 us
    pallas_call x1, Pallas kernels, own_part(): pl.pallas_call(own_kernel, out_shape=(jax.ShapeDtypeStruct((rows // 2, wi...  1.72 us
  transfers between devices with their start and end apart: 3, of which 2 were waited for; matrix products, arithmetic and copies ran while one was open for 0% of the time, Pallas kernels for 12%

profile of v13, /device:TPU:0, one launch (start us, length us, event | category | flops | bytes accessed | tf_op | source)
XLA Modules:
  0.0 53.5 jit_solution(8484130998286264057)
XLA Ops:
  0.6 0.0 copy-start
  0.6 0.0 copy-start.1
  0.7 0.0 copy-start.2
  0.7 5.6 %shard_map.68 = (bf16[64,8192]{1,0:T(8,128)(2,1)S(1)}, bf16[256,8192]{1,0:T(8,128)(2,1)S(1)}, bf16[256,128]{1,0:T(8,128)(2,1)S(1)}, bf16[256,64]{1,0:T(8,128)(2,1)S(1)}) custom-call(bf16[256,8192]{1,0:T(8,128)(2,1)} %hidden_hbm.1, bf16[128,8192]{1,0:T(8,128)(2,1)} %weight_hbm.5, bf16[64,256]{1,0:T(8,128)(2,1)} %bitcast.7, bf16[64,256]{1,0:T(8,128)(2,1)} %bitcast.9, ...), custom_call_target="tpu_custom_call" | custom-call | flops 805306368 | bytes 6291456 | tf_op jit(solution)/shard_map/pallas_call | solution.py:106
  6.2 0.5 collective-permute-start
  6.8 0.0 copy-done
  6.8 0.0 copy-done.1
  6.8 0.0 copy-done.2
  6.8 1.7 %shard_map.69 = (bf16[64,8192]{1,0:T(8,128)(2,1)S(1)}, bf16[256,128]{1,0:T(8,128)(2,1)S(1)}) custom-call(bf16[256,8192]{1,0:T(8,128)(2,1)S(1)} %get-tuple-element.14.hidden, bf16[256,128]{1,0:T(8,128)(2,1)S(1)} %get-tuple-element.15.query, bf16[256,64]{1,0:T(8,128)(2,1)S(1)} %get-tuple-element.16.others, bf16[64,256]{1,0:T(8,128)(2,1)S(1)} %bitcast.8, ...), custom_call_target="tpu_custom_call" | custom-call | flops 268435456 | bytes 4194304 | tf_op jit(solution)/shard_map/pallas_call | solution.py:148
  8.5 3.8 %shard_map.70.refs_0_ = bf16[256,8192]{1,0:T(8,128)(2,1)} custom-call(bf16[256,128]{1,0:T(8,128)(2,1)S(1)} %get-tuple-element.19.grad_query, bf16[128,8192]{1,0:T(8,128)(2,1)} %weight_hbm.5), custom_call_target="tpu_custom_call" | custom-call | flops 536870912 | bytes 6291456 | tf_op jit(solution)/shard_map/pallas_call | solution.py:190
  12.3 0.0 collective-permute-done
  12.3 0.2 fusion
  12.5 16.7 %all_to_all.10 = bf16[8,8,8192]{2,1,0:T(8,128)(2,1)S(1)} all-to-all(bf16[8,8,8192]{2,1,0:T(8,128)(2,1)S(1)} %fusion), channel_id=1, replica_groups={{14,12,10,8,6,4,2,0},{15,13,11,9,7,5,3,1},{22,20,18,16,30,28,26,24},{23..., dimensions={0} | all-to-all | bytes 2097152 | tf_op jit(solution)/shard_map/all_to_all | solution.py:261
  29.2 0.1 reduce_sum.12
  29.4 2.5 %collective-permute-start.1 = (bf16[8,8192]{1,0:T(8,128)(2,1)S(1)}, bf16[8,8192]{1,0:T(8,128)(2,1)S(1)}, u32[]{:S(2)}, u32[]{:S(2)}) collective-permute-start(bf16[8,8192]{1,0:T(8,128)(2,1)S(1)} %reduce_sum.12), channel_id=1, source_target_pairs={{0,24},{1,25},{2,26},{3,27},{4,28},{5,29},{6,30},{7,31},{8,16},{9,... | collective-permute-start | bytes 393224 | tf_op jit(solution)/shard_map/ppermute | solution.py:233
  31.9 0.1 shard_map.71
  32.0 4.3 %collective-permute-done.1 = bf16[8,8192]{1,0:T(8,128)(2,1)S(1)} collective-permute-done((bf16[8,8192]{1,0:T(8,128)(2,1)S(1)}, bf16[8,8192]{1,0:T(8,128)(2,1)S(1)}, u32[]{:S(2)}, u32[]{:S(2)}) %collective-permute-start.1) | collective-permute-done | bytes 131104 | tf_op jit(solution)/shard_map/ppermute | solution.py:233
  36.4 0.1 broadcast_in_dim.2
  36.4 13.4 %all_to_all.11 = bf16[8,8,8192]{2,1,0:T(8,128)(2,1)S(1)} all-to-all(bf16[8,8,8192]{2,1,0:T(8,128)(2,1)S(1)} %broadcast_in_dim.2), channel_id=1, replica_groups={{14,12,10,8,6,4,2,0},{15,13,11,9,7,5,3,1},{22,20,18,16,30,28,26,24},{23..., dimensions={0} | all-to-all | bytes 2097152 | tf_op jit(solution)/shard_map/all_to_all | solution.py:271
  49.9 0.0 collective-permute-start.2
  49.9 1.0 %shard_map.72.refs_0_ = bf16[128,8192]{1,0:T(8,128)(2,1)} custom-call(bf16[64,8192]{1,0:T(8,128)(2,1)S(1)} %bitcast.6), custom_call_target="tpu_custom_call" | custom-call | bytes 2097152 | tf_op jit(solution)/shard_map/pallas_call | solution.py:220
  50.9 1.7 %collective-permute-done.2.piece_hbm = bf16[64,8192]{1,0:T(8,128)(2,1)S(1)} collective-permute-done((bf16[64,8192]{1,0:T(8,128)(2,1)S(1)}, bf16[64,8192]{1,0:T(8,128)(2,1)S(1)}, u32[]{:S(2)}, u32[]{:S(2)}) %collective-permute-start.2) | collective-permute-done | bytes 1048608 | tf_op jit(solution)/shard_map/ppermute | solution.py:233
  52.5 1.0 %shard_map.73 = bf16[128,8192]{1,0:T(8,128)(2,1)} custom-call(bf16[64,8192]{1,0:T(8,128)(2,1)S(1)} %collective-permute-done.2.piece_hbm, bf16[128,8192]{1,0:T(8,128)(2,1)} %shard_map.72.refs_0_), custom_call_target="tpu_custom_call", output_to_operand_aliasing={{}: (1, {})} | custom-call | bytes 2097152 | tf_op jit(solution)/shard_map/pallas_call | solution.py:220
  (1 shorter events, 0.0 us)
Async XLA Ops:
  0.6 6.1 %copy-start = (bf16[256,128]{1,0:T(8,128)(2,1)S(1)}, bf16[256,128]{1,0:T(8,128)(2,1)}, u32[]{:S(2)}) copy-start(bf16[256,128]{1,0:T(8,128)(2,1)} %grad_out.1) | copy-start | bytes 196612
  0.6 6.1 %copy-start.1 = (bf16[256,64]{0,1:T(8,128)(2,1)S(1)}, bf16[256,64]{0,1:T(8,128)(2,1)}, u32[]{:S(2)}) copy-start(bf16[256,64]{0,1:T(8,128)(2,1)} %param.7) | copy-start | bytes 98308
  0.7 6.1 %copy-start.2 = (bf16[256,64]{0,1:T(8,128)(2,1)S(1)}, bf16[256,64]{0,1:T(8,128)(2,1)}, u32[]{:S(2)}) copy-start(bf16[256,64]{0,1:T(8,128)(2,1)} %param.8) | copy-start | bytes 98308
  6.2 6.0 %collective-permute-start = (bf16[64,8192]{1,0:T(8,128)(2,1)S(1)}, bf16[64,8192]{1,0:T(8,128)(2,1)S(1)}, u32[]{:S(2)}, u32[]{:S(2)}) collective-permute-start(bf16[64,8192]{1,0:T(8,128)(2,1)S(1)} %get-tuple-element.18), channel_id=1, source_target_pairs={{0,1},{1,0},{2,3},{3,2},{4,5},{5,4},{6,7},{7,6},{8,9},{9,8},{10,11... | collective-permute-start | bytes 3145736 | tf_op jit(solution)/shard_map/ppermute | solution.py:233
  29.4 6.9 %collective-permute-start.1 = (bf16[8,8192]{1,0:T(8,128)(2,1)S(1)}, bf16[8,8192]{1,0:T(8,128)(2,1)S(1)}, u32[]{:S(2)}, u32[]{:S(2)}) collective-permute-start(bf16[8,8192]{1,0:T(8,128)(2,1)S(1)} %reduce_sum.12), channel_id=1, source_target_pairs={{0,24},{1,25},{2,26},{3,27},{4,28},{5,29},{6,30},{7,31},{8,16},{9,... | collective-permute-start | bytes 393224 | tf_op jit(solution)/shard_map/ppermute | solution.py:233
  49.9 2.7 %collective-permute-start.2 = (bf16[64,8192]{1,0:T(8,128)(2,1)S(1)}, bf16[64,8192]{1,0:T(8,128)(2,1)S(1)}, u32[]{:S(2)}, u32[]{:S(2)}) collective-permute-start(bf16[64,8192]{1,0:T(8,128)(2,1)S(1)} %bitcast.5), channel_id=1, source_target_pairs={{0,1},{1,0},{2,3},{3,2},{4,5},{5,4},{6,7},{7,6},{8,9},{9,8},{10,11... | collective-permute-start | bytes 3145736 | tf_op jit(solution)/shard_map/ppermute | solution.py:233

commit v14 on v13

--- a/solution.py
+++ b/solution.py
@@ -241,8 +241,10 @@
     bits = count.bit_length() - 1
     wide = min(3, bits - 1)
     blocks = 1 << wide
+    falling = list(reversed(range(blocks)))
+    inward = [place for low in range(blocks // 2) for place in (blocks - 1 - low, low)] or falling
     groups = [
-        [high << (wide + 1) | (place ^ (high & 1) * (blocks >> 1)) << 1 | core for place in reversed(range(blocks))]
+        [high << (wide + 1) | (place ^ (high & 1) * (blocks >> 1)) << 1 | core for place in (inward, falling)[core]]
         for high in range(count >> (wide + 1))
         for core in range(2)
     ]

time: 53.7 us -> 53.3 us (level)
  no operation moved by 1% of the time
where the time goes in v14:
time: 53.3 us; the launch traced here: 53 us
  blocking collectives  29.7 us (56%)
  Pallas kernels  13.1 us (25%)
  waiting for transfers between devices  5.99 us (11%)
  starting transfers between devices  3.06 us (6%)
  between operations  0.73 us (1%)
    all_to_all x1, blocking collectives, per_device(): parts = lax.all_to_all(chip, 'dp', 0, 0, axis_index_groups=groups)  16.5 us
    all_to_all x1, blocking collectives, per_device(): lax.all_to_all(copies, 'dp', 0, 0, axis_index_groups=groups)  13.2 us
    ppermute x3, waiting for transfers between devices, swap(): return lax.ppermute(array, 'dp', [(i, i ^ step) for i in range(count)])  5.99 us
    pallas_call x1, Pallas kernels, query_and_other(): pl.pallas_call(query_kernel, out_shape=(jax.ShapeDtypeStruct((rows // 2,...  5.57 us
    pallas_call x2, Pallas kernels, hidden_part(): pl.pallas_call(functools.partial(hidden_kernel, turn), out_shape=jax.Shap...  3.84 us
    ppermute x3, starting transfers between devices, swap(): return lax.ppermute(array, 'dp', [(i, i ^ step) for i in range(count)])  3.06 us
    pallas_call x2, Pallas kernels, place(): pl.pallas_call(functools.partial(place_kernel, turned), out_shape=jax.Sha...  1.96 us
    pallas_call x1, Pallas kernels, own_part(): pl.pallas_call(own_kernel, out_shape=(jax.ShapeDtypeStruct((rows // 2, wi...  1.72 us
  transfers between devices with their start and end apart: 3, of which 2 were waited for; matrix products, arithmetic and copies ran while one was open for 0% of the time, Pallas kernels for 12%

profile of v14, /device:TPU:0, one launch (start us, length us, event | category | flops | bytes accessed | tf_op | source)
XLA Modules:
  0.0 53.0 jit_solution(11572439544670888269)
XLA Ops:
  0.6 0.0 copy-start
  0.6 0.0 copy-start.1
  0.7 0.0 copy-start.2
  0.7 5.6 %shard_map.68 = (bf16[64,8192]{1,0:T(8,128)(2,1)S(1)}, bf16[256,8192]{1,0:T(8,128)(2,1)S(1)}, bf16[256,128]{1,0:T(8,128)(2,1)S(1)}, bf16[256,64]{1,0:T(8,128)(2,1)S(1)}) custom-call(bf16[256,8192]{1,0:T(8,128)(2,1)} %hidden_hbm.1, bf16[128,8192]{1,0:T(8,128)(2,1)} %weight_hbm.5, bf16[64,256]{1,0:T(8,128)(2,1)} %bitcast.7, bf16[64,256]{1,0:T(8,128)(2,1)} %bitcast.9, ...), custom_call_target="tpu_custom_call" | custom-call | flops 805306368 | bytes 6291456 | tf_op jit(solution)/shard_map/pallas_call | solution.py:106
  6.2 0.5 collective-permute-start
  6.8 0.0 copy-done
  6.8 0.0 copy-done.1
  6.8 0.0 copy-done.2
  6.8 1.7 %shard_map.69 = (bf16[64,8192]{1,0:T(8,128)(2,1)S(1)}, bf16[256,128]{1,0:T(8,128)(2,1)S(1)}) custom-call(bf16[256,8192]{1,0:T(8,128)(2,1)S(1)} %get-tuple-element.14.hidden, bf16[256,128]{1,0:T(8,128)(2,1)S(1)} %get-tuple-element.15.query, bf16[256,64]{1,0:T(8,128)(2,1)S(1)} %get-tuple-element.16.others, bf16[64,256]{1,0:T(8,128)(2,1)S(1)} %bitcast.8, ...), custom_call_target="tpu_custom_call" | custom-call | flops 268435456 | bytes 4194304 | tf_op jit(solution)/shard_map/pallas_call | solution.py:148
  8.5 3.8 %shard_map.70.refs_0_ = bf16[256,8192]{1,0:T(8,128)(2,1)} custom-call(bf16[256,128]{1,0:T(8,128)(2,1)S(1)} %get-tuple-element.19.grad_query, bf16[128,8192]{1,0:T(8,128)(2,1)} %weight_hbm.5), custom_call_target="tpu_custom_call" | custom-call | flops 536870912 | bytes 6291456 | tf_op jit(solution)/shard_map/pallas_call | solution.py:190
  12.3 0.0 collective-permute-done
  12.3 0.2 fusion
  12.5 16.5 %all_to_all.10 = bf16[8,8,8192]{2,1,0:T(8,128)(2,1)S(1)} all-to-all(bf16[8,8,8192]{2,1,0:T(8,128)(2,1)S(1)} %fusion), channel_id=1, replica_groups={{14,0,12,2,10,4,8,6},{15,13,11,9,7,5,3,1},{22,24,20,26,18,28,16,30},{23..., dimensions={0} | all-to-all | bytes 2097152 | tf_op jit(solution)/shard_map/all_to_all | solution.py:263
  29.0 0.1 reduce_sum.12
  29.1 2.5 %collective-permute-start.1 = (bf16[8,8192]{1,0:T(8,128)(2,1)S(1)}, bf16[8,8192]{1,0:T(8,128)(2,1)S(1)}, u32[]{:S(2)}, u32[]{:S(2)}) collective-permute-start(bf16[8,8192]{1,0:T(8,128)(2,1)S(1)} %reduce_sum.12), channel_id=1, source_target_pairs={{0,24},{1,25},{2,26},{3,27},{4,28},{5,29},{6,30},{7,31},{8,16},{9,... | collective-permute-start | bytes 393224 | tf_op jit(solution)/shard_map/ppermute | solution.py:233
  31.7 0.1 shard_map.71
  31.8 4.3 %collective-permute-done.1 = bf16[8,8192]{1,0:T(8,128)(2,1)S(1)} collective-permute-done((bf16[8,8192]{1,0:T(8,128)(2,1)S(1)}, bf16[8,8192]{1,0:T(8,128)(2,1)S(1)}, u32[]{:S(2)}, u32[]{:S(2)}) %collective-permute-start.1) | collective-permute-done | bytes 131104 | tf_op jit(solution)/shard_map/ppermute | solution.py:233
  36.1 0.1 broadcast_in_dim.2
  36.2 13.2 %all_to_all.11 = bf16[8,8,8192]{2,1,0:T(8,128)(2,1)S(1)} all-to-all(bf16[8,8,8192]{2,1,0:T(8,128)(2,1)S(1)} %broadcast_in_dim.2), channel_id=1, replica_groups={{14,0,12,2,10,4,8,6},{15,13,11,9,7,5,3,1},{22,24,20,26,18,28,16,30},{23..., dimensions={0} | all-to-all | bytes 2097152 | tf_op jit(solution)/shard_map/all_to_all | solution.py:273
  49.4 0.0 collective-permute-start.2
  49.4 1.0 %shard_map.72.refs_0_ = bf16[128,8192]{1,0:T(8,128)(2,1)} custom-call(bf16[64,8192]{1,0:T(8,128)(2,1)S(1)} %bitcast.6), custom_call_target="tpu_custom_call" | custom-call | bytes 2097152 | tf_op jit(solution)/shard_map/pallas_call | solution.py:220
  50.4 1.7 %collective-permute-done.2.piece_hbm = bf16[64,8192]{1,0:T(8,128)(2,1)S(1)} collective-permute-done((bf16[64,8192]{1,0:T(8,128)(2,1)S(1)}, bf16[64,8192]{1,0:T(8,128)(2,1)S(1)}, u32[]{:S(2)}, u32[]{:S(2)}) %collective-permute-start.2) | collective-permute-done | bytes 1048608 | tf_op jit(solution)/shard_map/ppermute | solution.py:233
  52.1 1.0 %shard_map.73 = bf16[128,8192]{1,0:T(8,128)(2,1)} custom-call(bf16[64,8192]{1,0:T(8,128)(2,1)S(1)} %collective-permute-done.2.piece_hbm, bf16[128,8192]{1,0:T(8,128)(2,1)} %shard_map.72.refs_0_), custom_call_target="tpu_custom_call", output_to_operand_aliasing={{}: (1, {})} | custom-call | bytes 2097152 | tf_op jit(solution)/shard_map/pallas_call | solution.py:220
  (1 shorter events, 0.0 us)
Async XLA Ops:
  0.6 6.1 %copy-start = (bf16[256,128]{1,0:T(8,128)(2,1)S(1)}, bf16[256,128]{1,0:T(8,128)(2,1)}, u32[]{:S(2)}) copy-start(bf16[256,128]{1,0:T(8,128)(2,1)} %grad_out.1) | copy-start | bytes 196612
  0.6 6.1 %copy-start.1 = (bf16[256,64]{0,1:T(8,128)(2,1)S(1)}, bf16[256,64]{0,1:T(8,128)(2,1)}, u32[]{:S(2)}) copy-start(bf16[256,64]{0,1:T(8,128)(2,1)} %param.7) | copy-start | bytes 98308
  0.7 6.1 %copy-start.2 = (bf16[256,64]{0,1:T(8,128)(2,1)S(1)}, bf16[256,64]{0,1:T(8,128)(2,1)}, u32[]{:S(2)}) copy-start(bf16[256,64]{0,1:T(8,128)(2,1)} %param.8) | copy-start | bytes 98308
  6.2 6.0 %collective-permute-start = (bf16[64,8192]{1,0:T(8,128)(2,1)S(1)}, bf16[64,8192]{1,0:T(8,128)(2,1)S(1)}, u32[]{:S(2)}, u32[]{:S(2)}) collective-permute-start(bf16[64,8192]{1,0:T(8,128)(2,1)S(1)} %get-tuple-element.18), channel_id=1, source_target_pairs={{0,1},{1,0},{2,3},{3,2},{4,5},{5,4},{6,7},{7,6},{8,9},{9,8},{10,11... | collective-permute-start | bytes 3145736 | tf_op jit(solution)/shard_map/ppermute | solution.py:233
  29.1 6.9 %collective-permute-start.1 = (bf16[8,8192]{1,0:T(8,128)(2,1)S(1)}, bf16[8,8192]{1,0:T(8,128)(2,1)S(1)}, u32[]{:S(2)}, u32[]{:S(2)}) collective-permute-start(bf16[8,8192]{1,0:T(8,128)(2,1)S(1)} %reduce_sum.12), channel_id=1, source_target_pairs={{0,24},{1,25},{2,26},{3,27},{4,28},{5,29},{6,30},{7,31},{8,16},{9,... | collective-permute-start | bytes 393224 | tf_op jit(solution)/shard_map/ppermute | solution.py:233
  49.4 2.7 %collective-permute-start.2 = (bf16[64,8192]{1,0:T(8,128)(2,1)S(1)}, bf16[64,8192]{1,0:T(8,128)(2,1)S(1)}, u32[]{:S(2)}, u32[]{:S(2)}) collective-permute-start(bf16[64,8192]{1,0:T(8,128)(2,1)S(1)} %bitcast.5), channel_id=1, source_target_pairs={{0,1},{1,0},{2,3},{3,2},{4,5},{5,4},{6,7},{7,6},{8,9},{9,8},{10,11... | collective-permute-start | bytes 3145736 | tf_op jit(solution)/shard_map/ppermute | solution.py:233

commit v15 on v14

--- a/solution.py
+++ b/solution.py
@@ -206,26 +206,26 @@
     )(grad_query, pltpu.with_memory_space_constraint(query_weight, pltpu.HBM), *given)
 
 
-def place_kernel(turned, piece_hbm, *refs):
+def place_kernel(turned, offset, piece_hbm, *refs):
     out_hbm, sem = refs[-2:]
-    half = piece_hbm.shape[0]
-    rows = pl.ds(pl.multiple_of((own_core() ^ turned) * half, half), half)
+    half, size = out_hbm.shape[0] // 2, piece_hbm.shape[0]
+    rows = pl.ds(pl.multiple_of((own_core() ^ turned) * half + offset, size), size)
     copy = pltpu.make_async_copy(piece_hbm, out_hbm.at[rows], sem)
     copy.start()
     copy.wait()
 
 
-def place(turned, piece, before=None):
-    half, width = piece.shape
+def place(turned, offset, half, piece, before=None):
+    size, width = piece.shape
     return pl.pallas_call(
-        functools.partial(place_kernel, turned),
+        functools.partial(place_kernel, turned, offset),
         out_shape=jax.ShapeDtypeStruct((2 * half, width), jnp.bfloat16),
         in_specs=[ANY] + [ANY] * (before is not None),
         out_specs=ANY,
         scratch_shapes=[pltpu.SemaphoreType.DMA(())],
         input_output_aliases={} if before is None else {1: 0},
         compiler_params=pltpu.CompilerParams(vmem_limit_bytes=VMEM_LIMIT),
-        cost_estimate=pl.CostEstimate(flops=0, bytes_accessed=4 * half * width, transcendentals=0),
+        cost_estimate=pl.CostEstimate(flops=0, bytes_accessed=4 * size * width, transcendentals=0),
     )(piece, *(() if before is None else (before,)))
 
 
@@ -271,8 +271,11 @@
         total = add(total, arriving)
     copies = jnp.broadcast_to(total[None], (blocks, *total.shape))
     gathered = lax.all_to_all(copies, "dp", 0, 0, axis_index_groups=groups).reshape(half, width)
-    arriving = swap(gathered, 1, count)
-    grad_query_weight = place(1, arriving, place(0, gathered))
+    cuts = (0, half // 2)
+    arriving = [swap(gathered[cut : cut + half // 2], 1, count) for cut in cuts]
+    grad_query_weight = place(0, 0, half, gathered)
+    for cut, piece in zip(cuts, arriving):
+        grad_query_weight = place(1, cut, half, piece, grad_query_weight)
     if input_terms.shape[1] == given_width:
         grad_hidden = input_terms
     else:

time: 53.3 us -> 53.3 us (level)
  waiting for transfers between devices: 5.99 us -> 4.74 us
  Pallas kernels: 13.1 us -> 13.7 us
  starting transfers between devices: 3.06 us -> 3.63 us
    ppermute x3 -> x4, waiting for transfers between devices: 5.99 us -> 4.74 us  [swap(): return lax.ppermute(array, 'dp', [(i, i ^ step) for i in range(count)])]
    pallas_call x2 -> x3, Pallas kernels: 1.96 us -> 2.59 us  [place(): pl.pallas_call(functools.partial(place_kernel, turned, offset), out_shape...]
    ppermute x3 -> x4, starting transfers between devices: 3.06 us -> 3.63 us  [swap(): return lax.ppermute(array, 'dp', [(i, i ^ step) for i in range(count)])]
  transfers between devices with their start and end apart: 3 -> 4, of which waited for: 2 -> 2; matrix products, arithmetic and copies ran while one was open for 0% -> 0% of each run, Pallas kernels for 12% -> 14%
where the time goes in v15:
time: 53.3 us; the launch traced here: 53.1 us
  blocking collectives  29.7 us (56%)
  Pallas kernels  13.7 us (26%)
  waiting for transfers between devices  4.74 us (9%)
  starting transfers between devices  3.63 us (7%)
  between operations  0.75 us (1%)
    all_to_all x1, blocking collectives, per_device(): parts = lax.all_to_all(chip, 'dp', 0, 0, axis_index_groups=groups)  16.5 us
    all_to_all x1, blocking collectives, per_device(): lax.all_to_all(copies, 'dp', 0, 0, axis_index_groups=groups)  13.2 us
    pallas_call x1, Pallas kernels, query_and_other(): pl.pallas_call(query_kernel, out_shape=(jax.ShapeDtypeStruct((rows // 2,...  5.57 us
    ppermute x4, waiting for transfers between devices, swap(): return lax.ppermute(array, 'dp', [(i, i ^ step) for i in range(count)])  4.74 us
    pallas_call x2, Pallas kernels, hidden_part(): pl.pallas_call(functools.partial(hidden_kernel, turn), out_shape=jax.Shap...  3.84 us
    ppermute x4, starting transfers between devices, swap(): return lax.ppermute(array, 'dp', [(i, i ^ step) for i in range(count)])  3.63 us
    pallas_call x3, Pallas kernels, place(): pl.pallas_call(functools.partial(place_kernel, turned, offset), out_shape...  2.59 us
    pallas_call x1, Pallas kernels, own_part(): pl.pallas_call(own_kernel, out_shape=(jax.ShapeDtypeStruct((rows // 2, wi...  1.72 us
  transfers between devices with their start and end apart: 4, of which 2 were waited for; matrix products, arithmetic and copies ran while one was open for 0% of the time, Pallas kernels for 14%

profile of v15, /device:TPU:0, one launch (start us, length us, event | category | flops | bytes accessed | tf_op | source)
XLA Modules:
  0.0 53.1 jit_solution(4218355680743156957)
XLA Ops:
  0.6 0.0 copy-start
  0.6 0.0 copy-start.1
  0.7 0.0 copy-start.2
  0.7 5.6 %shard_map.68 = (bf16[64,8192]{1,0:T(8,128)(2,1)S(1)}, bf16[256,8192]{1,0:T(8,128)(2,1)S(1)}, bf16[256,128]{1,0:T(8,128)(2,1)S(1)}, bf16[256,64]{1,0:T(8,128)(2,1)S(1)}) custom-call(bf16[256,8192]{1,0:T(8,128)(2,1)} %hidden_hbm.1, bf16[128,8192]{1,0:T(8,128)(2,1)} %weight_hbm.5, bf16[64,256]{1,0:T(8,128)(2,1)} %bitcast.10, bf16[64,256]{1,0:T(8,128)(2,1)} %bitcast.12, ...), custom_call_target="tpu_custom_call" | custom-call | flops 805306368 | bytes 6291456 | tf_op jit(solution)/shard_map/pallas_call | solution.py:106
  6.2 0.5 collective-permute-start
  6.8 0.0 copy-done
  6.8 0.0 copy-done.1
  6.8 0.0 copy-done.2
  6.8 1.7 %shard_map.69 = (bf16[64,8192]{1,0:T(8,128)(2,1)S(1)}, bf16[256,128]{1,0:T(8,128)(2,1)S(1)}) custom-call(bf16[256,8192]{1,0:T(8,128)(2,1)S(1)} %get-tuple-element.14.hidden, bf16[256,128]{1,0:T(8,128)(2,1)S(1)} %get-tuple-element.15.query, bf16[256,64]{1,0:T(8,128)(2,1)S(1)} %get-tuple-element.16.others, bf16[64,256]{1,0:T(8,128)(2,1)S(1)} %bitcast.11, ...), custom_call_target="tpu_custom_call" | custom-call | flops 268435456 | bytes 4194304 | tf_op jit(solution)/shard_map/pallas_call | solution.py:148
  8.5 3.8 %shard_map.70.refs_0_ = bf16[256,8192]{1,0:T(8,128)(2,1)} custom-call(bf16[256,128]{1,0:T(8,128)(2,1)S(1)} %get-tuple-element.19.grad_query, bf16[128,8192]{1,0:T(8,128)(2,1)} %weight_hbm.5), custom_call_target="tpu_custom_call" | custom-call | flops 536870912 | bytes 6291456 | tf_op jit(solution)/shard_map/pallas_call | solution.py:190
  12.3 0.0 collective-permute-done
  12.3 0.2 fusion
  12.5 16.5 %all_to_all.10 = bf16[8,8,8192]{2,1,0:T(8,128)(2,1)S(1)} all-to-all(bf16[8,8,8192]{2,1,0:T(8,128)(2,1)S(1)} %fusion), channel_id=1, replica_groups={{14,0,12,2,10,4,8,6},{15,13,11,9,7,5,3,1},{22,24,20,26,18,28,16,30},{23..., dimensions={0} | all-to-all | bytes 2097152 | tf_op jit(solution)/shard_map/all_to_all | solution.py:263
  29.0 0.1 reduce_sum.12
  29.1 2.5 %collective-permute-start.1 = (bf16[8,8192]{1,0:T(8,128)(2,1)S(1)}, bf16[8,8192]{1,0:T(8,128)(2,1)S(1)}, u32[]{:S(2)}, u32[]{:S(2)}) collective-permute-start(bf16[8,8192]{1,0:T(8,128)(2,1)S(1)} %reduce_sum.12), channel_id=1, source_target_pairs={{0,24},{1,25},{2,26},{3,27},{4,28},{5,29},{6,30},{7,31},{8,16},{9,... | collective-permute-start | bytes 393224 | tf_op jit(solution)/shard_map/ppermute | solution.py:233
  31.7 0.1 shard_map.71
  31.8 4.3 %collective-permute-done.1 = bf16[8,8192]{1,0:T(8,128)(2,1)S(1)} collective-permute-done((bf16[8,8192]{1,0:T(8,128)(2,1)S(1)}, bf16[8,8192]{1,0:T(8,128)(2,1)S(1)}, u32[]{:S(2)}, u32[]{:S(2)}) %collective-permute-start.1) | collective-permute-done | bytes 131104 | tf_op jit(solution)/shard_map/ppermute | solution.py:233
  36.1 0.1 broadcast_in_dim.2
  36.2 13.2 %all_to_all.11 = bf16[8,8,8192]{2,1,0:T(8,128)(2,1)S(1)} all-to-all(bf16[8,8,8192]{2,1,0:T(8,128)(2,1)S(1)} %broadcast_in_dim.2), channel_id=1, replica_groups={{14,0,12,2,10,4,8,6},{15,13,11,9,7,5,3,1},{22,24,20,26,18,28,16,30},{23..., dimensions={0} | all-to-all | bytes 2097152 | tf_op jit(solution)/shard_map/all_to_all | solution.py:273
  49.4 0.1 slice_bitcast_fusion
  49.5 0.1 collective-permute-start.3
  49.6 0.5 collective-permute-start.2
  50.1 1.0 %shard_map.72.refs_0_ = bf16[128,8192]{1,0:T(8,128)(2,1)} custom-call(bf16[64,8192]{1,0:T(8,128)(2,1)S(1)} %bitcast.9), custom_call_target="tpu_custom_call" | custom-call | bytes 2097152 | tf_op jit(solution)/shard_map/pallas_call | solution.py:220
  51.0 0.4 collective-permute-done.3.piece_hbm
  51.5 0.8 %shard_map.73.refs_0_ = bf16[128,8192]{1,0:T(8,128)(2,1)} custom-call(bf16[32,8192]{1,0:T(8,128)(2,1)S(1)} %collective-permute-done.3.piece_hbm, bf16[128,8192]{1,0:T(8,128)(2,1)} %shard_map.72.refs_0_), custom_call_target="tpu_custom_call", output_to_operand_aliasing={{}: (1, {})} | custom-call | bytes 1048576 | tf_op jit(solution)/shard_map/pallas_call | solution.py:220
  52.3 0.0 collective-permute-done.2.piece_hbm
  52.3 0.8 %shard_map.74 = bf16[128,8192]{1,0:T(8,128)(2,1)} custom-call(bf16[32,8192]{1,0:T(8,128)(2,1)S(1)} %collective-permute-done.2.piece_hbm, bf16[128,8192]{1,0:T(8,128)(2,1)} %shard_map.73.refs_0_), custom_call_target="tpu_custom_call", output_to_operand_aliasing={{}: (1, {})} | custom-call | bytes 1048576 | tf_op jit(solution)/shard_map/pallas_call | solution.py:220
  (1 shorter events, 0.0 us)
Async XLA Ops:
  0.6 6.1 %copy-start = (bf16[256,128]{1,0:T(8,128)(2,1)S(1)}, bf16[256,128]{1,0:T(8,128)(2,1)}, u32[]{:S(2)}) copy-start(bf16[256,128]{1,0:T(8,128)(2,1)} %grad_out.1) | copy-start | bytes 196612
  0.6 6.1 %copy-start.1 = (bf16[256,64]{0,1:T(8,128)(2,1)S(1)}, bf16[256,64]{0,1:T(8,128)(2,1)}, u32[]{:S(2)}) copy-start(bf16[256,64]{0,1:T(8,128)(2,1)} %param.7) | copy-start | bytes 98308
  0.7 6.1 %copy-start.2 = (bf16[256,64]{0,1:T(8,128)(2,1)S(1)}, bf16[256,64]{0,1:T(8,128)(2,1)}, u32[]{:S(2)}) copy-start(bf16[256,64]{0,1:T(8,128)(2,1)} %param.8) | copy-start | bytes 98308
  6.2 6.0 %collective-permute-start = (bf16[64,8192]{1,0:T(8,128)(2,1)S(1)}, bf16[64,8192]{1,0:T(8,128)(2,1)S(1)}, u32[]{:S(2)}, u32[]{:S(2)}) collective-permute-start(bf16[64,8192]{1,0:T(8,128)(2,1)S(1)} %get-tuple-element.18), channel_id=1, source_target_pairs={{0,1},{1,0},{2,3},{3,2},{4,5},{5,4},{6,7},{7,6},{8,9},{9,8},{10,11... | collective-permute-start | bytes 3145736 | tf_op jit(solution)/shard_map/ppermute | solution.py:233
  29.1 6.9 %collective-permute-start.1 = (bf16[8,8192]{1,0:T(8,128)(2,1)S(1)}, bf16[8,8192]{1,0:T(8,128)(2,1)S(1)}, u32[]{:S(2)}, u32[]{:S(2)}) collective-permute-start(bf16[8,8192]{1,0:T(8,128)(2,1)S(1)} %reduce_sum.12), channel_id=1, source_target_pairs={{0,24},{1,25},{2,26},{3,27},{4,28},{5,29},{6,30},{7,31},{8,16},{9,... | collective-permute-start | bytes 393224 | tf_op jit(solution)/shard_map/ppermute | solution.py:233
  49.5 2.0 %collective-permute-start.3 = (bf16[32,8192]{1,0:T(8,128)(2,1)S(1)}, bf16[32,8192]{1,0:T(8,128)(2,1)S(1)}, u32[]{:S(2)}, u32[]{:S(2)}) collective-permute-start(bf16[32,8192]{1,0:T(8,128)(2,1)S(1)} %get-tuple-element.26), channel_id=1, source_target_pairs={{0,1},{1,0},{2,3},{3,2},{4,5},{5,4},{6,7},{7,6},{8,9},{9,8},{10,11... | collective-permute-start | bytes 1572872 | tf_op jit(solution)/shard_map/ppermute | solution.py:233
  49.6 2.7 %collective-permute-start.2 = (bf16[32,8192]{1,0:T(8,128)(2,1)S(1)}, bf16[32,8192]{1,0:T(8,128)(2,1)S(1)}, u32[]{:S(2)}, u32[]{:S(2)}) collective-permute-start(bf16[32,8192]{1,0:T(8,128)(2,1)S(1)} %get-tuple-element.27), channel_id=1, source_target_pairs={{0,1},{1,0},{2,3},{3,2},{4,5},{5,4},{6,7},{7,6},{8,9},{9,8},{10,11... | collective-permute-start | bytes 1572872 | tf_op jit(solution)/shard_map/ppermute | solution.py:233
